TPU v7x, 32 devices: a whole 2x2x4 slice. The times are simulated.
32 devices in a mesh: dp: 16 (over z, y, core), head: 2 (over x).
Axes of the slice: x: 2, y: 2, z: 4, core: 2. Of those that a mesh axis runs over, the one named last changes fastest.
Arguments:
- tokens: bfloat16 [32768, 768], P(('dp', 'head')), may hold values from -6 to 6
- lengths: int32 [16, 4], P('dp'), may hold values from 0 to 2048, as said below
- feature_map: bfloat16 [12, 64, 256], replicated, may hold values from -5 to 5
- qkv_weight: bfloat16 [768, 3, 768], replicated, may hold values from -0.21875 to 0.21875
- qkv_bias: float32 [3, 768], replicated, may hold values from -3 to 3
- out_weight: bfloat16 [768, 768], replicated, may hold values from -0.875 to 0.875
- out_bias: float32 [768], replicated, may hold values from -2 to 2
- ln1_gain: float32 [768], replicated, may hold values from 0.5 to 1.5
- ln1_shift: float32 [768], replicated, may hold values from -2 to 2
- up_weight: bfloat16 [768, 3072], replicated, may hold values from -0.21875 to 0.21875
- up_bias: float32 [3072], replicated, may hold values from -3 to 3
- down_weight: bfloat16 [768, 3072], replicated, may hold values from -0.109375 to 0.109375
- down_bias: float32 [768], replicated, may hold values from -2 to 2
- ln2_gain: float32 [768], replicated, may hold values from 0.5 to 1.5
- ln2_shift: float32 [768], replicated, may hold values from -2 to 2
- cotangent: bfloat16 [32768, 768], P(('dp', 'head')), may hold values from -6 to 6
Outputs:
- output: bfloat16 [32768, 768], P(('dp', 'head'))
- grad_tokens: bfloat16 [32768, 768], P(('dp', 'head'))
- grad_qkv_weight: float32 [768, 3, 768], P('dp', None, 'head')
- grad_qkv_bias: float32 [3, 768], replicated
- grad_out_weight: float32 [768, 768], P('dp', 'head')
- grad_out_bias: float32 [768], replicated
- grad_ln1_gain: float32 [768], replicated
- grad_ln1_shift: float32 [768], replicated
- grad_up_weight: float32 [768, 3072], P('dp', 'head')
- grad_up_bias: float32 [3072], replicated
- grad_down_weight: float32 [768, 3072], P('dp', 'head')
- grad_down_bias: float32 [768], replicated
- grad_ln2_gain: float32 [768], replicated
- grad_ln2_shift: float32 [768], replicated
Inputs may be any that keep to these rules, and one draw needn't show every extreme that they name: Each packed row of 2048 slots holds up to 4 sequences in order (a length may be 0), then padding; a row's lengths sum to at most 2048; in every row one sequence is longer than 1024 and covers slots 2048 // 2 - 1 and 1024, its place among the 4 varying from row to row; in some row one sequence fills all 2048 slots.
All inputs are finite; a program needn't handle non-finite values.
Results may differ from a plain program's by a relative error of at most 0.025.
Values may be sent and summed in bfloat16 or wider, within the bound.
No kernel may reach another device: no remote copies, remote signals or barrier semaphores. Data moves between devices by JAX's collectives and lax.ppermute only.
A program may use at most 256 MiB of HBM per device.

v0:
```python
import jax
import jax.numpy as jnp
from jax import lax
from jax.sharding import PartitionSpec as P

norm_epsilon = 1e-06
root_half = 0.7071067811865476
inv_root_tau = 0.3989422804014327
contract_last = (((1,), (1,)), ((), ()))


def norm_forward(values, norm_gain, norm_shift):
    centred = values - jnp.mean(values, axis=-1, keepdims=True)
    spread = jnp.mean(centred * centred, axis=-1, keepdims=True)
    inverse = lax.rsqrt(spread + norm_epsilon)
    scaled = centred * inverse
    return (scaled * norm_gain + norm_shift, scaled, inverse)


def norm_backward(incoming, scaled, inverse, norm_gain):
    weighted = incoming * norm_gain
    return inverse * (
        weighted
        - jnp.mean(weighted, axis=-1, keepdims=True)
        - scaled * jnp.mean(weighted * scaled, axis=-1, keepdims=True)
    )


def gelu_slope(inputs):
    return (
        0.5 * (1.0 + lax.erf(inputs * root_half))
        + inputs * jnp.exp(-0.5 * inputs * inputs) * inv_root_tau
    )


def row_members(first_slot, slot_count, row_lengths):
    seq_ends = jnp.cumsum(row_lengths)
    seq_starts = seq_ends - row_lengths
    positions = first_slot + jnp.arange(slot_count, dtype=jnp.int32)[:, None]
    inside = jnp.logical_and(positions >= seq_starts[None, :], positions < seq_ends[None, :])
    members_f32 = inside.astype(jnp.float32)
    return (members_f32, members_f32.astype(jnp.bfloat16), 1.0 - jnp.sum(members_f32, axis=1))


def batch_logits(rows_bf, feature_map, factor):
    projected = jnp.einsum("htd,hdm->htm", rows_bf, feature_map, preferred_element_type=jnp.float32)
    squares = jnp.sum(jnp.square(rows_bf.astype(jnp.float32)), axis=-1, keepdims=True)
    return factor * projected - 0.5 * factor * factor * squares


def mix_head(query_feat, members, dead_rows, segment_state, segment_norm):
    query_wide = members[:, :, None] * query_feat[:, None, :]
    numerator = jnp.einsum(
        "tsm,smd->td", query_wide, segment_state, preferred_element_type=jnp.float32
    )
    denominator = (
        jnp.einsum("tsm,sm->t", query_wide, segment_norm, preferred_element_type=jnp.float32)
        + dead_rows
    )
    mixed_head = (numerator / denominator[:, None]).astype(jnp.bfloat16)
    return (mixed_head, numerator, denominator)


def state_grad_terms(query_feat, members, grad_mixed, numerator, denominator):
    grad_num = (grad_mixed / denominator[:, None]).astype(jnp.bfloat16)
    grad_den = (-jnp.sum(grad_mixed * numerator, axis=-1) / (denominator * denominator)).astype(
        jnp.bfloat16
    )
    query_wide = members[:, :, None] * query_feat[:, None, :]
    state_part = jnp.einsum("tsm,td->smd", query_wide, grad_num, preferred_element_type=jnp.float32)
    norm_part = jnp.einsum("tsm,t->sm", query_wide, grad_den, preferred_element_type=jnp.float32)
    return (grad_num, grad_den, state_part, norm_part)


def feature_grads(
    key_feat,
    value_rows,
    members,
    members_f32,
    grad_num,
    grad_den,
    grad_state,
    grad_norm,
    segment_state,
    segment_norm,
):
    query_terms = (
        jnp.einsum("td,smd->tsm", grad_num, segment_state, preferred_element_type=jnp.float32)
        + grad_den.astype(jnp.float32)[:, None, None] * segment_norm.astype(jnp.float32)[None]
    )
    grad_qfeat = jnp.sum(query_terms * members_f32[:, :, None], axis=1)
    key_terms = (
        jnp.einsum("td,smd->tsm", value_rows, grad_state, preferred_element_type=jnp.float32)
        + grad_norm.astype(jnp.float32)[None]
    )
    grad_kfeat = jnp.sum(key_terms * members_f32[:, :, None], axis=1)
    key_wide = members[:, :, None] * key_feat[:, None, :]
    grad_value = jnp.einsum("tsm,smd->td", key_wide, grad_state, preferred_element_type=jnp.float32)
    return (grad_qfeat, grad_kfeat, grad_value)


def query_logit_grad(grad_qfeat, query_exp, query_logits, query_top):
    query_slope = grad_qfeat * query_exp
    query_peak = (query_logits == query_top).astype(jnp.float32)
    slope_total = jnp.sum(query_slope, axis=-1, keepdims=True)
    peak_total = jnp.sum(query_peak, axis=-1, keepdims=True)
    return (query_slope - query_peak * slope_total / peak_total).astype(jnp.bfloat16)


def rows_grad(grad_log, rows_bf, map_head, factor):
    return factor * jnp.dot(
        grad_log, map_head.T, preferred_element_type=jnp.float32
    ) - factor * factor * rows_bf.astype(jnp.float32) * jnp.sum(
        grad_log.astype(jnp.float32), axis=-1, keepdims=True
    )


def owner_blocks(gradient, dp_count, head_count):
    row_count = gradient.shape[0] // dp_count
    middle = gradient.shape[1:-1]
    col_count = gradient.shape[-1] // head_count
    blocked = gradient.reshape((dp_count, row_count) + middle + (head_count, col_count))
    last_axis = blocked.ndim - 1
    axes_order = (0, last_axis - 1) + tuple(range(1, last_axis - 1)) + (last_axis,)
    return blocked.transpose(axes_order).reshape(
        (dp_count * head_count * row_count,) + middle + (col_count,)
    )


def tokens_plan(
    tokens,
    lengths,
    feature_map,
    qkv_weight,
    qkv_bias,
    out_weight,
    out_bias,
    ln1_gain,
    ln1_shift,
    up_weight,
    up_bias,
    down_weight,
    down_bias,
    ln2_gain,
    ln2_shift,
    cotangent,
):
    shard_rows, model_width = tokens.shape
    head_total, head_size = (feature_map.shape[0], feature_map.shape[1])
    factor = head_size ** (-0.25)
    flat_qkv = qkv_weight.reshape(model_width, 3 * model_width)
    first_slot = lax.axis_index("head") * shard_rows
    members_f32, members, dead_rows = row_members(first_slot, shard_rows, lengths[0])
    projected = jnp.dot(tokens, flat_qkv, preferred_element_type=jnp.float32) + qkv_bias.reshape(
        1, 3 * model_width
    )
    split_heads = (
        projected.astype(jnp.bfloat16)
        .reshape(shard_rows, 3, head_total, head_size)
        .transpose(1, 2, 0, 3)
    )
    query_logits = batch_logits(split_heads[0], feature_map, factor)
    key_logits = batch_logits(split_heads[1], feature_map, factor)
    query_feat = jnp.exp(query_logits - jnp.max(query_logits, axis=-1, keepdims=True)).astype(
        jnp.bfloat16
    )

    def key_sums(operands):
        head_logits, value_rows = operands
        key_feat = jnp.exp(head_logits).astype(jnp.bfloat16)
        key_wide = members[:, :, None] * key_feat[:, None, :]
        state_part = jnp.einsum(
            "tsm,td->smd", key_wide, value_rows, preferred_element_type=jnp.float32
        )
        norm_part = jnp.einsum("ts,tm->sm", members, key_feat, preferred_element_type=jnp.float32)
        return (state_part, norm_part)

    state_part, norm_part = lax.map(key_sums, (key_logits, split_heads[2]))
    state_sum, norm_sum = lax.psum((state_part, norm_part), "head")
    states = state_sum.astype(jnp.bfloat16)
    seg_norms = norm_sum.astype(jnp.bfloat16)

    def mix_one(operands):
        head_feat, head_state, head_norm = operands
        return mix_head(head_feat, members, dead_rows, head_state, head_norm)

    mixed_heads, numerators, denominators = lax.map(mix_one, (query_feat, states, seg_norms))
    mixed_rows = mixed_heads.transpose(1, 0, 2).reshape(shard_rows, model_width)
    attended = lax.dot_general(
        mixed_rows, out_weight, contract_last, preferred_element_type=jnp.float32
    )
    hidden = tokens.astype(jnp.float32) + attended + out_bias
    normed, normed_scaled, normed_inverse = norm_forward(hidden, ln1_gain, ln1_shift)
    normed_bf = normed.astype(jnp.bfloat16)
    up_pre = jnp.dot(normed_bf, up_weight, preferred_element_type=jnp.float32) + up_bias
    activated = jax.nn.gelu(up_pre, approximate=False).astype(jnp.bfloat16)
    branch = lax.dot_general(
        activated, down_weight, contract_last, preferred_element_type=jnp.float32
    )
    final_sum = normed + branch + down_bias
    output, final_scaled, final_inverse = norm_forward(final_sum, ln2_gain, ln2_shift)
    incoming = cotangent.astype(jnp.float32)
    grad_final = norm_backward(incoming, final_scaled, final_inverse, ln2_gain)
    grad_ln2_gain = jnp.sum(incoming * final_scaled, axis=0)
    grad_ln2_shift = jnp.sum(incoming, axis=0)
    grad_down_bias = jnp.sum(grad_final, axis=0)
    branch_grad = grad_final.astype(jnp.bfloat16)
    grad_down_weight = jnp.einsum(
        "te,tf->ef", branch_grad, activated, preferred_element_type=jnp.float32
    )
    grad_act = jnp.dot(branch_grad, down_weight, preferred_element_type=jnp.float32)
    grad_up = (grad_act * gelu_slope(up_pre)).astype(jnp.bfloat16)
    grad_up_bias = jnp.sum(grad_up, axis=0, dtype=jnp.float32)
    grad_up_weight = jnp.einsum("te,tf->ef", normed_bf, grad_up, preferred_element_type=jnp.float32)
    grad_normed = grad_final + lax.dot_general(
        grad_up, up_weight, contract_last, preferred_element_type=jnp.float32
    )
    grad_hidden = norm_backward(grad_normed, normed_scaled, normed_inverse, ln1_gain)
    grad_ln1_gain = jnp.sum(grad_normed * normed_scaled, axis=0)
    grad_ln1_shift = jnp.sum(grad_normed, axis=0)
    grad_out_bias = jnp.sum(grad_hidden, axis=0)
    attn_grad = grad_hidden.astype(jnp.bfloat16)
    grad_out_weight = jnp.einsum(
        "te,tf->ef", attn_grad, mixed_rows, preferred_element_type=jnp.float32
    )
    grad_mixed = (
        jnp.dot(attn_grad, out_weight, preferred_element_type=jnp.float32)
        .reshape(shard_rows, head_total, head_size)
        .transpose(1, 0, 2)
    )

    def state_grads_one(operands):
        head_feat, head_grad, head_num, head_den = operands
        return state_grad_terms(head_feat, members, head_grad, head_num, head_den)

    grad_nums, grad_dens, grad_state_part, grad_norm_part = lax.map(
        state_grads_one, (query_feat, grad_mixed, numerators, denominators)
    )
    grad_state_sum, grad_norm_sum = lax.psum((grad_state_part, grad_norm_part), "head")
    grad_states = grad_state_sum.astype(jnp.bfloat16)
    grad_norms = grad_norm_sum.astype(jnp.bfloat16)

    def backward_one(operands):
        (
            query_rows,
            key_rows,
            value_rows,
            map_head,
            head_qlog,
            head_klog,
            grad_num,
            grad_den,
            grad_state,
            grad_norm,
            segment_state,
            segment_norm,
        ) = operands
        query_top = jnp.max(head_qlog, axis=-1, keepdims=True)
        query_exp = jnp.exp(head_qlog - query_top)
        key_exp = jnp.exp(head_klog)
        grad_qfeat, grad_kfeat, grad_value = feature_grads(
            key_exp.astype(jnp.bfloat16),
            value_rows,
            members,
            members_f32,
            grad_num,
            grad_den,
            grad_state,
            grad_norm,
            segment_state,
            segment_norm,
        )
        grad_qlog = query_logit_grad(grad_qfeat, query_exp, head_qlog, query_top)
        grad_klog = (grad_kfeat * key_exp).astype(jnp.bfloat16)
        return (
            rows_grad(grad_qlog, query_rows, map_head, factor),
            rows_grad(grad_klog, key_rows, map_head, factor),
            grad_value,
        )

    grad_queries, grad_keys, grad_values = lax.map(
        backward_one,
        (
            split_heads[0],
            split_heads[1],
            split_heads[2],
            feature_map,
            query_logits,
            key_logits,
            grad_nums,
            grad_dens,
            grad_states,
            grad_norms,
            states,
            seg_norms,
        ),
    )
    grad_split = (
        jnp.stack((grad_queries, grad_keys, grad_values))
        .astype(jnp.bfloat16)
        .transpose(2, 0, 1, 3)
        .reshape(shard_rows, 3 * model_width)
    )
    qkv_bias_full = jnp.sum(grad_split, axis=0, dtype=jnp.float32).reshape(3, model_width)
    grad_qkv_weight = jnp.einsum(
        "te,tc->ec", tokens, grad_split, preferred_element_type=jnp.float32
    ).reshape(model_width, 3, model_width)
    grad_tokens = (
        grad_hidden
        + lax.dot_general(grad_split, flat_qkv, contract_last, preferred_element_type=jnp.float32)
    ).astype(jnp.bfloat16)
    dp_count = lax.axis_size("dp")
    head_count = lax.axis_size("head")
    grad_qkv_weight, grad_out_weight, grad_up_weight, grad_down_weight = (
        lax.psum_scatter(
            owner_blocks(grad_qkv_weight, dp_count, head_count),
            ("dp", "head"),
            scatter_dimension=0,
            tiled=True,
        ),
        lax.psum_scatter(
            owner_blocks(grad_out_weight, dp_count, head_count),
            ("dp", "head"),
            scatter_dimension=0,
            tiled=True,
        ),
        lax.psum_scatter(
            owner_blocks(grad_up_weight, dp_count, head_count),
            ("dp", "head"),
            scatter_dimension=0,
            tiled=True,
        ),
        lax.psum_scatter(
            owner_blocks(grad_down_weight, dp_count, head_count),
            ("dp", "head"),
            scatter_dimension=0,
            tiled=True,
        ),
    )
    vectors = jnp.stack(
        (
            grad_out_bias,
            grad_ln1_gain,
            grad_ln1_shift,
            grad_down_bias,
            grad_ln2_gain,
            grad_ln2_shift,
        )
    )
    return (
        output.astype(jnp.bfloat16),
        grad_tokens,
        grad_qkv_weight,
        grad_out_weight,
        grad_up_weight,
        grad_down_weight,
        qkv_bias_full,
        grad_up_bias,
        vectors,
    )


def body(
    tokens,
    lengths,
    feature_map,
    qkv_weight,
    qkv_bias,
    out_weight,
    out_bias,
    ln1_gain,
    ln1_shift,
    up_weight,
    up_bias,
    down_weight,
    down_bias,
    ln2_gain,
    ln2_shift,
    cotangent,
):
    results = tokens_plan(
        tokens,
        lengths,
        feature_map,
        qkv_weight,
        qkv_bias,
        out_weight,
        out_bias,
        ln1_gain,
        ln1_shift,
        up_weight,
        up_bias,
        down_weight,
        down_bias,
        ln2_gain,
        ln2_shift,
        cotangent,
    )
    (
        output,
        grad_tokens,
        grad_qkv_weight,
        grad_out_weight,
        grad_up_weight,
        grad_down_weight,
        qkv_bias_full,
        up_bias_full,
        vectors,
    ) = results
    qkv_bias_sum, up_bias_sum, vector_sum = lax.psum(
        (qkv_bias_full, up_bias_full, vectors), ("dp", "head")
    )
    return (
        output,
        grad_tokens,
        grad_qkv_weight,
        qkv_bias_sum,
        grad_out_weight,
        vector_sum[0],
        vector_sum[1],
        vector_sum[2],
        grad_up_weight,
        up_bias_sum,
        grad_down_weight,
        vector_sum[3],
        vector_sum[4],
        vector_sum[5],
    )


def solution(mesh):
    in_specs = (
        P(("dp", "head"), None),
        P("dp", None),
        P(),
        P(),
        P(),
        P(),
        P(),
        P(),
        P(),
        P(),
        P(),
        P(),
        P(),
        P(),
        P(),
        P(("dp", "head"), None),
    )
    out_specs = (
        P(("dp", "head"), None),
        P(("dp", "head"), None),
        P("dp", None, "head"),
        P(),
        P("dp", "head"),
        P(),
        P(),
        P(),
        P("dp", "head"),
        P(),
        P("dp", "head"),
        P(),
        P(),
        P(),
    )
    return jax.shard_map(body, mesh=mesh, in_specs=in_specs, out_specs=out_specs, check_vma=False)
```

profile of v0, /device:TPU:0, one launch (start us, length us, event | category | flops | bytes accessed | tf_op | source)
XLA Modules:
  0.0 1188.4 jit_solution(13592791070779563393)
XLA Ops:
  7.3 6.2 copy.79
  13.5 7.5 add_convert_fusion
  21.0 6.7 copy.80
  37.8 7.7 multiply_subtract_fusion
  45.5 12.7 %copy.82 = f32[12,1024,256]{2,1,0:T(8,128)} copy(f32[12,1024,256]{1,2,0:T(8,128)} %multiply_subtract_fusion) | data formatting | bytes 25165824
  60.6 38.2 %while.65 = (s32[]{:T(128)}, f32[12,4,256,64]{2,3,1,0:T(8,128)}, f32[12,4,256]{2,1,0:T(4,128)S(1)}, f32[12,1024,256]{2,1,0:T(8,128)}, bf16[12,1024,64]{1,2,0:T(8...) while((s32[]{:T(128)}, f32[12,4,256,64]{2,3,1,0:T(8,128)}, ...), condition=%wide.region_5.6_spmd.clone.clone, body=%wide.region_4.5_spmd.clone.sunk.clone | while | flops 140812288 | bytes 3045501 | solution.py:178
  98.8 8.8 exponential_convert_fusion.1
  107.7 8.6 copy.83
  116.3 80.0 %all-reduce.5 = (bf16[12,4,256,64]{2,3,1,0:T(8,128)(2,1)}, bf16[12,4,256]{2,1,0:T(4,128)(2,1)}) all-reduce(f32[12,4,256,64]{2,3,1,0:T(8,128)} %get-tuple-element.245, f32[12,4,256]{2,1,0:T(4,128)S(1)} %get-tuple-element.246), channel_id=1, replica_groups=mesh['dp'=16,'head'=2] {'head'}, use_global_device_ids=true, to_apply=%region_6.7 | all-reduce | flops 798720 | bytes 4792320 | tf_op jit(solution)/shard_map/psum | solution.py:179
  197.7 74.1 %while.66 = (s32[]{:T(128)}, bf16[12,1024,64]{1,2,0:T(8,128)(2,1)}, f32[12,1024,64]{1,2,0:T(8,128)}, f32[12,1024]{1,0:T(8,128)S(1)}, bf16[12,1024,256]{2,1,0:T(8...) while((s32[]{:T(128)}, bf16[12,1024,64]{1,2,0:T(8,128)(2,1)}, ...), condition=%wide.region_10.11_spmd.clone.clone, body=%wide.region_9.10_spmd.clone.sunk.clone | while | flops 138564608 | bytes 3210905 | solution.py:187
  275.7 34.8 %fusion.117 = (bf16[1024,3072]{1,0:T(8,128)(2,1)S(1)}, f32[1024,3072]{1,0:T(8,128)}) fusion(f32[3072]{0:T(1024)S(1)} %copy-done.31, bf16[768,3072]{1,0:T(8,128)(2,1)S(1)} %bitcast.412, f32[1024,768]{0,1:T(8,128)S(1)} %get-tuple-element.839, f32[768]{0:T(1024)S(1)} %copy-done.34, f32[768]{0:T(1024)S(1)} %copy-done.29, f32[1024]{0:T(1024)S(1)} %add_rsqrt_fusion.1, ...), kind=kOutput, calls=%fused_computation.141 | convolution fusion | flops 5043388416 | bytes 26765312 | tf_op jit(solution)/shard_map/dot_general | solution.py:195
  310.6 5.2 fusion.155
  323.2 14.7 %convert_reduce_fusion.3 = (f32[3072]{0:T(1024)}, bf16[1024,3072]{1,0:T(8,128)(2,1)S(1)}) fusion(f32[1024,3072]{1,0:T(8,128)} %get-tuple-element.841, f32[3072]{0:T(1024)S(1)} %copy-done.31, bf16[768,3072]{1,0:T(8,128)(2,1)} %param.35, f32[1024]{0:T(1024)S(1)} %get-tuple-element.847, f32[1024,768]{0,1:T(8,128)S(1)} %copy-done.3, ...), kind=kOutput, calls=%fused_computation.148 | convolution fusion | flops 4879807488 | bytes 28355584 | tf_op jit(solution)/shard_map/dot_general | solution.py:211
  337.9 10.8 multiply_reduce_fusion.2
  358.5 7.7 multiply_subtract_fusion.1
  371.5 79.4 %while.67 = (s32[]{:T(128)}, bf16[12,1024,64]{1,2,0:T(8,128)(2,1)S(1)}, bf16[12,1024]{1,0:T(8,128)(2,1)S(1)}, f32[12,4,256,64]{2,3,1,0:T(8,128)}, f32[12,4,256]{...) while((s32[]{:T(128)}, ...), condition=%wide.region_21.22_spmd.clone.clone, body=%wide.region_19.21_spmd.clone.sunk.clone | while | flops 141978624 | bytes 3636397 | solution.py:236
  450.9 75.5 %all-reduce.6 = (bf16[12,4,256,64]{2,3,1,0:T(8,128)(2,1)}, bf16[12,4,256]{2,1,0:T(4,128)(2,1)S(1)}) all-reduce(f32[12,4,256,64]{2,3,1,0:T(8,128)} %get-tuple-element.252, f32[12,4,256]{2,1,0:T(4,128)S(1)} %get-tuple-element.253), channel_id=1, replica_groups=mesh['dp'=16,'head'=2] {'head'}, use_global_device_ids=true, to_apply=%region_22.23 | all-reduce | flops 798720 | bytes 4792320 | tf_op jit(solution)/shard_map/psum | solution.py:239
  526.3 218.0 %while.68 = (s32[]{:T(128)}, bf16[12,1024,64]{1,2,0:T(8,128)(2,1)}, bf16[12,1024,64]{1,2,0:T(8,128)(2,1)}, bf16[12,1024,64]{1,2,0:T(8,128)(2,1)}, bf16[12,1024,6...) while((s32[]{:T(128)}, bf16[12,1024,64]{1,2,0:T(8,128)(2,1)}, ...), condition=%wide.region_32.33_spmd.clone.clone.clone, body=%wide.region_24.32_spmd.clone.clone.sunk.clone | while | flops 485773312 | bytes 35503932 | solution.py:281
  749.2 5.8 convolution_bitcast_fusion.1
  755.0 8.0 copy.89
  763.0 9.3 reshape_reshape.3
  772.3 6.4 copy.90
  780.1 10.8 fusion.139
  790.9 13.3 %reshape.234 = f32[16,48,2,1536]{3,2,1,0:T(2,128)} reshape(f32[768,3072]{1,0:T(8,128)} %fusion.139) | data formatting | bytes 18874368 | tf_op jit(solution)/shard_map/reshape | solution.py:122
  804.2 9.3 copy.92
  813.6 10.8 fusion.144
  824.4 13.3 %reshape.232 = f32[16,48,2,1536]{3,2,1,0:T(2,128)} reshape(f32[768,3072]{1,0:T(8,128)} %fusion.144) | data formatting | bytes 18874368 | tf_op jit(solution)/shard_map/reshape | solution.py:122
  837.8 9.0 copy.91
  852.0 9.6 add_convert_fusion.1
  866.1 40.8 %all-reduce = (f32[3,768]{1,0:T(4,128)}, f32[6,768]{1,0:T(8,128)S(1)}, f32[3072]{0:T(1024)}) all-reduce(f32[3,768]{1,0:T(4,128)S(1)} %reshape.230, f32[6,768]{1,0:T(8,128)S(1)} %stack.47, f32[3072]{0:T(1024)S(1)} %copy-done.28), channel_id=1, replica_groups=mesh['dp'=16,'head'=2] {'dp','head'}, use_global_device_ids=true, to_apply=%region_35.36 | all-reduce | flops 9984 | bytes 79872 | tf_op jit(solution)/shard_map/psum | solution.py:410
  907.6 132.3 %reduce-scatter.11.cloned.1.call-done = f32[48,1536]{1,0:T(8,128)} async-done(((f32[1536,1536]{1,0:T(8,128)}), f32[48,1536]{1,0:T(8,128)}) %reduce-scatter.11.cloned.1.call-update) | async-done | bytes 294928 | tf_op jit(solution)/shard_map/reduce_scatter | solution.py:333
  1039.9 141.8 %reduce-scatter.9.cloned.1.call-done = f32[48,1536]{1,0:T(8,128)} async-done(((f32[1536,1536]{1,0:T(8,128)}), f32[48,1536]{1,0:T(8,128)}) %reduce-scatter.9.cloned.1.call-update) | async-done | bytes 294928 | tf_op jit(solution)/shard_map/reduce_scatter | solution.py:327
  (694 shorter events, 464.0 us)
Async XLA Ops:
  7.2 264.7 %copy-start = (bf16[768,768]{1,0:T(8,128)(2,1)S(1)}, bf16[768,768]{1,0:T(8,128)(2,1)}, u32[]{:S(2)}) copy-start(bf16[768,768]{1,0:T(8,128)(2,1)} %param.29) | copy-start | bytes 3538948
  7.2 6.3 copy-start.27
  7.2 6.3 copy-start.18
  7.2 900.3 %reduce-scatter.7.cloned.1.call-start = ((), (), s32[]{:S(2)}) async-start(), calls=%async_computation.5 | async-start | bytes 2433024 | tf_op jit(solution)/shard_map/reduce_scatter | solution.py:321
  45.5 12.7 %copy-start.35 = (s32[1,4]{1,0:T(1,128)S(1)}, s32[1,4]{1,0:T(1,128)}, u32[]{:S(2)}) copy-start(s32[1,4]{1,0:T(1,128)} %param.25) | copy-start | bytes 52
  98.8 8.9 copy-start.17
  98.8 8.8 copy-start.24
  197.7 74.2 %copy-start.20 = (bf16[1024,768]{0,1:T(8,128)(2,1)S(1)}, bf16[1024,768]{0,1:T(8,128)(2,1)}, u32[]{:S(2)}) copy-start(bf16[1024,768]{0,1:T(8,128)(2,1)} %copy.78) | copy-start | bytes 4718596
  197.7 74.2 %copy-start.32 = (f32[768]{0:T(1024)S(1)}, f32[768]{0:T(1024)}, u32[]{:S(2)}) copy-start(f32[768]{0:T(1024)} %param.30) | copy-start | bytes 9220
  271.9 38.7 %slice-start = ((s8[4718592]{0:T(1024)(128)(4,1)}), s8[4194304]{0:T(1024)(128)(4,1)S(1)}, s32[]{:S(2)}) async-start(s8[4718592]{0:T(1024)(128)(4,1)} %bitcast.409), calls=%async_computation.8 | async-start | bytes 8388608
  274.9 35.7 %copy-start.7 = (f32[1024,768]{0,1:T(8,128)}, f32[1024,768]{0,1:T(8,128)S(1)}, u32[]{:S(2)}) copy-start(f32[1024,768]{0,1:T(8,128)S(1)} %get-tuple-element.839) | copy-start | bytes 9437188
  275.7 34.9 %slice-start.1 = ((s8[4718592]{0:T(1024)(128)(4,1)}), s8[524288]{0:T(1024)(128)(4,1)S(1)}, s32[]{:S(2)}) async-start(s8[4718592]{0:T(1024)(128)(4,1)} %bitcast.409), calls=%async_computation.9 | async-start | bytes 1048576
  275.7 34.9 %copy-start.33 = (f32[768]{0:T(1024)S(1)}, f32[768]{0:T(1024)}, u32[]{:S(2)}) copy-start(f32[768]{0:T(1024)} %param.36) | copy-start | bytes 9220
  319.8 18.1 %copy-start.5 = (bf16[1024,768]{0,1:T(8,128)(2,1)}, bf16[1024,768]{0,1:T(8,128)(2,1)S(1)}, u32[]{:S(2)}) copy-start(bf16[1024,768]{0,1:T(8,128)(2,1)S(1)} %copy.84) | copy-start | bytes 4718596
  323.2 14.7 %copy-start.8 = (f32[1024,768]{0,1:T(8,128)S(1)}, f32[1024,768]{0,1:T(8,128)}, u32[]{:S(2)}) copy-start(f32[1024,768]{0,1:T(8,128)} %copy-done.7) | copy-start | bytes 9437188
  337.9 10.8 copy-start.36
  355.3 552.3 %reduce-scatter.5.cloned.1.call-start = ((), (), s32[]{:S(2)}) async-start(), calls=%async_computation.4 | async-start | bytes 7299072 | tf_op jit(solution)/shard_map/reduce_scatter | solution.py:315
  538.6 6.3 copy-start.22
  556.7 6.3 copy-start.22
  574.8 6.3 copy-start.22
  593.0 6.3 copy-start.22
  611.1 6.3 copy-start.22
  629.2 6.3 copy-start.22
  647.4 6.3 copy-start.22
  665.5 6.3 copy-start.22
  683.6 6.3 copy-start.22
  701.7 6.3 copy-start.22
  719.9 6.3 copy-start.22
  738.0 6.3 copy-start.22
  778.7 261.1 %reduce-scatter.11.cloned.1.call-start = ((), (), s32[]{:S(2)}) async-start(), calls=%async_computation.7 | async-start | bytes 9732096 | tf_op jit(solution)/shard_map/reduce_scatter | solution.py:333
  813.5 368.2 %reduce-scatter.9.cloned.1.call-start = ((), (), s32[]{:S(2)}) async-start(), calls=%async_computation.6 | async-start | bytes 9732096 | tf_op jit(solution)/shard_map/reduce_scatter | solution.py:327
  852.0 329.8 %copy-start.1 = (bf16[768,768]{1,0:T(8,128)(2,1)S(1)}, bf16[768,768]{1,0:T(8,128)(2,1)}, u32[]{:S(2)}) copy-start(bf16[768,768]{1,0:T(8,128)(2,1)} %param.29) | copy-start | bytes 3538948
  (47 other events, 141.0 us)
Sparse Core Ops, SparseCore 0:
  355.4 99.3 reduce-scatter.6
  778.9 119.8 reduce-scatter.4
  905.2 134.6 reduce-scatter.10
  1047.2 134.4 reduce-scatter.8
where the time goes:
time: 1210 us; the launch traced here: 1190 us
  matrix products  381 us (31%)
  waiting for transfers between devices  274 us (23%)
  blocking collectives  196 us (16%)
  local copies, waits for them, and re-layouts  183 us (15%)
  other arithmetic  136 us (11%)
  between operations  14.5 us (1%)
    reduce_scatter x1, waiting for transfers between devices, tokens_plan(): lax.psum_scatter(owner_blocks(grad_up_weight, dp_count, head_count), ('dp...  142 us
    reduce_scatter x1, waiting for transfers between devices, tokens_plan(): lax.psum_scatter(owner_blocks(grad_down_weight, dp_count, head_count), ('...  132 us
    psum x1, blocking collectives, tokens_plan(): state_sum, norm_sum = lax.psum((state_part, norm_part), 'head')  80 us
    psum x1, blocking collectives, tokens_plan(): lax.psum((grad_state_part, grad_norm_part), 'head')  75.5 us
    dot_general x24, matrix products, rows_grad(): jnp.dot(grad_log, map_head.T, preferred_element_type=jnp.float32)  54.1 us
    unnamed x87, local copies, waits for them, and re-layouts  47.9 us
    psum x1, blocking collectives, body(): lax.psum((qkv_bias_full, up_bias_full, vectors), ('dp', 'head'))  40.8 us
    dot_general x1, matrix products, tokens_plan(): jnp.dot(normed_bf, up_weight, preferred_element_type=jnp.float32) + up_bias  34.8 us
  transfers between devices with their start and end apart: 4, of which 2 were waited for; matrix products, arithmetic and copies ran while one was open for 36% of the time, Pallas kernels for 0%

commit v1 on v0

v1 whole, which is shorter than its diff:
```python
import functools

import jax
import jax.numpy as jnp
from jax import lax
from jax.experimental import pallas as pl
from jax.experimental.pallas import tpu as pltpu
from jax.sharding import PartitionSpec as P

bf16 = jnp.bfloat16
f32 = jnp.float32
norm_epsilon = 1e-06
root_half = 0.7071067811865476
inv_root_tau = 0.3989422804014327
vmem_limit = 60 * 1024 * 1024
nt_dims = (((1,), (1,)), ((), ()))


def mm(a, b):
    return jnp.dot(a, b, preferred_element_type=f32)


def mm_nt(a, b):
    return lax.dot_general(a, b, nt_dims, preferred_element_type=f32)


def iota(shape, dim):
    return lax.broadcasted_iota(jnp.int32, shape, dim)


def bounds(len_ref, nseg):
    starts, ends, run = [], [], jnp.int32(0)
    for s in range(nseg):
        starts.append(run)
        run = run + len_ref[0, s]
        ends.append(run)
    return starts, ends


def spanning(ends, half):
    count = jnp.int32(0)
    for end in ends:
        count = count + (end < half).astype(jnp.int32)
    return count


def pick(index, values):
    out = jnp.full(index.shape, values[-1], jnp.int32)
    for s in range(len(values) - 2, -1, -1):
        out = jnp.where(index == s, values[s], out)
    return out


def inside(pos, index, starts, ends):
    return jnp.logical_and(pos >= pick(index, starts), pos < pick(index, ends))


def as_bf(mask):
    return jnp.where(mask, 1.0, 0.0).astype(bf16)


def split_hi_lo(v):
    hi = v.astype(bf16)
    lo = (v - hi.astype(f32)).astype(bf16)
    return jnp.concatenate([hi, lo], axis=1)


def masked_rows(rows_t, lane_masks, tail):
    return jnp.concatenate([rows_t * m for m in lane_masks] + [tail], axis=0)


def head_map(map_ref, h):
    m = map_ref[h]
    z = jnp.zeros_like(m)
    return jnp.concatenate([m, z] if h % 2 == 0 else [z, m], axis=0)


def key_offset(k_pair, low_half, j):
    sq = jnp.square(k_pair.astype(f32))
    mine = low_half if j == 0 else jnp.logical_not(low_half)
    return jnp.sum(jnp.where(mine, sq, 0.0), axis=-1, keepdims=True)


def put_states(own_ref, tot_ref, span_ref, recv_ref, st_ref, totp_ref, here, nseg, heads, hdim):
    wide = nseg * hdim
    feat = st_ref.shape[1]
    recv_tot = recv_ref[heads * hdim :, :].astype(f32)
    seg_row = iota((8, feat), 0)
    for h in range(heads):
        st_ref[h * wide : (h + 1) * wide, :] = own_ref[h * wide : (h + 1) * wide, :]
        both = span_ref[h * hdim : (h + 1) * hdim, :] + recv_ref[h * hdim : (h + 1) * hdim, :].astype(f32)
        at = pl.multiple_of(h * wide + here * hdim, hdim)
        st_ref[pl.ds(at, hdim), :] = both.astype(bf16)
        tot = tot_ref[8 * h : 8 * h + 8, :]
        tot = jnp.where(seg_row == here, tot + recv_tot[h : h + 1, :], tot)
        parts = [tot]
        if h > 0:
            parts.insert(0, jnp.zeros((8 * h, feat), f32))
        if 8 * h + 8 < 128:
            parts.append(jnp.zeros((128 - 8 * h - 8, feat), f32))
        totp_ref[128 * h : 128 * (h + 1), :] = jnp.concatenate(parts, axis=0).astype(bf16)


def emit_states(acc_ref, own_ref, tot_ref, span_ref, send_ref, here, nseg, heads, hdim):
    wide = nseg * hdim
    feat = acc_ref.shape[2]
    for h in range(heads):
        own_ref[h * wide : (h + 1) * wide, :] = acc_ref[h, 0:wide, :].astype(bf16)
        tot_ref[8 * h : 8 * h + 8, :] = acc_ref[h, wide : wide + 8, :]
        at = pl.multiple_of(here * hdim, hdim)
        part = acc_ref[h, pl.ds(at, hdim), :]
        span_ref[h * hdim : (h + 1) * hdim, :] = part
        send_ref[h * hdim : (h + 1) * hdim, :] = part.astype(bf16)
    row = iota((16, feat), 0)
    seg_row = iota((8, feat), 0)
    tots = jnp.zeros((16, feat), f32)
    for h in range(heads):
        mine = jnp.sum(jnp.where(seg_row == here, acc_ref[h, wide : wide + 8, :], 0.0), axis=0, keepdims=True)
        tots = jnp.where(row == h, mine, tots)
    send_ref[heads * hdim :, :] = tots.astype(bf16)


def lane_segment_masks(first, rows, hdim, starts, ends):
    pos = first + iota((hdim, rows), 1)
    masks = [as_bf(jnp.logical_and(pos >= a, pos < b)) for a, b in zip(starts, ends)]
    pos = first + iota((16, rows), 1)
    seg = iota((16, rows), 0)
    tail = as_bf(jnp.logical_and(seg < len(starts), inside(pos, seg, starts, ends)))
    return masks, tail


def forward_keys(
    len_ref, tok_ref, w_ref, b_ref, map_ref, qkv_ref, own_ref, tot_ref, span_ref, send_ref, acc_ref,
    *, half, nseg, heads, hdim, width
):
    step = pl.program_id(0)
    rows = tok_ref.shape[0]
    starts, ends = bounds(len_ref, nseg)
    here = spanning(ends, half)
    first = lax.axis_index("head") * half + step * rows
    factor = hdim ** (-0.25)

    @pl.when(step == 0)
    def _():
        acc_ref[...] = jnp.zeros_like(acc_ref)

    masks, tail = lane_segment_masks(first, rows, hdim, starts, ends)
    qkv_ref[...] = (mm(tok_ref[...], w_ref[...]) + b_ref[...]).astype(bf16)
    low_half = iota((rows, 128), 1) < hdim
    for p in range(heads // 2):
        k_pair = qkv_ref[:, width + 128 * p : width + 128 * (p + 1)]
        v_t = qkv_ref[:, 2 * width + 128 * p : 2 * width + 128 * (p + 1)].T
        for j in range(2):
            h = 2 * p + j
            logits = factor * mm(k_pair, head_map(map_ref, h)) - (0.5 * factor * factor) * key_offset(k_pair, low_half, j)
            feats = jnp.exp(logits).astype(bf16)
            lhs = masked_rows(v_t[j * hdim : (j + 1) * hdim, :], masks, tail)
            acc_ref[h] += mm(lhs, feats)

    @pl.when(step == pl.num_programs(0) - 1)
    def _():
        emit_states(acc_ref, own_ref, tot_ref, span_ref, send_ref, here, nseg, heads, hdim)


def norm_backward(incoming, scaled, inverse, gain):
    weighted = incoming * gain
    return inverse * (
        weighted
        - jnp.mean(weighted, axis=-1, keepdims=True)
        - scaled * jnp.mean(weighted * scaled, axis=-1, keepdims=True)
    )


def norm_parts(values):
    centred = values - jnp.mean(values, axis=-1, keepdims=True)
    spread = jnp.mean(centred * centred, axis=-1, keepdims=True)
    inverse = lax.rsqrt(spread + norm_epsilon)
    return centred * inverse, inverse


def gelu_parts(u):
    bell = jnp.exp(-0.5 * (u * u))
    t = 1.0 / (1.0 + (0.3275911 * root_half) * jnp.abs(u))
    poly = 0.5 * 1.061405429
    for c in (-1.453152027, 1.421413741, -0.284496736, 0.254829592):
        poly = poly * t + 0.5 * c
    tail = poly * t * bell
    cdf = jnp.where(u < 0.0, tail, 1.0 - tail)
    return u * cdf, cdf + u * (inv_root_tau * bell)


def chain(
    len_ref, tok_ref, q_ref, map_ref, own_ref, tot_ref, span_ref, recv_ref, wo_ref, bo_ref, g1_ref, s1_ref,
    wup_ref, bup_ref, wdn_ref, bdn_ref, g2_ref, s2_ref, cot_ref,
    out_ref, normed_ref, act_ref, bgrad_ref, ugrad_ref, agrad_ref, mixed_ref, num_ref, dgm_ref,
    st_ref, totp_ref, sown_ref, stot_ref, sspan_ref, ssend_ref, vec_ref,
    qf_ref, slope_ref, acc_ref,
    *, half, nseg, heads, hdim, chunk
):
    step = pl.program_id(0)
    rows, width = tok_ref.shape
    feat = map_ref.shape[2]
    wide = nseg * hdim
    starts, ends = bounds(len_ref, nseg)
    here = spanning(ends, half)
    first = lax.axis_index("head") * half + step * rows
    factor = hdim ** (-0.25)

    @pl.when(step == 0)
    def _():
        acc_ref[...] = jnp.zeros_like(acc_ref)
        vec_ref[...] = jnp.zeros_like(vec_ref)
        put_states(own_ref, tot_ref, span_ref, recv_ref, st_ref, totp_ref, here, nseg, heads, hdim)

    pos = first + iota((rows, wide), 0)
    seg_wide = inside(pos, iota((rows, wide), 1) // hdim, starts, ends)
    lane8 = iota((rows, 128), 1) % 8
    pos8 = first + iota((rows, 128), 0)
    seg8 = jnp.logical_and(lane8 < nseg, inside(pos8, lane8, starts, ends))
    total_end = ends[-1]
    low_half = iota((rows, 128), 1) < hdim

    nums = []
    den_c = jnp.zeros((rows, 128), f32)
    for p in range(heads // 2):
        q_pair = q_ref[:, 128 * p : 128 * (p + 1)]
        folded = []
        for j in range(2):
            h = 2 * p + j
            proj = mm(q_pair, head_map(map_ref, h))
            feats = jnp.exp(factor * (proj - jnp.max(proj, axis=-1, keepdims=True))).astype(bf16)
            qf_ref[:, feat * h : feat * (h + 1)] = feats
            den_c += mm_nt(feats, totp_ref[128 * h : 128 * (h + 1), :])
            r = jnp.where(seg_wide, mm_nt(feats, st_ref[wide * h : wide * (h + 1), :]), 0.0)
            folded.append(r[:, :128] + r[:, 128:])
        straight = jnp.where(low_half, folded[0], folded[1])
        crossed = jnp.where(low_half, folded[1], folded[0])
        nums.append(straight + pltpu.roll(crossed, hdim, 1))
    numer = jnp.concatenate(nums, axis=1)
    den_parts = split_hi_lo(jnp.where(seg8, den_c, 0.0))
    row_h = (iota((256, width), 0) % 128) // 8
    expand = as_bf(row_h == iota((256, width), 1) // hdim)
    same8 = as_bf((iota((256, 128), 0) % 128) // 8 == iota((256, 128), 1) // 8)
    dead = jnp.where(first + iota((rows, 128), 0) < total_end, 0.0, 1.0)
    spare = jnp.where(iota((rows, 128), 1) < 8 * heads, dead, 1.0)
    inv_c = 1.0 / (mm(den_parts, same8) + spare)
    den_w = mm(den_parts, expand) + jnp.concatenate([dead] * (width // 128), axis=1)
    inv_w = 1.0 / den_w
    ratio = numer * inv_w
    mixed = ratio.astype(bf16)
    mixed_ref[...] = mixed

    hidden = tok_ref[...].astype(f32) + mm_nt(mixed, wo_ref[...]) + bo_ref[...]
    scaled1, inverse1 = norm_parts(hidden)
    normed = scaled1 * g1_ref[...] + s1_ref[...]
    normed_bf = normed.astype(bf16)
    normed_ref[...] = normed_bf
    branch = jnp.zeros((rows, width), f32)
    hidden_units = wup_ref.shape[1]
    for c in range(hidden_units // chunk):
        cols = slice(c * chunk, (c + 1) * chunk)
        up = mm(normed_bf, wup_ref[:, cols]) + bup_ref[:, cols]
        act, slope = gelu_parts(up)
        act = act.astype(bf16)
        act_ref[:, cols] = act
        slope_ref[:, cols] = slope
        branch += mm_nt(act, wdn_ref[:, cols])
    final = normed + branch + bdn_ref[...]
    scaled2, inverse2 = norm_parts(final)
    out_ref[...] = (scaled2 * g2_ref[...] + s2_ref[...]).astype(bf16)
    incoming = cot_ref[...].astype(f32)
    grad_final = norm_backward(incoming, scaled2, inverse2, g2_ref[...])
    bgrad = grad_final.astype(bf16)
    bgrad_ref[...] = bgrad

    def add_row(row, values):
        vec_ref[row : row + 1, :] += jnp.sum(values, axis=0, keepdims=True)

    add_row(3, grad_final)
    add_row(4, incoming * scaled2)
    add_row(5, incoming)
    back = jnp.zeros((rows, width), f32)
    for c in range(hidden_units // chunk):
        cols = slice(c * chunk, (c + 1) * chunk)
        ugrad = (mm(bgrad, wdn_ref[:, cols]) * slope_ref[:, cols]).astype(bf16)
        ugrad_ref[:, cols] = ugrad
        sums = jnp.sum(ugrad.astype(f32), axis=0, keepdims=True)
        for k in range(chunk // width):
            row = 6 + (c * chunk) // width + k
            vec_ref[row : row + 1, :] += sums[:, k * width : (k + 1) * width]
        back += mm_nt(ugrad, wup_ref[:, cols])
    grad_normed = grad_final + back
    grad_hidden = norm_backward(grad_normed, scaled1, inverse1, g1_ref[...])
    add_row(0, grad_hidden)
    add_row(1, grad_normed * scaled1)
    add_row(2, grad_normed)
    agrad = grad_hidden.astype(bf16)
    agrad_ref[...] = agrad

    grad_mixed = mm(agrad, wo_ref[...])
    num_grad = (grad_mixed * inv_w).astype(bf16)
    num_ref[...] = num_grad
    inner = split_hi_lo(grad_mixed * ratio)
    gather = as_bf((iota((2 * width, 128), 0) % width) // hdim == iota((2 * width, 128), 1) // 8)
    den_grad = -(mm(inner, gather) * inv_c)
    den_m = jnp.where(seg8, den_grad, 0.0).astype(bf16)
    dgm_ref[...] = den_m
    den_t = den_m.T
    masks, _ = lane_segment_masks(first, rows, hdim, starts, ends)
    pad = jnp.zeros((8, rows), bf16)
    for p in range(heads // 2):
        num_t = num_grad[:, 128 * p : 128 * (p + 1)].T
        tails = den_t[16 * p : 16 * p + 16, :]
        for j in range(2):
            h = 2 * p + j
            tail = jnp.concatenate([tails[8 * j : 8 * j + 8, :], pad], axis=0)
            lhs = masked_rows(num_t[j * hdim : (j + 1) * hdim, :], masks, tail)
            acc_ref[h] += mm(lhs, qf_ref[:, feat * h : feat * (h + 1)])

    @pl.when(step == pl.num_programs(0) - 1)
    def _():
        emit_states(acc_ref, sown_ref, stot_ref, sspan_ref, ssend_ref, here, nseg, heads, hdim)


def replicate(pair, low_half, hdim):
    wide = pair.astype(f32)
    other = pltpu.roll(wide, hdim, 1)
    return (jnp.where(low_half, wide, other).astype(bf16), jnp.where(low_half, other, wide).astype(bf16))


def attention_back(
    len_ref, qkv_ref, num_ref, dgm_ref, map_ref, st_ref, totp_ref, sown_ref, stot_ref, sspan_ref, srecv_ref,
    pg_ref, vec_ref, sg_ref, sgt_ref, mapg_ref,
    *, half, nseg, heads, hdim, width
):
    step = pl.program_id(0)
    rows = qkv_ref.shape[0]
    feat = map_ref.shape[2]
    wide = nseg * hdim
    starts, ends = bounds(len_ref, nseg)
    here = spanning(ends, half)
    first = lax.axis_index("head") * half + step * rows
    factor = hdim ** (-0.25)

    @pl.when(step == 0)
    def _():
        vec_ref[...] = jnp.zeros_like(vec_ref)
        put_states(sown_ref, stot_ref, sspan_ref, srecv_ref, sg_ref, sgt_ref, here, nseg, heads, hdim)
        one, zero = jnp.ones((hdim, feat), bf16), jnp.zeros((hdim, feat), bf16)
        for p in range(heads // 2):
            left = jnp.concatenate([map_ref[2 * p], zero, one, zero], axis=0)
            right = jnp.concatenate([zero, map_ref[2 * p + 1], zero, one], axis=0)
            mapg_ref[p] = jnp.concatenate([left, right], axis=1)

    pos = first + iota((rows, wide), 0)
    seg_wide = inside(pos, iota((rows, wide), 1) // hdim, starts, ends)
    seg_wide_bf = as_bf(seg_wide)
    lane8 = iota((rows, 128), 1) % 8
    pos8 = first + iota((rows, 128), 0)
    seg8_bf = as_bf(jnp.logical_and(lane8 < nseg, inside(pos8, lane8, starts, ends)))
    low_half = iota((rows, 128), 1) < hdim
    den_m = dgm_ref[...]

    for p in range(heads // 2):
        q_pair = qkv_ref[:, 128 * p : 128 * (p + 1)]
        k_pair = qkv_ref[:, width + 128 * p : width + 128 * (p + 1)]
        v_pair = qkv_ref[:, 2 * width + 128 * p : 2 * width + 128 * (p + 1)]
        num_reps = replicate(num_ref[:, 128 * p : 128 * (p + 1)], low_half, hdim)
        v_reps = replicate(v_pair, low_half, hdim)
        q_logs, k_logs, folded = [], [], []
        for j in range(2):
            h = 2 * p + j
            own_map = head_map(map_ref, h)
            proj = mm(q_pair, own_map)
            shifted = proj - jnp.max(proj, axis=-1, keepdims=True)
            lhs = jnp.concatenate([num_reps[j]] * 2, axis=1) * seg_wide_bf
            q_slope = mm(lhs, st_ref[wide * h : wide * (h + 1), :]) + mm(den_m, totp_ref[128 * h : 128 * (h + 1), :])
            q_slope = q_slope * jnp.exp(factor * shifted)
            peak = jnp.where(shifted == 0.0, 1.0, 0.0)
            share = jnp.sum(q_slope, axis=-1, keepdims=True) / jnp.sum(peak, axis=-1, keepdims=True)
            q_logs.append((q_slope - peak * share).astype(bf16))

            logits = factor * mm(k_pair, own_map) - (0.5 * factor * factor) * key_offset(k_pair, low_half, j)
            k_exp = jnp.exp(logits)
            lhs = jnp.concatenate([v_reps[j]] * 2, axis=1) * seg_wide_bf
            state_grad = sg_ref[wide * h : wide * (h + 1), :]
            k_slope = mm(lhs, state_grad) + mm(seg8_bf, sgt_ref[128 * h : 128 * (h + 1), :])
            k_logs.append((k_slope * k_exp).astype(bf16))
            r = jnp.where(seg_wide, mm_nt(k_exp.astype(bf16), state_grad), 0.0)
            folded.append(r[:, :128] + r[:, 128:])
        straight = jnp.where(low_half, folded[0], folded[1])
        crossed = jnp.where(low_half, folded[1], folded[0])
        v_grad = (straight + pltpu.roll(crossed, hdim, 1)).astype(bf16)
        for at, rows_bf, logs in ((0, q_pair, q_logs), (1, k_pair, k_logs)):
            r = mm_nt(jnp.concatenate(logs, axis=1), mapg_ref[p])
            grad = factor * r[:, :128] - (factor * factor) * rows_bf.astype(f32) * r[:, 128:]
            pg_ref[:, at * width + 128 * p : at * width + 128 * (p + 1)] = grad.astype(bf16)
        pg_ref[:, 2 * width + 128 * p : 2 * width + 128 * (p + 1)] = v_grad
    for at in range(3):
        grads = pg_ref[:, at * width : (at + 1) * width].astype(f32)
        vec_ref[at : at + 1, :] += jnp.sum(grads, axis=0, keepdims=True)


def weight_grads(normed_ref, bgrad_ref, agrad_ref, ugrad_ref, act_ref, mixed_ref, dup_ref, ddn_ref, dout_ref, nt_ref, bt_ref, at_ref):
    @pl.when(pl.program_id(0) == 0)
    def _():
        nt_ref[...] = normed_ref[...].T
        bt_ref[...] = bgrad_ref[...].T
        at_ref[...] = agrad_ref[...].T

    ddn_ref[...] = mm(bt_ref[...], act_ref[...]).astype(bf16)
    dup_ref[...] = mm(nt_ref[...], ugrad_ref[...]).astype(bf16)
    dout_ref[...] = mm(at_ref[...], mixed_ref[...]).astype(bf16)


def qkv_weight_grads(tok_ref, pg_ref, dw_ref, tt_ref):
    @pl.when(pl.program_id(0) == 0)
    def _():
        tt_ref[...] = tok_ref[...].T

    dw_ref[...] = mm(tt_ref[...], pg_ref[...]).astype(bf16)


def params(flops=0, moved=0):
    return dict(
        compiler_params=pltpu.CompilerParams(vmem_limit_bytes=vmem_limit),
        cost_estimate=pl.CostEstimate(flops=int(flops), bytes_accessed=int(moved), transcendentals=0),
    )


def whole(shape):
    return pl.BlockSpec(shape, lambda i: (0,) * len(shape), pipeline_mode=pl.Buffered(1))


def resident(shape):
    return pl.BlockSpec(shape, lambda i: (0,) * len(shape))


def sds(shape, dtype):
    return jax.ShapeDtypeStruct(shape, dtype)


def reduce_scatter(grad, dp_count, order):
    bits = dp_count.bit_length() - 1
    row_count = grad.shape[0] // dp_count
    left = list(range(bits - 1, -1, -1))
    me = lax.axis_index("dp")
    x = lax.axis_index("head")
    part = grad.reshape((2,) * bits + (row_count, grad.shape[1]))
    for n, stage in enumerate(order):
        if stage == "x":
            axis, pairs, mine = "head", [(0, 1), (1, 0)], x
            half = part.shape[-1] // 2
            send = lax.dynamic_slice_in_dim(part, (1 - x) * half, half, axis=part.ndim - 1)
            keep = lax.dynamic_slice_in_dim(part, x * half, half, axis=part.ndim - 1)
        else:
            axis, pairs = "dp", [(i, i ^ (1 << stage)) for i in range(dp_count)]
            mine = (me >> stage) & 1
            dim = left.index(stage)
            left.remove(stage)
            send = lax.dynamic_index_in_dim(part, 1 - mine, dim, keepdims=False)
            keep = lax.dynamic_index_in_dim(part, mine, dim, keepdims=False)
        got = lax.ppermute(send, axis, pairs)
        part = keep.astype(f32) + got.astype(f32)
        if n < len(order) - 1:
            part = part.astype(bf16)
    return part


def sum_all(values, dp_count):
    for stage in ["x"] + list(range(dp_count.bit_length() - 1)):
        if stage == "x":
            got = lax.ppermute(values, "head", [(0, 1), (1, 0)])
        else:
            got = lax.ppermute(values, "dp", [(i, i ^ (1 << stage)) for i in range(dp_count)])
        values = values + got
    return values


def body(
    tokens, lengths, feature_map, qkv_weight, qkv_bias, out_weight, out_bias, ln1_gain, ln1_shift,
    up_weight, up_bias, down_weight, down_bias, ln2_gain, ln2_shift, cotangent,
):
    half, width = tokens.shape
    heads, hdim, feat = feature_map.shape
    nseg = lengths.shape[1]
    hidden_units = up_weight.shape[1]
    wide = nseg * hdim
    dp_count = lax.axis_size("dp")
    head_count = lax.axis_size("head")
    bits = dp_count.bit_length() - 1
    assert head_count == 2 and dp_count == 1 << bits and 2 * hdim == 128 and wide == 256 and 8 * heads <= 128
    flat_w = qkv_weight.reshape(width, 3 * width)
    flat_b = qkv_bias.reshape(1, 3 * width)
    rows = min(256, half)
    steps = half // rows
    span_rows = heads * hdim + 16
    state_shapes = [
        sds((heads * wide, feat), bf16), sds((heads * 8, feat), f32),
        sds((span_rows - 16, feat), f32), sds((span_rows, feat), bf16),
    ]
    state_specs = [resident(s.shape) for s in state_shapes]
    lens = pl.BlockSpec(memory_space=pltpu.SMEM)

    def tile(cols, col=0):
        return pl.BlockSpec((rows, cols), lambda i: (i, col))

    static = dict(half=half, nseg=nseg, heads=heads, hdim=hdim)
    dense = 2 * half * width

    qkv, own, tot, span, send = pl.pallas_call(
        functools.partial(forward_keys, width=width, **static),
        grid=(steps,),
        in_specs=[lens, tile(width), whole(flat_w.shape), whole(flat_b.shape), whole(feature_map.shape)],
        out_specs=[tile(3 * width)] + state_specs,
        out_shape=[sds((half, 3 * width), bf16)] + state_shapes,
        scratch_shapes=[pltpu.VMEM((heads, wide + 16, feat), f32)],
        **params(dense * 3 * width, 16e6),
    )(lengths, tokens, flat_w, flat_b, feature_map)
    recv = lax.ppermute(send, "head", [(0, 1), (1, 0)])

    row = lambda v: v.reshape(1, -1)
    vec_rows = 6 + hidden_units // width
    vec_rows += -vec_rows % 8
    chunk = width
    (output, normed, act, bgrad, ugrad, agrad, mixed, num_grad, den_m, states, totals, s_own, s_tot, s_span, s_send, vec_b) = pl.pallas_call(
        functools.partial(chain, chunk=chunk, **static),
        grid=(steps,),
        in_specs=[lens, tile(width), tile(width), whole(feature_map.shape)]
        + [whole(v.shape) for v in (own, tot, span, recv)]
        + [whole(out_weight.shape), whole((1, width)), whole((1, width)), whole((1, width))]
        + [whole(up_weight.shape), whole((1, hidden_units)), whole(down_weight.shape)]
        + [whole((1, width))] * 3
        + [tile(width)],
        out_specs=[tile(width), tile(width), tile(hidden_units), tile(width), tile(hidden_units), tile(width), tile(width), tile(width), tile(128)]
        + [resident((heads * wide, feat)), resident((heads * 128, feat))]
        + state_specs
        + [resident((vec_rows, width))],
        out_shape=[sds((half, c), bf16) for c in (width, width, hidden_units, width, hidden_units, width, width, width, 128)]
        + [sds((heads * wide, feat), bf16), sds((heads * 128, feat), bf16)]
        + state_shapes
        + [sds((vec_rows, width), f32)],
        scratch_shapes=[
            pltpu.VMEM((rows, heads * feat), bf16),
            pltpu.VMEM((rows, hidden_units), f32),
            pltpu.VMEM((heads, wide + 16, feat), f32),
        ],
        **params(dense * (4 * hidden_units + 4 * width), 40e6),
    )(
        lengths, tokens, qkv, feature_map, own, tot, span, recv, out_weight, row(out_bias), row(ln1_gain), row(ln1_shift),
        up_weight, row(up_bias), down_weight, row(down_bias), row(ln2_gain), row(ln2_shift), cotangent,
    )
    s_recv = lax.ppermute(s_send, "head", [(0, 1), (1, 0)])

    cols = 512
    parts = hidden_units // cols
    out_cols = width // parts
    col_tile = lambda r, c: pl.BlockSpec((r, c), lambda i: (0, i))
    d_up, d_down, d_out = pl.pallas_call(
        weight_grads,
        grid=(parts,),
        in_specs=[whole((half, width))] * 3 + [col_tile(half, cols), col_tile(half, cols), col_tile(half, out_cols)],
        out_specs=[col_tile(width, cols), col_tile(width, cols), col_tile(width, out_cols)],
        out_shape=[sds((width, hidden_units), bf16), sds((width, hidden_units), bf16), sds((width, width), bf16)],
        scratch_shapes=[pltpu.VMEM((width, half), bf16)] * 3,
        **params(dense * (2 * hidden_units + width), 30e6),
    )(normed, bgrad, agrad, ugrad, act, mixed)

    proj_grad, vec_c = pl.pallas_call(
        functools.partial(attention_back, width=width, **static),
        grid=(steps,),
        in_specs=[lens, tile(3 * width), tile(width), tile(128), whole(feature_map.shape)]
        + [whole(v.shape) for v in (states, totals, s_own, s_tot, s_span, s_recv)],
        out_specs=[tile(3 * width), resident((8, width))],
        out_shape=[sds((half, 3 * width), bf16), sds((8, width), f32)],
        scratch_shapes=[
            pltpu.VMEM((heads * wide, feat), bf16),
            pltpu.VMEM((heads * 128, feat), bf16),
            pltpu.VMEM((heads // 2, 4 * hdim, 2 * feat), bf16),
        ],
        **params(dense * 3 * width, 16e6),
    )(lengths, qkv, num_grad, den_m, feature_map, states, totals, s_own, s_tot, s_span, s_recv)

    half_w = width // 2
    d_qkv = pl.pallas_call(
        qkv_weight_grads,
        grid=(6,),
        in_specs=[whole((half, width)), col_tile(half, half_w)],
        out_specs=pl.BlockSpec((width, half_w), lambda i: (0, (i % 2) * 3 + i // 2)),
        out_shape=sds((width, 3 * width), bf16),
        scratch_shapes=[pltpu.VMEM((width, half), bf16)],
        **params(dense * 3 * width, 10e6),
    )(tokens, proj_grad)
    grad_tokens = (agrad.astype(f32) + mm_nt(proj_grad, flat_w)).astype(bf16)

    upper = list(range(2, bits))
    order_a = [0, "x", 1] + upper
    order_b = [0, 1, "x"] + upper
    d_down = reduce_scatter(d_down, dp_count, order_a)
    d_up = reduce_scatter(d_up, dp_count, order_b)
    d_out = reduce_scatter(d_out, dp_count, order_a)
    d_qkv = reduce_scatter(d_qkv, dp_count, order_b)
    vectors = sum_all(jnp.concatenate([vec_b, vec_c], axis=0), dp_count)
    up_rows = hidden_units // width
    return (
        output,
        grad_tokens,
        d_qkv.reshape(-1, 3, half_w),
        vectors[vec_rows : vec_rows + 3],
        d_out,
        vectors[0],
        vectors[1],
        vectors[2],
        d_up,
        vectors[6 : 6 + up_rows].reshape(-1),
        d_down,
        vectors[3],
        vectors[4],
        vectors[5],
    )


def solution(mesh):
    rows = P(("dp", "head"), None)
    in_specs = (rows, P("dp", None)) + (P(),) * 13 + (rows,)
    out_specs = (
        rows, rows, P("dp", None, "head"), P(), P("dp", "head"), P(), P(), P(),
        P("dp", "head"), P(), P("dp", "head"), P(), P(), P(),
    )
    return jax.shard_map(body, mesh=mesh, in_specs=in_specs, out_specs=out_specs, check_vma=False)
```

time: 1210 us -> 309 us (0.26); the launches traced: 1190 us -> 305 us
  matrix products: 381 us -> 4.9 us
  waiting for transfers between devices: 274 us -> 76.4 us
  blocking collectives: 196 us -> 0 us
  local copies, waits for them, and re-layouts: 183 us -> 38.9 us
  Pallas kernels: 0 us -> 139 us
  other arithmetic: 136 us -> 16.5 us
  starting transfers between devices: 0.16 us -> 27.9 us
  between operations: 14.5 us -> 1.42 us
    dot_general x146 -> x1, matrix products: 372 us -> 4.9 us  [mm_nt(): return lax.dot_general(a, b, nt_dims, preferred_element_type=f32)]
    reduce_scatter x4 -> x0, waiting for transfers between devices: 274 us -> none  [the longest x1 142 us: tokens_plan(): lax.psum_scatter(owner_blocks(grad_up_weight, dp_count, head_count), ('dp...]
    psum x3 -> x0, blocking collectives: 196 us -> none  [the longest x1 80 us: tokens_plan(): state_sum, norm_sum = lax.psum((state_part, norm_part), 'head')]
    pallas_call x0 -> x5, Pallas kernels: none -> 139 us  [the longest x1 68.8 us: body(): pl.pallas_call(functools.partial(chain, chunk=chunk, **static), grid=(ste...]
    ppermute x0 -> x27, waiting for transfers between devices: none -> 76.4 us  [the longest x20 70.2 us: reduce_scatter(): got = lax.ppermute(send, axis, pairs)]
    reduce_sum x56 -> x0, other arithmetic: 61.8 us -> none  [the longest x24 25.2 us: rows_grad(): jnp.sum(grad_log.astype(jnp.float32), axis=-1, keepdims=True)]
    unnamed x87 -> x29, local copies, waits for them, and re-layouts: 47.9 us -> 6.32 us
    ppermute x0 -> x27, starting transfers between devices: none -> 27.9 us  [the longest x20 16.9 us: reduce_scatter(): got = lax.ppermute(send, axis, pairs)]
  transfers between devices with their start and end apart: 4 -> 27, of which waited for: 2 -> 14; matrix products, arithmetic and copies ran while one was open for 36% -> 16% of each run, Pallas kernels for 0% -> 10%
where the time goes in v1:
time: 309 us; the launch traced here: 305 us
  Pallas kernels  139 us (45%)
  waiting for transfers between devices  76.4 us (25%)
  local copies, waits for them, and re-layouts  38.9 us (13%)
  starting transfers between devices  27.9 us (9%)
  other arithmetic  16.5 us (5%)
  matrix products  4.9 us (2%)
    ppermute x20, waiting for transfers between devices, reduce_scatter(): got = lax.ppermute(send, axis, pairs)  70.2 us
    pallas_call x1, Pallas kernels, body(): pl.pallas_call(functools.partial(chain, chunk=chunk, **static), grid=(ste...  68.8 us
    pallas_call x1, Pallas kernels, body(): pl.pallas_call(functools.partial(attention_back, width=width, **static),...  24.9 us
    pallas_call x1, Pallas kernels, body(): pl.pallas_call(weight_grads, grid=(parts,), in_specs=[whole((half, width)...  19.5 us
    ppermute x20, starting transfers between devices, reduce_scatter(): got = lax.ppermute(send, axis, pairs)  16.9 us
    pallas_call x1, Pallas kernels, body(): pl.pallas_call(functools.partial(forward_keys, width=width, **static), gr...  16.2 us
    dynamic_slice x3, local copies, waits for them, and re-layouts, reduce_scatter(): keep = lax.dynamic_index_in_dim(part, mine, dim, keepdims=False)  12.9 us
    convert_element_type x16, other arithmetic, reduce_scatter(): part = part.astype(bf16)  11.8 us
  transfers between devices with their start and end apart: 27, of which 14 were waited for; matrix products, arithmetic and copies ran while one was open for 16% of the time, Pallas kernels for 10%

profile of v1, /device:TPU:0, one launch (start us, length us, event | category | flops | bytes accessed | tf_op | source)
XLA Modules:
  0.0 305.4 jit_solution(13434021690137575298)
XLA Ops:
  0.6 4.3 %copy.37 = bf16[768,3,768]{0,2,1:T(8,128)(2,1)S(1)} copy(bf16[768,3,768]{2,0,1:T(8,128)(2,1)} %param.19) | data formatting | bytes 7077888 | tf_op args[3]
  4.9 4.0 %copy.38.w_ref = bf16[768,2304]{1,0:T(8,128)(2,1)} copy(bf16[768,2304]{0,1:T(8,128)(2,1)S(1)} %bitcast.107) | data formatting | bytes 7077888 | tf_op jit(solution)/shard_map/reshape | solution.py:493
  9.6 16.2 %shard_map.263 = (bf16[1024,2304]{1,0:T(8,128)(2,1)}, bf16[3072,256]{1,0:T(8,128)(2,1)}, f32[96,256]{1,0:T(8,128)}, f32[768,256]{1,0:T(8,128)}, bf16[784,256]{1,0:T(8,128)(2,1)}) custom-call(s32[1,4]{1,0:T(1,128)} %len_ref.5, bf16[1024,768]{1,0:T(8,128)(2,1)} %tok_ref.5, bf16[768,2304]{1,0:T(8,128)(2,1)} %copy.38.w_ref, f32[1,2304]{1,0:T(1,128)} %bitcast.116, ...), custom_call_target="tpu_custom_call" | custom-call | flops 3623878656 | bytes 16000000 | tf_op jit(solution)/shard_map/pallas_call | solution.py:511
  25.8 3.0 collective-permute-start
  33.7 4.7 %collective-permute-done.recv_ref = bf16[784,256]{1,0:T(8,128)(2,1)} collective-permute-done((bf16[784,256]{1,0:T(8,128)(2,1)}, bf16[784,256]{1,0:T(8,128)(2,1)}, u32[]{:S(2)}, u32[]{:S(2)}) %collective-permute-start) | collective-permute-done | bytes 401440 | tf_op jit(solution)/shard_map/ppermute | solution.py:520
  38.4 68.8 %shard_map.264 = (bf16[1024,768]{1,0:T(8,128)(2,1)}, bf16[1024,768]{1,0:T(8,128)(2,1)}, bf16[1024,3072]{1,0:T(8,128)(2,1)}, bf16[1024,768]{1,0:T(8,128)(2,1)}, b...) custom-call(s32[1,4]{1,0:T(1,128)} %len_ref.5, ...), custom_call_target="tpu_custom_call" | custom-call | flops 24159191040 | bytes 40000000 | tf_op jit(solution)/shard_map/pallas_call | solution.py:526
  107.2 1.8 collective-permute-start.1
  109.0 19.5 %shard_map.267 = (bf16[768,3072]{1,0:T(8,128)(2,1)}, bf16[768,3072]{1,0:T(8,128)(2,1)}, bf16[768,768]{1,0:T(8,128)(2,1)}) custom-call(bf16[1024,768]{1,0:T(8,128)(2,1)} %get-tuple-element.58.normed_ref, bf16[1024,768]{1,0:T(8,128)(2,1)} %get-tuple-element.59.bgrad_ref, bf16[1024,768]{1,0:T(8,128)(2,1)} %get-tuple-element.46.agrad_ref, ...), custom_call_target="tpu_custom_call" | custom-call | flops 10871635968 | bytes 30000000 | tf_op jit(solution)/shard_map/pallas_call | solution.py:559
  129.9 24.9 %shard_map.265 = (bf16[1024,2304]{1,0:T(8,128)(2,1)}, f32[8,768]{1,0:T(8,128)}) custom-call(s32[1,4]{1,0:T(1,128)} %len_ref.5, bf16[1024,2304]{1,0:T(8,128)(2,1)} %get-tuple-element.40.q_ref.qkv_ref, bf16[1024,768]{1,0:T(8,128)(2,1)} %get-tuple-element.47.num_ref, bf16[1024,128]{1,0:T(8,128)(2,1)} %get-tuple-element.48.dgm_ref, ...), custom_call_target="tpu_custom_call" | custom-call | flops 3623878656 | bytes 16000000 | tf_op jit(solution)/shard_map/pallas_call | solution.py:569
  156.4 2.2 constant_dynamic-slice_fusion.8
  161.8 7.3 %constant_dynamic-slice_fusion.2 = (bf16[2,2,2,1,48,3072]{5,4,3,2,1,0:T(8,128)(2,1)}, bf16[2,2,2,1,48,3072]{5,4,3,2,1,0:T(8,128)(2,1)S(1)}, bf16[2,2,2,1,48,3072...) fusion(bf16[2,2,2,2,48,3072]{5,4,3,2,1,0:T(8,128)(2,1)} %bitcast.110, s32[]{:T(128)S(6)} %select_n.81, ...), kind=kLoop, calls=%fused_computation.56 | loop fusion | bytes 18874376 | tf_op jit(solution)/shard_map/jit(dynamic_index_in_dim)/dynamic_slice | solution.py:462
  169.1 1.7 copy.72
  177.9 10.0 %shard_map.266 = bf16[768,2304]{1,0:T(8,128)(2,1)} custom-call(bf16[1024,768]{1,0:T(8,128)(2,1)} %tok_ref.5, bf16[1024,2304]{1,0:T(8,128)(2,1)} %get-tuple-element.55.pg_ref), custom_call_target="tpu_custom_call" | custom-call | flops 3623878656 | bytes 10000000 | tf_op jit(solution)/shard_map/pallas_call | solution.py:585
  192.3 3.5 %constant_dynamic-slice_fusion.11 = (bf16[2,2,2,1,48,2304]{5,4,3,2,1,0:T(8,128)(2,1)}, bf16[2,2,2,1,48,2304]{5,4,3,2,1,0:T(8,128)(2,1)S(1)}) fusion(bf16[2,2,2,2,48,2304]{5,4,3,2,1,0:T(8,128)(2,1)} %bitcast.111, s32[]{:T(128)S(6)} %select_n.81, s32[]{:T(128)S(6)} %select_n.82), kind=kLoop, calls=%fused_computation.65 | loop fusion | bytes 7077896 | tf_op jit(solution)/shard_map/jit(dynamic_index_in_dim)/dynamic_slice | solution.py:462
  197.2 2.7 collective-permute-start.11
  200.5 4.9 %add_convert_fusion = bf16[1024,768]{1,0:T(8,128)(2,1)} fusion(bf16[1024,768]{1,0:T(8,128)(2,1)S(1)} %copy-done.10, bf16[1024,2304]{1,0:T(8,128)(2,1)S(1)} %bitcast.119, bf16[768,2304]{0,1:T(8,128)(2,1)S(1)} %bitcast.108), kind=kOutput, calls=%fused_computation.6 | convolution fusion | flops 3626237952 | bytes 11403264 | tf_op jit(solution)/shard_map/dot_general | solution.py:24
  207.9 3.0 collective-permute-done.16
  211.5 2.6 fusion.2
  215.8 2.6 fusion.1
  219.1 17.8 %collective-permute-done.3 = bf16[2,2,48,2304]{3,2,0,1:T(8,128)(2,1)S(1)} collective-permute-done((bf16[2,2,48,2304]{3,2,0,1:T(8,128)(2,1)S(1)}, bf16[2,2,48,2304]{3,2,0,1:T(8,128)(2,1)S(1)}, u32[]{:S(2)}, u32[]{:S(2)}) %collective-permute-start.3) | collective-permute-done | bytes 884768 | tf_op jit(solution)/shard_map/ppermute | solution.py:463
  238.3 2.6 fusion
  242.0 8.3 %collective-permute-done.4 = bf16[2,2,48,1152]{3,2,0,1:T(8,128)(2,1)S(1)} collective-permute-done((bf16[2,2,48,1152]{3,2,0,1:T(8,128)(2,1)S(1)}, bf16[2,2,48,1152]{3,2,0,1:T(8,128)(2,1)S(1)}, u32[]{:S(2)}, u32[]{:S(2)}) %collective-permute-start.4) | collective-permute-done | bytes 442400 | tf_op jit(solution)/shard_map/ppermute | solution.py:463
  251.6 8.3 %collective-permute-done.18 = bf16[2,2,48,3072]{3,2,0,1:T(8,128)(2,1)S(1)} collective-permute-done((bf16[2,2,48,3072]{3,2,0,1:T(8,128)(2,1)S(1)}, bf16[2,2,48,3072]{3,2,0,1:T(8,128)(2,1)S(1)}, u32[]{:S(2)}, u32[]{:S(2)}) %collective-permute-start.18) | collective-permute-done | bytes 1179680 | tf_op jit(solution)/shard_map/ppermute | solution.py:463
  261.6 13.9 %collective-permute-done.23 = bf16[2,2,2,48,1536]{4,3,0,1,2:T(8,128)(2,1)S(1)} collective-permute-done((bf16[2,2,2,48,1536]{4,3,0,1,2:T(8,128)(2,1)S(1)}, bf16[2,2,2,48,1536]{4,3,0,1,2:T(8,128)(2,1)S(1)}, u32[]{:S(2)}, u32[]{:S(2)}) %collective-permute-start.23) | collective-permute-done | bytes 1179680 | tf_op jit(solution)/shard_map/ppermute | solution.py:463
  277.7 5.3 %collective-permute-done.6 = bf16[48,1152]{1,0:T(8,128)(2,1)S(1)} collective-permute-done((bf16[48,1152]{1,0:T(8,128)(2,1)S(1)}, bf16[48,1152]{1,0:T(8,128)(2,1)S(1)}, u32[]{:S(2)}, u32[]{:S(2)}) %collective-permute-start.6) | collective-permute-done | bytes 110624 | tf_op jit(solution)/shard_map/ppermute | solution.py:463
  284.2 1.9 collective-permute-done.24
  286.3 1.9 collective-permute-start.25
  288.2 4.6 %collective-permute-done.20 = bf16[2,48,1536]{2,1,0:T(8,128)(2,1)S(1)} collective-permute-done((bf16[2,48,1536]{2,1,0:T(8,128)(2,1)S(1)}, bf16[2,48,1536]{2,1,0:T(8,128)(2,1)S(1)}, u32[]{:S(2)}, u32[]{:S(2)}) %collective-permute-start.20) | collective-permute-done | bytes 294944 | tf_op jit(solution)/shard_map/ppermute | solution.py:463
  292.9 1.9 collective-permute-start.21
  294.8 2.7 collective-permute-done.25
  297.6 2.0 collective-permute-start.26
  301.5 2.8 collective-permute-done.26
  (119 shorter events, 42.5 us)
Async XLA Ops:
  9.6 19.8 %copy-start.6 = (f32[768]{0:T(1024)S(1)}, f32[768]{0:T(1024)}, u32[]{:S(2)}) copy-start(f32[768]{0:T(1024)} %param.23) | copy-start | bytes 9220
  9.6 20.4 %copy-start.7 = (f32[768]{0:T(1024)S(1)}, f32[768]{0:T(1024)}, u32[]{:S(2)}) copy-start(f32[768]{0:T(1024)} %param.24) | copy-start | bytes 9220
  9.6 20.9 %copy-start.8 = (f32[768]{0:T(1024)S(1)}, f32[768]{0:T(1024)}, u32[]{:S(2)}) copy-start(f32[768]{0:T(1024)} %param.28) | copy-start | bytes 9220
  25.8 12.6 %collective-permute-start = (bf16[784,256]{1,0:T(8,128)(2,1)}, bf16[784,256]{1,0:T(8,128)(2,1)}, u32[]{:S(2)}, u32[]{:S(2)}) collective-permute-start(bf16[784,256]{1,0:T(8,128)(2,1)} %get-tuple-element.44), channel_id=1, source_target_pairs={{0,1},{1,0},{2,3},{3,2},{4,5},{5,4},{6,7},{7,6},{8,9},{9,8},{10,11... | collective-permute-start | bytes 1204232 | tf_op jit(solution)/shard_map/ppermute | solution.py:520
  107.2 22.0 %collective-permute-start.1 = (bf16[784,256]{1,0:T(8,128)(2,1)}, bf16[784,256]{1,0:T(8,128)(2,1)S(1)}, u32[]{:S(2)}, u32[]{:S(2)}) collective-permute-start(bf16[784,256]{1,0:T(8,128)(2,1)} %get-tuple-element.54), channel_id=1, source_target_pairs={{0,1},{1,0},{2,3},{3,2},{4,5},{5,4},{6,7},{7,6},{8,9},{9,8},{10,11... | collective-permute-start | bytes 1204232 | tf_op jit(solution)/shard_map/ppermute | solution.py:553
  109.0 19.5 %copy-start.3 = (f32[16,768]{1,0:T(8,128)S(1)}, f32[16,768]{1,0:T(8,128)}, u32[]{:S(2)}) copy-start(f32[16,768]{1,0:T(8,128)} %get-tuple-element.56) | copy-start | bytes 147460
  156.2 4.7 %collective-permute-start.7 = (f32[24,768]{1,0:T(8,128)}, f32[24,768]{1,0:T(8,128)}, u32[]{:S(2)}, u32[]{:S(2)}) collective-permute-start(f32[24,768]{1,0:T(8,128)} %constant_dynamic-update-slice_fusion), channel_id=1, source_target_pairs={{0,1},{1,0},{2,3},{3,2},{4,5},{5,4},{6,7},{7,6},{8,9},{9,8},{10,11... | collective-permute-start | bytes 221192 | tf_op jit(solution)/shard_map/ppermute | solution.py:473
  159.5 15.6 %collective-permute-start.12 = (bf16[2,2,2,48,768]{4,3,0,1,2:T(8,128)(2,1)}, bf16[2,2,2,48,768]{4,3,0,1,2:T(8,128)(2,1)}, u32[]{:S(2)}, u32[]{:S(2)}) collective-permute-start(bf16[2,2,2,48,768]{4,3,0,1,2:T(8,128)(2,1)} %bitcast.105), channel_id=1, source_target_pairs={{0,2},{2,0},{4,6},{6,4},{8,10},{10,8},{12,14},{14,12},{16,18},{18,... | collective-permute-start | bytes 1769480 | tf_op jit(solution)/shard_map/ppermute | solution.py:463
  161.8 11.2 %collective-permute-start.8 = (f32[24,768]{1,0:T(8,128)S(1)}, f32[24,768]{1,0:T(8,128)S(1)}, u32[]{:S(2)}, u32[]{:S(2)}) collective-permute-start(f32[24,768]{1,0:T(8,128)S(1)} %add.179), channel_id=1, source_target_pairs={{0,2},{2,0},{4,6},{6,4},{8,10},{10,8},{12,14},{14,12},{16,18},{18,... | collective-permute-start | bytes 221192 | tf_op jit(solution)/shard_map/ppermute | solution.py:475
  170.8 45.0 %collective-permute-start.17 = (bf16[2,2,2,48,3072]{4,3,0,1,2:T(8,128)(2,1)}, bf16[2,2,2,48,3072]{4,3,0,1,2:T(8,128)(2,1)}, u32[]{:S(2)}, u32[]{:S(2)}) collective-permute-start(bf16[2,2,2,48,3072]{4,3,0,1,2:T(8,128)(2,1)} %bitcast.103), channel_id=1, source_target_pairs={{0,2},{2,0},{4,6},{6,4},{8,10},{10,8},{12,14},{14,12},{16,18},{18,... | collective-permute-start | bytes 7077896 | tf_op jit(solution)/shard_map/ppermute | solution.py:463
  172.9 65.4 %collective-permute-start.22 = (bf16[2,2,2,48,3072]{4,3,0,1,2:T(8,128)(2,1)}, bf16[2,2,2,48,3072]{4,3,0,1,2:T(8,128)(2,1)}, u32[]{:S(2)}, u32[]{:S(2)}) collective-permute-start(bf16[2,2,2,48,3072]{4,3,0,1,2:T(8,128)(2,1)} %bitcast.102), channel_id=1, source_target_pairs={{0,2},{2,0},{4,6},{6,4},{8,10},{10,8},{12,14},{14,12},{16,18},{18,... | collective-permute-start | bytes 7077896 | tf_op jit(solution)/shard_map/ppermute | solution.py:463
  173.6 14.4 %collective-permute-start.9 = (f32[24,768]{1,0:T(8,128)}, f32[24,768]{1,0:T(8,128)}, u32[]{:S(2)}, u32[]{:S(2)}) collective-permute-start(f32[24,768]{1,0:T(8,128)} %add.180), channel_id=1, source_target_pairs={{0,4},{2,6},{4,0},{6,2},{8,12},{10,14},{12,8},{14,10},{16,20},{18,... | collective-permute-start | bytes 221192 | tf_op jit(solution)/shard_map/ppermute | solution.py:475
  177.1 13.5 %collective-permute-start.13 = (bf16[2,2,2,48,384]{4,3,0,1,2:T(8,128)(2,1)}, bf16[2,2,2,48,384]{4,3,0,1,2:T(8,128)(2,1)}, u32[]{:S(2)}, u32[]{:S(2)}) collective-permute-start(bf16[2,2,2,48,384]{4,3,0,1,2:T(8,128)(2,1)} %constant_dynamic-slice_fusion.6), channel_id=1, source_target_pairs={{0,1},{1,0},{2,3},{3,2},{4,5},{5,4},{6,7},{7,6},{8,9},{9,8},{10,11... | collective-permute-start | bytes 884744 | tf_op jit(solution)/shard_map/ppermute | solution.py:463
  188.9 8.3 %collective-permute-start.10 = (f32[24,768]{1,0:T(8,128)S(1)}, f32[24,768]{1,0:T(8,128)S(1)}, u32[]{:S(2)}, u32[]{:S(2)}) collective-permute-start(f32[24,768]{1,0:T(8,128)S(1)} %add.181), channel_id=1, source_target_pairs={{0,8},{2,10},{4,12},{6,14},{8,0},{10,2},{12,4},{14,6},{16,24},{18,... | collective-permute-start | bytes 221192 | tf_op jit(solution)/shard_map/ppermute | solution.py:475
  191.8 8.1 %collective-permute-start.14 = (bf16[2,2,48,384]{3,2,0,1:T(8,128)(2,1)S(1)}, bf16[2,2,48,384]{3,2,0,1:T(8,128)(2,1)S(1)}, u32[]{:S(2)}, u32[]{:S(2)}) collective-permute-start(bf16[2,2,48,384]{3,2,0,1:T(8,128)(2,1)S(1)} %dynamic-slice_bitcast_fusion.8), channel_id=1, source_target_pairs={{0,4},{2,6},{4,0},{6,2},{8,12},{10,14},{12,8},{14,10},{16,20},{18,... | collective-permute-start | bytes 442376 | tf_op jit(solution)/shard_map/ppermute | solution.py:463
  197.2 14.3 %collective-permute-start.2 = (bf16[2,2,2,48,2304]{4,3,0,1,2:T(8,128)(2,1)}, bf16[2,2,2,48,2304]{4,3,0,1,2:T(8,128)(2,1)}, u32[]{:S(2)}, u32[]{:S(2)}) collective-permute-start(bf16[2,2,2,48,2304]{4,3,0,1,2:T(8,128)(2,1)} %bitcast.104), channel_id=1, source_target_pairs={{0,2},{2,0},{4,6},{6,4},{8,10},{10,8},{12,14},{14,12},{16,18},{18,... | collective-permute-start | bytes 5308424 | tf_op jit(solution)/shard_map/ppermute | solution.py:463
  197.2 8.2 %collective-permute-start.11 = (f32[24,768]{1,0:T(8,128)S(1)}, f32[24,768]{1,0:T(8,128)S(1)}, u32[]{:S(2)}, u32[]{:S(2)}) collective-permute-start(f32[24,768]{1,0:T(8,128)S(1)} %add.182), channel_id=1, source_target_pairs={{0,16},{2,18},{4,20},{6,22},{8,24},{10,26},{12,28},{14,30},{16,0},... | collective-permute-start | bytes 221192 | tf_op jit(solution)/shard_map/ppermute | solution.py:475
  200.0 5.9 %collective-permute-start.15 = (bf16[2,48,384]{2,1,0:T(8,128)(2,1)S(1)}, bf16[2,48,384]{2,1,0:T(8,128)(2,1)S(1)}, u32[]{:S(2)}, u32[]{:S(2)}) collective-permute-start(bf16[2,48,384]{2,1,0:T(8,128)(2,1)S(1)} %dynamic-slice_bitcast_fusion.10), channel_id=1, source_target_pairs={{0,8},{2,10},{4,12},{6,14},{8,0},{10,2},{12,4},{14,6},{16,24},{18,... | collective-permute-start | bytes 221192 | tf_op jit(solution)/shard_map/ppermute | solution.py:463
  206.0 4.9 %collective-permute-start.16 = (bf16[48,384]{1,0:T(8,128)(2,1)S(1)}, bf16[48,384]{1,0:T(8,128)(2,1)S(1)}, u32[]{:S(2)}, u32[]{:S(2)}) collective-permute-start(bf16[48,384]{1,0:T(8,128)(2,1)S(1)} %dynamic-slice_bitcast_fusion.11), channel_id=1, source_target_pairs={{0,16},{2,18},{4,20},{6,22},{8,24},{10,26},{12,28},{14,30},{16,0},... | collective-permute-start | bytes 110600 | tf_op jit(solution)/shard_map/ppermute | solution.py:463
  214.2 22.7 %collective-permute-start.3 = (bf16[2,2,48,2304]{3,2,0,1:T(8,128)(2,1)S(1)}, bf16[2,2,48,2304]{3,2,0,1:T(8,128)(2,1)S(1)}, u32[]{:S(2)}, u32[]{:S(2)}) collective-permute-start(bf16[2,2,48,2304]{3,2,0,1:T(8,128)(2,1)S(1)} %dynamic-slice_bitcast_fusion.1), channel_id=1, source_target_pairs={{0,4},{2,6},{4,0},{6,2},{8,12},{10,14},{12,8},{14,10},{16,20},{18,... | collective-permute-start | bytes 2654216 | tf_op jit(solution)/shard_map/ppermute | solution.py:463
  218.5 19.9 %copy-start = (bf16[2,2,2,1,48,3072]{5,4,3,2,1,0:T(8,128)(2,1)S(1)}, bf16[2,2,2,1,48,3072]{5,4,3,2,1,0:T(8,128)(2,1)}, u32[]{:S(2)}) copy-start(bf16[2,2,2,1,48,3072]{5,4,3,2,1,0:T(8,128)(2,1)} %get-tuple-element.86) | copy-start | bytes 7077892
  218.5 41.4 %collective-permute-start.18 = (bf16[2,2,48,3072]{3,2,0,1:T(8,128)(2,1)S(1)}, bf16[2,2,48,3072]{3,2,0,1:T(8,128)(2,1)S(1)}, u32[]{:S(2)}, u32[]{:S(2)}) collective-permute-start(bf16[2,2,48,3072]{3,2,0,1:T(8,128)(2,1)S(1)} %dynamic-slice_bitcast_fusion), channel_id=1, source_target_pairs={{0,4},{2,6},{4,0},{6,2},{8,12},{10,14},{12,8},{14,10},{16,20},{18,... | collective-permute-start | bytes 3538952 | tf_op jit(solution)/shard_map/ppermute | solution.py:463
  237.1 13.2 %collective-permute-start.4 = (bf16[2,2,48,1152]{3,2,0,1:T(8,128)(2,1)S(1)}, bf16[2,2,48,1152]{3,2,0,1:T(8,128)(2,1)S(1)}, u32[]{:S(2)}, u32[]{:S(2)}) collective-permute-start(bf16[2,2,48,1152]{3,2,0,1:T(8,128)(2,1)S(1)} %constant_dynamic-slice_fusion.9), channel_id=1, source_target_pairs={{0,1},{1,0},{2,3},{3,2},{4,5},{5,4},{6,7},{7,6},{8,9},{9,8},{10,11... | collective-permute-start | bytes 1327112 | tf_op jit(solution)/shard_map/ppermute | solution.py:463
  241.1 34.5 %collective-permute-start.23 = (bf16[2,2,2,48,1536]{4,3,0,1,2:T(8,128)(2,1)S(1)}, bf16[2,2,2,48,1536]{4,3,0,1,2:T(8,128)(2,1)S(1)}, u32[]{:S(2)}, u32[]{:S(2)}) collective-permute-start(bf16[2,2,2,48,1536]{4,3,0,1,2:T(8,128)(2,1)S(1)} %constant_dynamic-slice_fusion), channel_id=1, source_target_pairs={{0,1},{1,0},{2,3},{3,2},{4,5},{5,4},{6,7},{7,6},{8,9},{9,8},{10,11... | collective-permute-start | bytes 3538952 | tf_op jit(solution)/shard_map/ppermute | solution.py:463
  250.4 25.5 %collective-permute-start.5 = (bf16[2,48,1152]{2,1,0:T(8,128)(2,1)S(1)}, bf16[2,48,1152]{2,1,0:T(8,128)(2,1)S(1)}, u32[]{:S(2)}, u32[]{:S(2)}) collective-permute-start(bf16[2,48,1152]{2,1,0:T(8,128)(2,1)S(1)} %dynamic-slice_bitcast_fusion.5), channel_id=1, source_target_pairs={{0,8},{2,10},{4,12},{6,14},{8,0},{10,2},{12,4},{14,6},{16,24},{18,... | collective-permute-start | bytes 663560 | tf_op jit(solution)/shard_map/ppermute | solution.py:463
  260.4 23.4 %collective-permute-start.19 = (bf16[2,2,48,1536]{3,2,0,1:T(8,128)(2,1)S(1)}, bf16[2,2,48,1536]{3,2,0,1:T(8,128)(2,1)S(1)}, u32[]{:S(2)}, u32[]{:S(2)}) collective-permute-start(bf16[2,2,48,1536]{3,2,0,1:T(8,128)(2,1)S(1)} %constant_dynamic-slice_fusion.3), channel_id=1, source_target_pairs={{0,1},{1,0},{2,3},{3,2},{4,5},{5,4},{6,7},{7,6},{8,9},{9,8},{10,11... | collective-permute-start | bytes 1769480 | tf_op jit(solution)/shard_map/ppermute | solution.py:463
  276.0 7.0 %collective-permute-start.6 = (bf16[48,1152]{1,0:T(8,128)(2,1)S(1)}, bf16[48,1152]{1,0:T(8,128)(2,1)S(1)}, u32[]{:S(2)}, u32[]{:S(2)}) collective-permute-start(bf16[48,1152]{1,0:T(8,128)(2,1)S(1)} %dynamic-slice_bitcast_fusion.9), channel_id=1, source_target_pairs={{0,16},{2,18},{4,20},{6,22},{8,24},{10,26},{12,28},{14,30},{16,0},... | collective-permute-start | bytes 331784 | tf_op jit(solution)/shard_map/ppermute | solution.py:463
  276.2 9.9 %collective-permute-start.24 = (bf16[2,2,48,1536]{3,2,0,1:T(8,128)(2,1)S(1)}, bf16[2,2,48,1536]{3,2,0,1:T(8,128)(2,1)S(1)}, u32[]{:S(2)}, u32[]{:S(2)}) collective-permute-start(bf16[2,2,48,1536]{3,2,0,1:T(8,128)(2,1)S(1)} %dynamic-slice_bitcast_fusion.2), channel_id=1, source_target_pairs={{0,4},{2,6},{4,0},{6,2},{8,12},{10,14},{12,8},{14,10},{16,20},{18,... | collective-permute-start | bytes 1769480 | tf_op jit(solution)/shard_map/ppermute | solution.py:463
  283.9 8.9 %collective-permute-start.20 = (bf16[2,48,1536]{2,1,0:T(8,128)(2,1)S(1)}, bf16[2,48,1536]{2,1,0:T(8,128)(2,1)S(1)}, u32[]{:S(2)}, u32[]{:S(2)}) collective-permute-start(bf16[2,48,1536]{2,1,0:T(8,128)(2,1)S(1)} %dynamic-slice_bitcast_fusion.4), channel_id=1, source_target_pairs={{0,8},{2,10},{4,12},{6,14},{8,0},{10,2},{12,4},{14,6},{16,24},{18,... | collective-permute-start | bytes 884744 | tf_op jit(solution)/shard_map/ppermute | solution.py:463
  286.3 11.2 %collective-permute-start.25 = (bf16[2,48,1536]{2,1,0:T(8,128)(2,1)S(1)}, bf16[2,48,1536]{2,1,0:T(8,128)(2,1)S(1)}, u32[]{:S(2)}, u32[]{:S(2)}) collective-permute-start(bf16[2,48,1536]{2,1,0:T(8,128)(2,1)S(1)} %dynamic-slice_bitcast_fusion.3), channel_id=1, source_target_pairs={{0,8},{2,10},{4,12},{6,14},{8,0},{10,2},{12,4},{14,6},{16,24},{18,... | collective-permute-start | bytes 884744 | tf_op jit(solution)/shard_map/ppermute | solution.py:463
  292.9 7.8 %collective-permute-start.21 = (bf16[48,1536]{1,0:T(8,128)(2,1)S(1)}, bf16[48,1536]{1,0:T(8,128)(2,1)S(1)}, u32[]{:S(2)}, u32[]{:S(2)}) collective-permute-start(bf16[48,1536]{1,0:T(8,128)(2,1)S(1)} %dynamic-slice_bitcast_fusion.7), channel_id=1, source_target_pairs={{0,16},{2,18},{4,20},{6,22},{8,24},{10,26},{12,28},{14,30},{16,0},... | collective-permute-start | bytes 442376 | tf_op jit(solution)/shard_map/ppermute | solution.py:463
  297.6 6.6 %collective-permute-start.26 = (bf16[48,1536]{1,0:T(8,128)(2,1)S(1)}, bf16[48,1536]{1,0:T(8,128)(2,1)S(1)}, u32[]{:S(2)}, u32[]{:S(2)}) collective-permute-start(bf16[48,1536]{1,0:T(8,128)(2,1)S(1)} %dynamic-slice_bitcast_fusion.6), channel_id=1, source_target_pairs={{0,16},{2,18},{4,20},{6,22},{8,24},{10,26},{12,28},{14,30},{16,0},... | collective-permute-start | bytes 442376 | tf_op jit(solution)/shard_map/ppermute | solution.py:463
  (8 other events, 54.9 us)

commit v2 on v1

v2 whole, which is shorter than its diff:
```python
import functools

import jax
import jax.numpy as jnp
from jax import lax
from jax.experimental import pallas as pl
from jax.experimental.pallas import tpu as pltpu
from jax.sharding import PartitionSpec as P

bf16 = jnp.bfloat16
f32 = jnp.float32
norm_epsilon = 1e-06
root_half = 0.7071067811865476
inv_root_tau = 0.3989422804014327
vmem_limit = 60 * 1024 * 1024
nt_dims = (((1,), (1,)), ((), ()))


def mm(a, b):
    return jnp.dot(a, b, preferred_element_type=f32)


def mm_nt(a, b):
    return lax.dot_general(a, b, nt_dims, preferred_element_type=f32)


def iota(shape, dim):
    return lax.broadcasted_iota(jnp.int32, shape, dim)


def bounds(len_ref, nseg):
    starts, ends, run = [], [], jnp.int32(0)
    for s in range(nseg):
        starts.append(run)
        run = run + len_ref[0, s]
        ends.append(run)
    return starts, ends


def spanning(ends, half):
    count = jnp.int32(0)
    for end in ends:
        count = count + (end < half).astype(jnp.int32)
    return count


def pick(index, values):
    out = jnp.full(index.shape, values[-1], jnp.int32)
    for s in range(len(values) - 2, -1, -1):
        out = jnp.where(index == s, values[s], out)
    return out


def inside(pos, index, starts, ends):
    return jnp.logical_and(pos >= pick(index, starts), pos < pick(index, ends))


def as_bf(mask):
    return jnp.where(mask, 1.0, 0.0).astype(bf16)


def split_hi_lo(v):
    hi = v.astype(bf16)
    lo = (v - hi.astype(f32)).astype(bf16)
    return jnp.concatenate([hi, lo], axis=1)


def masked_rows(rows_t, lane_masks, tail):
    return jnp.concatenate([rows_t * m for m in lane_masks] + [tail], axis=0)


def head_map(map_ref, h):
    m = map_ref[h]
    z = jnp.zeros_like(m)
    return jnp.concatenate([m, z] if h % 2 == 0 else [z, m], axis=0)


def key_offset(k_pair, low_half, j):
    sq = jnp.square(k_pair.astype(f32))
    mine = low_half if j == 0 else jnp.logical_not(low_half)
    return jnp.sum(jnp.where(mine, sq, 0.0), axis=-1, keepdims=True)


def put_states(own_ref, tot_ref, span_ref, recv_ref, st_ref, totp_ref, here, nseg, heads, hdim):
    wide = nseg * hdim
    feat = st_ref.shape[1]
    recv_tot = recv_ref[heads * hdim :, :].astype(f32)
    seg_row = iota((8, feat), 0)
    for h in range(heads):
        st_ref[h * wide : (h + 1) * wide, :] = own_ref[h * wide : (h + 1) * wide, :]
        both = span_ref[h * hdim : (h + 1) * hdim, :] + recv_ref[h * hdim : (h + 1) * hdim, :].astype(f32)
        at = pl.multiple_of(h * wide + here * hdim, hdim)
        st_ref[pl.ds(at, hdim), :] = both.astype(bf16)
        tot = tot_ref[8 * h : 8 * h + 8, :]
        tot = jnp.where(seg_row == here, tot + recv_tot[h : h + 1, :], tot)
        parts = [tot]
        if h > 0:
            parts.insert(0, jnp.zeros((8 * h, feat), f32))
        if 8 * h + 8 < 128:
            parts.append(jnp.zeros((128 - 8 * h - 8, feat), f32))
        totp_ref[:, feat * h : feat * (h + 1)] = jnp.concatenate(parts, axis=0).astype(bf16)


def emit_states(acc_ref, own_ref, tot_ref, span_ref, send_ref, here, nseg, heads, hdim):
    wide = nseg * hdim
    feat = acc_ref.shape[2]
    for h in range(heads):
        own_ref[h * wide : (h + 1) * wide, :] = acc_ref[h, 0:wide, :].astype(bf16)
        tot_ref[8 * h : 8 * h + 8, :] = acc_ref[h, wide : wide + 8, :]
        at = pl.multiple_of(here * hdim, hdim)
        part = acc_ref[h, pl.ds(at, hdim), :]
        span_ref[h * hdim : (h + 1) * hdim, :] = part
        send_ref[h * hdim : (h + 1) * hdim, :] = part.astype(bf16)
    row = iota((16, feat), 0)
    seg_row = iota((8, feat), 0)
    tots = jnp.zeros((16, feat), f32)
    for h in range(heads):
        mine = jnp.sum(jnp.where(seg_row == here, acc_ref[h, wide : wide + 8, :], 0.0), axis=0, keepdims=True)
        tots = jnp.where(row == h, mine, tots)
    send_ref[heads * hdim :, :] = tots.astype(bf16)


def lane_segment_masks(first, rows, hdim, starts, ends):
    pos = first + iota((hdim, rows), 1)
    masks = [as_bf(jnp.logical_and(pos >= a, pos < b)) for a, b in zip(starts, ends)]
    pos = first + iota((16, rows), 1)
    seg = iota((16, rows), 0)
    tail = as_bf(jnp.logical_and(seg < len(starts), inside(pos, seg, starts, ends)))
    return masks, tail


def seg_masks(first, rows, hdim, nseg, starts, ends):
    pos = first + iota((rows, nseg * hdim), 0)
    wide = inside(pos, iota((rows, nseg * hdim), 1) // hdim, starts, ends)
    lane8 = iota((rows, 128), 1) % 8
    pos = first + iota((rows, 128), 0)
    eight = jnp.logical_and(lane8 < nseg, inside(pos, lane8, starts, ends))
    return wide, eight


def block_of(p, dp_count):
    top = dp_count.bit_length() - 1
    return (p >> (top - 1)) & 1 | ((p >> (top - 2)) & 1) << 1 | (p & (dp_count // 4 - 1)) << 2


def dp_index():
    return (lax.axis_index("z") * 2 + lax.axis_index("y")) * 2 + lax.axis_index("c")


def row_sources(dp_count):
    return [jnp.bitwise_xor(dp_index(), block_of(p, dp_count)) for p in range(dp_count)]


def put_transposed(lhs_ref, tmp_ref, values, at, sources):
    rows, width = values.shape
    cols = pl.ds(at, rows)
    if not sources:
        lhs_ref[:, cols] = values.T
        return
    block = width // len(sources)
    tmp_ref[...] = values.T
    for p, source in enumerate(sources):
        lhs_ref[p * block : (p + 1) * block, cols] = tmp_ref[pl.ds(pl.multiple_of(source * block, 16), block), :]


def fold_pair(folded, low_half, hdim):
    straight = jnp.where(low_half, folded[0], folded[1])
    crossed = jnp.where(low_half, folded[1], folded[0])
    return straight + pltpu.roll(crossed, hdim, 1)


def forward_keys(
    len_ref, tok_ref, wk_ref, wv_ref, b_ref, map_ref, kv_ref, own_ref, tot_ref, span_ref, send_ref, acc_ref,
    *, half, nseg, heads, hdim
):
    step = pl.program_id(0)
    rows, width = tok_ref.shape
    starts, ends = bounds(len_ref, nseg)
    here = spanning(ends, half)
    first = lax.axis_index("x") * half + step * rows
    factor = hdim ** (-0.25)

    @pl.when(step == 0)
    def _():
        acc_ref[...] = jnp.zeros_like(acc_ref)

    masks, tail = lane_segment_masks(first, rows, hdim, starts, ends)
    tok = tok_ref[...]
    keys = (mm(tok, wk_ref[...]) + b_ref[1:2, :]).astype(bf16)
    vals = (mm(tok, wv_ref[...]) + b_ref[2:3, :]).astype(bf16)
    kv_ref[:, :width] = keys
    kv_ref[:, width:] = vals
    low_half = iota((rows, 128), 1) < hdim
    for p in range(heads // 2):
        k_pair = keys[:, 128 * p : 128 * (p + 1)]
        v_t = vals[:, 128 * p : 128 * (p + 1)].T
        for j in range(2):
            h = 2 * p + j
            logits = factor * mm(k_pair, head_map(map_ref, h)) - (0.5 * factor * factor) * key_offset(k_pair, low_half, j)
            feats = jnp.exp(logits).astype(bf16)
            lhs = masked_rows(v_t[j * hdim : (j + 1) * hdim, :], masks, tail)
            acc_ref[h] += mm(lhs, feats)

    @pl.when(step == pl.num_programs(0) - 1)
    def _():
        emit_states(acc_ref, own_ref, tot_ref, span_ref, send_ref, here, nseg, heads, hdim)


def forward_queries(tok_ref, wq_ref, b_ref, map_ref, q_ref, qf_ref, *, heads, hdim):
    feat = map_ref.shape[2]
    factor = hdim ** (-0.25)
    queries = (mm(tok_ref[...], wq_ref[...]) + b_ref[0:1, :]).astype(bf16)
    q_ref[...] = queries
    for h in range(heads):
        proj = mm(queries[:, 128 * (h // 2) : 128 * (h // 2 + 1)], head_map(map_ref, h))
        top = jnp.max(proj, axis=-1, keepdims=True)
        qf_ref[:, feat * h : feat * (h + 1)] = jnp.exp(factor * (proj - top)).astype(bf16)


def norm_backward(incoming, scaled, inverse, gain):
    weighted = incoming * gain
    return inverse * (
        weighted
        - jnp.mean(weighted, axis=-1, keepdims=True)
        - scaled * jnp.mean(weighted * scaled, axis=-1, keepdims=True)
    )


def norm_parts(values):
    centred = values - jnp.mean(values, axis=-1, keepdims=True)
    spread = jnp.mean(centred * centred, axis=-1, keepdims=True)
    inverse = lax.rsqrt(spread + norm_epsilon)
    return centred * inverse, inverse


def gelu_parts(u):
    cdf = 0.5 + 0.5 * lax.erf(u * root_half)
    return u * cdf, cdf + u * (inv_root_tau * jnp.exp(-0.5 * (u * u)))


def flat_row(ref):
    return ref[...].reshape(1, -1)


def add_row(vec_ref, row, values):
    vec_ref[row : row + 1, :] += jnp.sum(values, axis=0, keepdims=True)


def put_grad(keep_ref, send_ref, grad):
    quarter = grad.shape[0] // 4
    for b in range(grad.shape[1] // 128):
        cols = slice(128 * b, 128 * (b + 1))
        for y in range(2):
            keep_ref[y, 0, b] = grad[y * quarter : (y + 1) * quarter, cols].astype(bf16)
            send_ref[y, 0, b] = grad[(2 + y) * quarter : (3 + y) * quarter, cols].astype(bf16)


def half_cols(xr, half_width):
    x = lax.axis_index("x")
    return pl.multiple_of(jnp.bitwise_xor(x, xr) * half_width, 128)


def chain(
    len_ref, tok_ref, qf_ref, cot_ref, own_ref, tot_ref, span_ref, recv_ref, wo_ref, bo_ref, g1_ref, s1_ref,
    wup_hbm, bup_ref, wdn_hbm, bdn_ref, g2_ref, s2_ref,
    out_ref, agrad_ref, num_ref, dgm_ref, vec_ref, sown_ref, stot_ref, sspan_ref, ssend_ref,
    dkeep_ref, dsend_ref, ukeep_ref, usend_ref, okeep_ref, osend_ref,
    st_ref, totp_ref, acc_ref, act_ref, up_ref, mix_ref, slope_ref, dlhs_ref, ulhs_ref, olhs_ref, tmp_ref, wup_ref, wdn_ref, sem,
    *, half, nseg, heads, hdim, chunk, steps, dp_count, sort
):
    step = pl.program_id(0)
    rows, width = tok_ref.shape
    wide = nseg * hdim
    feat = st_ref.shape[1]
    hidden_units = wup_ref.shape[1]
    starts, ends = bounds(len_ref, nseg)
    here = spanning(ends, half)
    first = lax.axis_index("x") * half + step * rows
    fetch = [pltpu.make_async_copy(wup_hbm, wup_ref, sem.at[0]), pltpu.make_async_copy(wdn_hbm, wdn_ref, sem.at[1])]

    @pl.when(step == 0)
    def _():
        fetch[0].start()
        fetch[1].start()
        vec_ref[...] = jnp.zeros_like(vec_ref)
        acc_ref[...] = jnp.zeros_like(acc_ref)
        put_states(own_ref, tot_ref, span_ref, recv_ref, st_ref, totp_ref, here, nseg, heads, hdim)

    @pl.when(step < steps)
    def _():
        at = pl.multiple_of(step * rows, 128)
        mine = pl.ds(at, rows)
        seg_wide, seg8 = seg_masks(first, rows, hdim, nseg, starts, ends)
        low_half = iota((rows, 128), 1) < hdim
        nums = []
        for p in range(heads // 2):
            folded = []
            for j in range(2):
                h = 2 * p + j
                r = mm_nt(qf_ref[:, feat * h : feat * (h + 1)], st_ref[wide * h : wide * (h + 1), :])
                r = jnp.where(seg_wide, r, 0.0)
                folded.append(r[:, :128] + r[:, 128:])
            nums.append(fold_pair(folded, low_half, hdim))
        numer = jnp.concatenate(nums, axis=1)
        den_parts = split_hi_lo(jnp.where(seg8, mm_nt(qf_ref[...], totp_ref[...]), 0.0))
        expand = as_bf((iota((256, width), 0) % 128) // 8 == iota((256, width), 1) // hdim)
        same8 = as_bf((iota((256, 128), 0) % 128) // 8 == iota((256, 128), 1) // 8)
        dead = jnp.where(first + iota((rows, 128), 0) < ends[-1], 0.0, 1.0)
        spare = jnp.where(iota((rows, 128), 1) < 8 * heads, dead, 1.0)
        inv_c = 1.0 / (mm(den_parts, same8) + spare)
        inv_w = 1.0 / (mm(den_parts, expand) + jnp.concatenate([dead] * (width // 128), axis=1))
        ratio = numer * inv_w
        mixed = ratio.astype(bf16)
        mix_ref[mine, :] = mixed

        hidden = tok_ref[...].astype(f32) + mm_nt(mixed, wo_ref[...]) + flat_row(bo_ref)
        scaled1, inverse1 = norm_parts(hidden)
        normed = scaled1 * flat_row(g1_ref) + flat_row(s1_ref)
        normed_bf = normed.astype(bf16)
        put_transposed(ulhs_ref, tmp_ref, normed_bf, at, row_sources(dp_count) if sort else [])

        @pl.when(step == 0)
        def _():
            fetch[0].wait()
            fetch[1].wait()

        count = hidden_units // chunk
        cols = [slice(c * chunk, (c + 1) * chunk) for c in range(count)]
        bup = flat_row(bup_ref)
        up = mm(normed_bf, wup_ref[:, cols[0]]) + bup[:, cols[0]]
        branch = normed + flat_row(bdn_ref)
        last = None
        for c in range(count):
            later = mm(normed_bf, wup_ref[:, cols[c + 1]]) + bup[:, cols[c + 1]] if c + 1 < count else None
            act, slope = gelu_parts(up)
            act = act.astype(bf16)
            act_ref[mine, cols[c]] = act
            slope_ref[:, cols[c]] = slope.astype(slope_ref.dtype)
            if last is not None:
                branch += mm_nt(last, wdn_ref[:, cols[c - 1]])
            last, up = act, later
        final = branch + mm_nt(last, wdn_ref[:, cols[count - 1]])
        scaled2, inverse2 = norm_parts(final)
        gain2 = flat_row(g2_ref)
        out_ref[...] = (scaled2 * gain2 + flat_row(s2_ref)).astype(bf16)
        incoming = cot_ref[...].astype(f32)
        grad_final = norm_backward(incoming, scaled2, inverse2, gain2)
        bgrad = grad_final.astype(bf16)
        add_row(vec_ref, 0, grad_final)
        add_row(vec_ref, 1, incoming * scaled2)
        add_row(vec_ref, 2, incoming)
        put_transposed(dlhs_ref, tmp_ref, bgrad, at, row_sources(dp_count) if sort else [])

        grad_normed = grad_final
        wide_grad = mm(bgrad, wdn_ref[:, cols[0]])
        last = None
        for c in range(count):
            later = mm(bgrad, wdn_ref[:, cols[c + 1]]) if c + 1 < count else None
            ugrad = (wide_grad * slope_ref[:, cols[c]].astype(f32)).astype(bf16)
            up_ref[mine, cols[c]] = ugrad
            sums = jnp.sum(ugrad.astype(f32), axis=0, keepdims=True)
            for k in range(0, chunk, 128):
                row, col = divmod(c * chunk + k, width)
                vec_ref[6 + row : 7 + row, col : col + 128] += sums[:, k : k + 128]
            if last is not None:
                grad_normed += mm_nt(last, wup_ref[:, cols[c - 1]])
            last, wide_grad = ugrad, later
        grad_normed += mm_nt(last, wup_ref[:, cols[count - 1]])

        grad_hidden = norm_backward(grad_normed, scaled1, inverse1, flat_row(g1_ref))
        add_row(vec_ref, 3, grad_hidden)
        add_row(vec_ref, 4, grad_normed * scaled1)
        add_row(vec_ref, 5, grad_normed)
        agrad = grad_hidden.astype(bf16)
        agrad_ref[...] = agrad
        put_transposed(olhs_ref, tmp_ref, agrad, at, row_sources(dp_count) if sort else [])

        grad_mixed = mm(agrad, wo_ref[...])
        num_grad = (grad_mixed * inv_w).astype(bf16)
        num_ref[...] = num_grad
        inner = split_hi_lo(grad_mixed * ratio)
        gather = as_bf((iota((2 * width, 128), 0) % width) // hdim == iota((2 * width, 128), 1) // 8)
        den_m = jnp.where(seg8, -(mm(inner, gather) * inv_c), 0.0).astype(bf16)
        dgm_ref[...] = den_m
        den_t = den_m.T
        masks, _ = lane_segment_masks(first, rows, hdim, starts, ends)
        pad = jnp.zeros((8, rows), bf16)
        for p in range(heads // 2):
            num_t = num_grad[:, 128 * p : 128 * (p + 1)].T
            tails = den_t[16 * p : 16 * p + 16, :]
            for j in range(2):
                h = 2 * p + j
                tail = jnp.concatenate([tails[8 * j : 8 * j + 8, :], pad], axis=0)
                lhs = masked_rows(num_t[j * hdim : (j + 1) * hdim, :], masks, tail)
                acc_ref[h] += mm(lhs, qf_ref[:, feat * h : feat * (h + 1)])

    @pl.when(step == steps - 1)
    def _():
        emit_states(acc_ref, sown_ref, stot_ref, sspan_ref, ssend_ref, here, nseg, heads, hdim)

    own = hidden_units // 2
    count = hidden_units // chunk
    tile = step - steps

    @pl.when(jnp.logical_and(tile >= 0, tile < count))
    def _():
        xr = tile // (count // 2)
        at = half_cols(xr, own) + (tile - xr * (count // 2)) * chunk
        rhs = act_ref[:, pl.ds(pl.multiple_of(at, 128), chunk)]
        put_grad(dkeep_ref, dsend_ref, mm(dlhs_ref[...], rhs))

    @pl.when(jnp.logical_and(tile >= count, tile < 2 * count))
    def _():
        xr = (tile - count) // (count // 2)
        at = half_cols(xr, own) + (tile - count - xr * (count // 2)) * chunk
        put_grad(ukeep_ref, usend_ref, mm(ulhs_ref[...], up_ref[:, pl.ds(pl.multiple_of(at, 128), chunk)]))

    @pl.when(tile >= 2 * count)
    def _():
        rhs = mix_ref[:, pl.ds(half_cols(tile - 2 * count, width // 2), width // 2)]
        put_grad(okeep_ref, osend_ref, mm(olhs_ref[...], rhs))


def replicate(pair, low_half, hdim):
    wide = pair.astype(f32)
    other = pltpu.roll(wide, hdim, 1)
    return (jnp.where(low_half, wide, other).astype(bf16), jnp.where(low_half, other, wide).astype(bf16))


def map_back(map_ref, mapg_ref, heads, hdim):
    one, zero = jnp.ones((hdim, map_ref.shape[2]), bf16), jnp.zeros((hdim, map_ref.shape[2]), bf16)
    for p in range(heads // 2):
        left = jnp.concatenate([map_ref[2 * p], zero, one, zero], axis=0)
        right = jnp.concatenate([zero, map_ref[2 * p + 1], zero, one], axis=0)
        mapg_ref[p] = jnp.concatenate([left, right], axis=1)


def rows_grad(logs, mapg, rows_bf, factor):
    r = mm_nt(jnp.concatenate(logs, axis=1), mapg)
    return (factor * r[:, :128] - (factor * factor) * rows_bf.astype(f32) * r[:, 128:]).astype(bf16)


def weight_parts(step, steps, lhs_ref, pg_ref, keep_ref, send_ref, width):
    own = width // 2
    for xr in range(2):

        @pl.when(step == steps + xr)
        def _():
            rhs = [pg_ref[:, pl.ds(c * width + half_cols(xr, own), own)] for c in range(pg_ref.shape[1] // width)]
            put_grad(keep_ref, send_ref, mm(lhs_ref[...], jnp.concatenate(rhs, axis=1)))


def key_back(
    len_ref, kv_ref, tok_ref, map_ref, own_ref, tot_ref, span_ref, recv_ref,
    *refs,
    half, nseg, heads, hdim, steps, dp_count, sort
):
    pgo_ref, vec_ref, keep_ref, send_ref, sg_ref, sgt_ref, mapg_ref, pg_ref, lhs_ref, tmp_ref = refs[-10:]
    step = pl.program_id(0)
    rows, width = tok_ref.shape
    feat = map_ref.shape[2]
    wide = nseg * hdim
    starts, ends = bounds(len_ref, nseg)
    here = spanning(ends, half)
    first = lax.axis_index("x") * half + step * rows
    factor = hdim ** (-0.25)

    @pl.when(step == 0)
    def _():
        vec_ref[...] = jnp.zeros_like(vec_ref)
        put_states(own_ref, tot_ref, span_ref, recv_ref, sg_ref, sgt_ref, here, nseg, heads, hdim)
        map_back(map_ref, mapg_ref, heads, hdim)

    @pl.when(step < steps)
    def _():
        at = pl.multiple_of(step * rows, 128)
        mine = pl.ds(at, rows)
        seg_wide, seg8 = seg_masks(first, rows, hdim, nseg, starts, ends)
        seg_wide_bf, seg8_bf = as_bf(seg_wide), as_bf(seg8)
        low_half = iota((rows, 128), 1) < hdim
        for p in range(heads // 2):
            k_cols, v_cols = slice(128 * p, 128 * (p + 1)), slice(width + 128 * p, width + 128 * (p + 1))
            k_pair = kv_ref[:, k_cols]
            v_reps = replicate(kv_ref[:, v_cols], low_half, hdim)
            logs, folded = [], []
            for j in range(2):
                h = 2 * p + j
                logits = factor * mm(k_pair, head_map(map_ref, h)) - (0.5 * factor * factor) * key_offset(k_pair, low_half, j)
                feats = jnp.exp(logits)
                lhs = jnp.concatenate([v_reps[j]] * 2, axis=1) * seg_wide_bf
                state_grad = sg_ref[wide * h : wide * (h + 1), :]
                slope = mm(lhs, state_grad) + mm(seg8_bf, sgt_ref[:, feat * h : feat * (h + 1)])
                logs.append((slope * feats).astype(bf16))
                r = jnp.where(seg_wide, mm_nt(feats.astype(bf16), state_grad), 0.0)
                folded.append(r[:, :128] + r[:, 128:])
            pg_ref[mine, k_cols] = rows_grad(logs, mapg_ref[p], k_pair, factor)
            pg_ref[mine, v_cols] = fold_pair(folded, low_half, hdim).astype(bf16)
        grads = pg_ref[mine, :]
        pgo_ref[...] = grads
        add_row(vec_ref, 1, grads[:, :width].astype(f32))
        add_row(vec_ref, 2, grads[:, width:].astype(f32))
        put_transposed(lhs_ref, tmp_ref, tok_ref[...], at, row_sources(dp_count) if sort else [])

    weight_parts(step, steps, lhs_ref, pg_ref, keep_ref, send_ref, width)


def query_back(
    len_ref, q_ref, num_ref, dgm_ref, tok_ref, map_ref, own_ref, tot_ref, span_ref, recv_ref,
    *refs,
    half, nseg, heads, hdim, steps, dp_count, sort
):
    pgo_ref, vec_ref, keep_ref, send_ref, st_ref, totp_ref, mapg_ref, pg_ref, lhs_ref, tmp_ref = refs[-10:]
    step = pl.program_id(0)
    rows, width = tok_ref.shape
    feat = map_ref.shape[2]
    wide = nseg * hdim
    starts, ends = bounds(len_ref, nseg)
    first = lax.axis_index("x") * half + step * rows
    factor = hdim ** (-0.25)

    @pl.when(step == 0)
    def _():
        vec_ref[...] = jnp.zeros_like(vec_ref)
        put_states(own_ref, tot_ref, span_ref, recv_ref, st_ref, totp_ref, spanning(ends, half), nseg, heads, hdim)
        map_back(map_ref, mapg_ref, heads, hdim)

    @pl.when(step < steps)
    def _():
        at = pl.multiple_of(step * rows, 128)
        mine = pl.ds(at, rows)
        seg_wide, _ = seg_masks(first, rows, hdim, nseg, starts, ends)
        seg_wide_bf = as_bf(seg_wide)
        low_half = iota((rows, 128), 1) < hdim
        den_m = dgm_ref[...]
        for p in range(heads // 2):
            cols = slice(128 * p, 128 * (p + 1))
            q_pair = q_ref[:, cols]
            reps = replicate(num_ref[:, cols], low_half, hdim)
            logs = []
            for j in range(2):
                h = 2 * p + j
                proj = mm(q_pair, head_map(map_ref, h))
                shifted = proj - jnp.max(proj, axis=-1, keepdims=True)
                lhs = jnp.concatenate([reps[j]] * 2, axis=1) * seg_wide_bf
                slope = mm(lhs, st_ref[wide * h : wide * (h + 1), :]) + mm(den_m, totp_ref[:, feat * h : feat * (h + 1)])
                slope = slope * jnp.exp(factor * shifted)
                peak = jnp.where(shifted == 0.0, 1.0, 0.0)
                share = jnp.sum(slope, axis=-1, keepdims=True) / jnp.sum(peak, axis=-1, keepdims=True)
                logs.append((slope - peak * share).astype(bf16))
            pg_ref[mine, cols] = rows_grad(logs, mapg_ref[p], q_pair, factor)
        grads = pg_ref[mine, :]
        pgo_ref[...] = grads
        add_row(vec_ref, 0, grads.astype(f32))
        put_transposed(lhs_ref, tmp_ref, tok_ref[...], at, row_sources(dp_count) if sort else [])

    weight_parts(step, steps, lhs_ref, pg_ref, keep_ref, send_ref, width)


def token_grads(agrad_ref, pgq_ref, pgkv_ref, wq_ref, wk_ref, wv_ref, *refs):
    out_ref = refs[-1]
    width = agrad_ref.shape[1]
    total = agrad_ref[...].astype(f32) + mm_nt(pgq_ref[...], wq_ref[...])
    total += mm_nt(pgkv_ref[:, :width], wk_ref[...])
    out_ref[...] = (total + mm_nt(pgkv_ref[:, width:], wv_ref[...])).astype(bf16)


def params(micros):
    return dict(
        compiler_params=pltpu.CompilerParams(vmem_limit_bytes=vmem_limit),
        cost_estimate=pl.CostEstimate(flops=int(micros * 1.1e9), bytes_accessed=int(micros * 1e6), transcendentals=0),
    )


def whole(shape):
    return pl.BlockSpec(shape, lambda i: (0,) * len(shape), pipeline_mode=pl.Buffered(1))


def resident(shape):
    return pl.BlockSpec(shape, lambda i: (0,) * len(shape))


def sds(shape, dtype):
    return jax.ShapeDtypeStruct(shape, dtype)


every_axis = ("z", "y", "c", "x")


def exchange(values, mask, dp_count):
    return lax.ppermute(values, every_axis, [(i, i ^ mask) for i in range(2 * dp_count)])


def sort_rows(keep, send, dp_count):
    _, _, blocks, quarter, _ = keep.shape
    natural = jnp.stack([keep, send]).transpose(0, 1, 4, 2, 3, 5).reshape(dp_count, -1, 2, blocks, 128)
    rows = jnp.take(natural, jnp.stack(row_sources(dp_count)), axis=0)
    rows = rows.reshape(2, 2, quarter, 2, blocks, 128).transpose(0, 1, 3, 4, 2, 5)
    return rows[0], rows[1]


def route(name, arrays, outs, moves, vec=None, after=()):
    rows = arrays[0].shape[-2]
    grid = 2 if rows % 32 == 0 else 1
    own, got, send = vec if vec is not None else (None, None, None)
    extra = [own] if vec is not None else []
    if vec is not None:
        count, blocks = own.shape[0], own.shape[1] // 128
        assert grid == 2 and 2 * count * blocks == rows

    def spec(shape):
        lead = len(shape) - 2
        return pl.BlockSpec(tuple(shape[:lead]) + (rows // grid, 128), lambda i: (0,) * lead + (i, 0))

    def kernel(*refs):
        ins, results = refs[: len(arrays)], refs[len(arrays) + len(extra) + len(after) :]
        for out, to, parts in moves:
            total = ins[parts[0][0]][parts[0][1]].astype(f32)
            for n, at in parts[1:]:
                total = total + ins[n][at].astype(f32)
            results[out][to] = total.astype(bf16)
        if vec is not None:
            step = pl.program_id(0)
            sums_ref = results[-1]

            @pl.when(step == 0)
            def _():
                sums_ref[...] = refs[len(arrays)][...]

            if got is not None:
                other = ins[got[0]][got[1]].astype(f32)
                sums_ref[...] += jnp.concatenate([other[b * count : (b + 1) * count] for b in range(blocks)], axis=1)
            if send is not None:
                sums = sums_ref[...]
                hi = sums.astype(bf16)
                part = jnp.where(step == 0, hi.astype(f32), sums - hi.astype(f32)).astype(bf16)
                rows_of = [part[:, 128 * b : 128 * (b + 1)] for b in range(blocks)]
                results[send[0]][send[1]] = jnp.concatenate(rows_of, axis=0)

    shapes = [sds(v, bf16) for v in outs]
    specs = [spec(v) for v in outs]
    if vec is not None:
        shapes.append(sds(own.shape, f32))
        specs.append(resident(own.shape))
    return pl.pallas_call(
        kernel,
        name=name,
        grid=(grid,),
        in_specs=[spec(a.shape) for a in arrays] + [resident(v.shape) for v in extra] + [pl.BlockSpec(memory_space=pl.ANY)] * len(after),
        out_specs=specs,
        out_shape=shapes,
        **params(3),
    )(*arrays, *extra, *after)


def first_moves(groups, left):
    moves, n = [], 0
    for array, blocks in groups:
        for b in range(blocks):
            for y in range(2):
                for x in range(2):
                    parts = [(array, (y, x, b)), (array + 1, (y, x, b))]
                    moves.append((x, (y, n), parts) if n < left else (2 + y, (x, n - left), parts))
            n += 1
    return moves


def second_moves(array, left, right, out):
    moves = []
    for b in range(left):
        moves += [(out if y == 0 else out + 1, (b,), [(array, (y, b)), (array + 1, (y, b))]) for y in range(2)]
    for b in range(right):
        moves += [(out if x == 0 else out + 2, (left + b if x == 0 else b,), [(array + 2, (x, b)), (array + 3, (x, b))]) for x in range(2)]
    return moves


def third_sum(keep, left_got, right_got):
    return added(bf16, keep, jnp.concatenate([left_got, right_got], axis=0))


def added(dtype, *parts):
    return functools.reduce(jnp.add, [p.astype(f32) for p in parts]).astype(dtype)


def odd_even(part, count):
    pairs = part.reshape(part.shape[0], count // 2, 2, -1, 128)
    return [pairs[:, :, k].reshape(part.shape[0], -1, 128) for k in range(2)]


def columns(part):
    return part.transpose(1, 0, 2).reshape(part.shape[1], -1)


def body(
    tokens, lengths, feature_map, qkv_weight, qkv_bias, out_weight, out_bias, ln1_gain, ln1_shift,
    up_weight, up_bias, down_weight, down_bias, ln2_gain, ln2_shift, cotangent,
):
    half, width = tokens.shape
    heads, hdim, feat = feature_map.shape
    nseg = lengths.shape[1]
    hidden_units = up_weight.shape[1]
    wide = nseg * hdim
    dp_count = lax.axis_size(("z", "y", "c"))
    assert lax.axis_size("x") == 2 and dp_count & (dp_count - 1) == 0 and dp_count >= 8
    assert 2 * hdim == 128 and wide == 256 and 8 * heads <= 128
    sort = (width // dp_count) % 16 == 0
    layout = dict(dp_count=dp_count, sort=sort)
    wq, wk, wv = (qkv_weight[:, c, :] for c in range(3))
    rows = min(256, half)
    steps = half // rows
    big = min(512, half)
    span_rows = heads * hdim + 16
    state_shapes = [
        sds((heads * wide, feat), bf16), sds((heads * 8, feat), f32),
        sds((span_rows - 16, feat), f32), sds((span_rows, feat), bf16),
    ]
    state_specs = [resident(s.shape) for s in state_shapes]
    lens = pl.BlockSpec(memory_space=pltpu.SMEM)
    acc = pltpu.VMEM((heads, wide + 16, feat), f32)
    features = whole(feature_map.shape)
    square = whole((width, width))

    def tile(cols):
        return pl.BlockSpec((rows, cols), lambda i: (jnp.minimum(i, steps - 1), 0))

    def vector(size):
        return pl.BlockSpec((size,), lambda i: (0,))

    static = dict(half=half, nseg=nseg, heads=heads, hdim=hdim)
    dense = 2 * half * width

    def parts(cols, before, count):
        shape = sds((2, 2, cols // 128, width // 4, 128), bf16)
        at = lambda i: (0, jnp.maximum(i - before, 0) // count, 0, 0, 0)
        return [pl.BlockSpec((2, 1, cols // 128, width // 4, 128), at)] * 2, [shape] * 2

    def run(kernel, name, grid, in_specs, args, after, **more):
        fence = [pl.BlockSpec(memory_space=pl.ANY)] * len(after)
        return pl.pallas_call(kernel, name=name, grid=grid, in_specs=list(in_specs) + fence, **more)(*args, *after)

    def over_core(keep, send):
        if not sort:
            keep, send = sort_rows(keep, send, dp_count)
        return keep, exchange(send, 2, dp_count)

    kv, own, tot, span, send = pl.pallas_call(
        functools.partial(forward_keys, **static),
        name="key_states",
        grid=(steps,),
        in_specs=[lens, tile(width), square, square, whole((3, width)), features],
        out_specs=[tile(2 * width)] + state_specs,
        out_shape=[sds((half, 2 * width), bf16)] + state_shapes,
        scratch_shapes=[acc],
        **params(12),
    )(lengths, tokens, wk, wv, qkv_bias, feature_map)
    recv = exchange(send, 1, dp_count)
    q_rows, q_feats = pl.pallas_call(
        functools.partial(forward_queries, heads=heads, hdim=hdim),
        name="query_features",
        grid=(steps,),
        in_specs=[tile(width), square, whole((3, width)), features],
        out_specs=[tile(width), tile(heads * feat)],
        out_shape=[sds((half, width), bf16), sds((half, heads * feat), bf16)],
        **params(7),
    )(tokens, wq, qkv_bias, feature_map)

    chunk = 512
    count = hidden_units // chunk
    half_w, half_u = width // 2, hidden_units // 2
    vec_rows = 6 + hidden_units // width
    vec_rows += -vec_rows % 8

    def tiles(cols, size, before):
        per = cols // size

        def at(i):
            t = jnp.clip(i - before, 0, 2 * per - 1)
            return (0, t // per, t % per, 0, 0)

        shape = sds((2, 2, cols // 128, width // 4, 128), bf16)
        return [pl.BlockSpec((2, 1, size // 128, width // 4, 128), at)] * 2, [shape] * 2

    d_specs, d_shapes = tiles(half_u, chunk, steps)
    u_specs, u_shapes = tiles(half_u, chunk, steps + count)
    o_specs, o_shapes = tiles(half_w, half_w, steps + 2 * count)
    hbm = pl.BlockSpec(memory_space=pl.ANY)
    (output, agrad, num_grad, den_m, vec_1, s_own, s_tot, s_span, s_send, d_keep, d_send, u_keep, u_send, o_keep, o_send) = run(
        functools.partial(chain, chunk=chunk, steps=steps, **layout, **static),
        "chain",
        (steps + 2 * count + 2,),
        [lens, tile(width), tile(heads * feat), tile(width)]
        + [whole(v.shape) for v in (own, tot, span, recv)]
        + [square, vector(width), vector(width), vector(width)]
        + [hbm, vector(hidden_units), hbm]
        + [vector(width)] * 3,
        (
            lengths, tokens, q_feats, cotangent, own, tot, span, recv, out_weight, out_bias, ln1_gain, ln1_shift,
            up_weight, up_bias, down_weight, down_bias, ln2_gain, ln2_shift,
        ),
        (),
        out_specs=[tile(c) for c in (width, width, width, 128)] + [resident((vec_rows, width))] + state_specs + d_specs + u_specs + o_specs,
        out_shape=[sds((half, c), bf16) for c in (width, width, width, 128)]
        + [sds((vec_rows, width), f32)]
        + state_shapes + d_shapes + u_shapes + o_shapes,
        scratch_shapes=[
            pltpu.VMEM((heads * wide, feat), bf16),
            pltpu.VMEM((128, heads * feat), bf16),
            acc,
            pltpu.VMEM((half, hidden_units), bf16),
            pltpu.VMEM((half, hidden_units), bf16),
            pltpu.VMEM((half, width), bf16),
            pltpu.VMEM((rows, hidden_units), bf16),
            pltpu.VMEM((width, half), bf16),
            pltpu.VMEM((width, half), bf16),
            pltpu.VMEM((width, half), bf16),
            pltpu.VMEM((width, rows), bf16),
            pltpu.VMEM(up_weight.shape, bf16),
            pltpu.VMEM(down_weight.shape, bf16),
            pltpu.SemaphoreType.DMA((2,)),
        ],
        **params(66),
    )
    s_recv = exchange(s_send, 1, dp_count)
    d_keep, d_got = over_core(d_keep, d_send)
    u_keep, u_got = over_core(u_keep, u_send)
    o_keep, o_got = over_core(o_keep, o_send)
    block = (width // 4, 128)
    d_n, u_n, o_n = half_u // 128, half_u // 128, half_w // 128
    d_l, uo_l, qkv_n, qkv_l = d_n // 2, (u_n + o_n) // 2, 3 * o_n, 3 * o_n // 2
    d_r, uo_r, qkv_r = d_n - d_l, u_n + o_n - uo_l, qkv_n - qkv_l
    pair = lambda n: (2, n) + block
    d_lk, d_ls, d_rk, d_rs = route("down_1", [d_keep, d_got], [pair(d_l)] * 2 + [pair(d_r)] * 2, first_moves([(0, d_n)], d_l))
    x_got, y_got = exchange(d_ls, 1, dp_count), exchange(d_rs, 4, dp_count)
    rows = min(512, half)
    steps = half // rows

    def back_scratch(n):
        return [
            pltpu.VMEM((heads // 2, 4 * hdim, 2 * feat), bf16),
            pltpu.VMEM((half, n * width), bf16),
            pltpu.VMEM((width, half), bf16),
            pltpu.VMEM((width, rows), bf16),
        ]

    q_specs, q_shapes = parts(half_w, steps, 1)
    state_scratch = [pltpu.VMEM((heads * wide, feat), bf16), pltpu.VMEM((128, heads * feat), bf16)]
    pg_q, vec_2, q_keep, q_send = run(
        functools.partial(query_back, steps=steps, **layout, **static),
        "query_back",
        (steps + 2,),
        [lens, tile(width), tile(width), tile(128), tile(width), features] + [whole(v.shape) for v in (own, tot, span, recv)],
        (lengths, q_rows, num_grad, den_m, tokens, feature_map, own, tot, span, recv),
        (d_lk,),
        out_specs=[tile(width), resident((8, width))] + q_specs,
        out_shape=[sds((half, width), bf16), sds((8, width), f32)] + q_shapes,
        scratch_shapes=state_scratch + back_scratch(1),
        **params(18),
    )
    q_keep, q_got = over_core(q_keep, q_send)
    arrays = [d_lk, x_got, d_rk, y_got, u_keep, u_got, o_keep, o_got]
    moves = second_moves(0, d_l, d_r, 0)
    shift = {1: 4, 2: 3}
    moves = [(shift.get(out, out), at, terms) for out, at, terms in moves]
    for out, at, terms in first_moves([(4, u_n), (6, o_n)], uo_l):
        place = at[0] * (uo_l if out < 2 else uo_r) + at[1]
        if out in (0, 2):
            moves.append((1 if out == 0 else 2, at, terms))
        else:
            moves.append((3, (d_r + place,), terms) if out == 1 else (4, (d_l + place,), terms))
    flat = lambda n: (n,) + block
    d_part, uo_lk, uo_rk, x_send, y_send = route(
        "down_2_up_1", arrays, [flat(d_n), pair(uo_l), pair(uo_r), flat(d_r + 2 * uo_l), flat(d_l + 2 * uo_r)], moves
    )
    x_got, y_got = exchange(x_send, 1, dp_count), exchange(y_send, 4, dp_count)

    kv_specs, kv_shapes = parts(2 * half_w, steps, 1)
    pg_kv, vec_3, kv_keep, kv_send = run(
        functools.partial(key_back, steps=steps, **layout, **static),
        "key_back",
        (steps + 2,),
        [lens, tile(2 * width), tile(width), features] + [whole(v.shape) for v in (s_own, s_tot, s_span, s_recv)],
        (lengths, kv, tokens, feature_map, s_own, s_tot, s_span, s_recv),
        (d_part, vec_2),
        out_specs=[tile(2 * width), resident((8, width))] + kv_specs,
        out_shape=[sds((half, 2 * width), bf16), sds((8, width), f32)] + kv_shapes,
        scratch_shapes=state_scratch + back_scratch(2),
        **params(18),
    )
    kv_keep, kv_got = over_core(kv_keep, kv_send)
    up_rows = hidden_units // width
    vec = jnp.concatenate([vec_1[: 6 + up_rows], (vec_2 + vec_3)[:3]], axis=0)
    vec = jnp.pad(vec, ((0, -vec.shape[0] % 16), (0, 0)))
    vec_got = exchange(vec, 2, dp_count)
    d_x, uo_x = x_got[:d_r], x_got[d_r:].reshape(pair(uo_l))
    d_y, uo_y = y_got[:d_l], y_got[d_l:].reshape(pair(uo_r))
    uo_part, uo_ls, uo_rs = route(
        "up_2", [uo_lk, uo_x, uo_rk, uo_y], [flat(uo_l + uo_r), flat(uo_l), flat(uo_r)], second_moves(0, uo_l, uo_r, 0)
    )
    x_got, y_got = exchange(uo_rs, 1, dp_count), exchange(uo_ls, 4, dp_count)
    z_bits = [8 << b for b in range((dp_count // 4).bit_length() - 1)]
    left_z = [dp_count // 4 >> n for n in range(len(z_bits))]

    def start_z(part, n):
        keep, send = odd_even(part, left_z[n])
        return keep, exchange(send, z_bits[n], dp_count)

    def end_z(keep, got, n):
        return added(bf16 if n + 1 < len(z_bits) else f32, keep, got)

    down_z = start_z(third_sum(d_part, d_y, d_x), 0)
    qkv_lk, qkv_ls, qkv_rk, qkv_rs, vec = route(
        "qkv_1",
        [q_keep, q_got, kv_keep, kv_got],
        [pair(qkv_l), flat(2 * qkv_l + 1), pair(qkv_r), pair(qkv_r)],
        [
            (out, (at[0] * qkv_l + at[1],) if out == 1 else at, terms)
            for out, at, terms in first_moves([(0, o_n), (2, 2 * o_n)], qkv_l)
        ],
        (vec + vec_got, None, (1, (2 * qkv_l,))),
        (uo_part, down_z[0]),
    )
    qkv_x, qkv_y = exchange(qkv_ls, 1, dp_count), exchange(qkv_rs, 4, dp_count)

    grad_tokens = run(
        token_grads,
        "token_grads",
        (steps,),
        [tile(width), tile(width), tile(2 * width), square, square, square],
        (agrad, pg_q, pg_kv, wq, wk, wv),
        (qkv_lk,),
        out_specs=tile(width),
        out_shape=sds((half, width), bf16),
        **params(8),
    )
    up_z = start_z(third_sum(uo_part, y_got, x_got), 0)
    down_part = end_z(*down_z, 0)
    if len(z_bits) > 1:
        down_z = start_z(down_part, 1)
    moves = []
    for out, at, terms in second_moves(0, qkv_l, qkv_r, 0):
        terms = [(n, (at_n[0] * qkv_l + at_n[1],) if n == 1 else at_n) for n, at_n in terms]
        moves.append((out, at, terms))
    qkv_part, qkv_ls, qkv_rs, vec = route(
        "qkv_2",
        [qkv_lk, qkv_x, qkv_rk, qkv_y],
        [flat(qkv_n), flat(qkv_l + 1), flat(qkv_r)],
        moves,
        (vec, (1, (2 * qkv_l,)), (1, (qkv_l,))),
        (up_z[0], down_z[0], grad_tokens),
    )
    qkv_x, qkv_y = exchange(qkv_rs, 1, dp_count), exchange(qkv_ls, 4, dp_count)

    def rest(part, z, first):
        for n in range(first, len(z_bits)):
            part = end_z(*z, n)
            if n + 1 < len(z_bits):
                z = start_z(part, n + 1)
        return columns(part)

    d_down = rest(down_part, down_z, 1) if len(z_bits) > 1 else columns(down_part)
    d_up_out = rest(None, up_z, 0)

    def add_vec(vec, got):
        count, blocks = vec.shape[0], vec.shape[1] // 128
        got = got.reshape(-1, 128).astype(f32)
        got = got[: count * blocks] + got[count * blocks :]
        return vec + jnp.concatenate([got[b * count : (b + 1) * count] for b in range(blocks)], axis=1)

    def vec_rows_of(vec):
        hi = vec.astype(bf16)
        lo = (vec - hi.astype(f32)).astype(bf16)
        return jnp.concatenate([v[:, 128 * b : 128 * (b + 1)] for v in (hi, lo) for b in range(vec.shape[1] // 128)], axis=0)

    vec = add_vec(vec, qkv_y[qkv_l])
    part = third_sum(qkv_part, qkv_y[:qkv_l], qkv_x)
    for n, bit in enumerate(z_bits):
        keep, send = odd_even(part, left_z[n])
        got = exchange(jnp.concatenate([send.reshape(-1, 128), vec_rows_of(vec)], axis=0), bit, dp_count)
        size = send.size // 128
        vec = add_vec(vec, got[size:])
        part = end_z(keep, got[:size].reshape(send.shape), n)
    d_qkv = part.reshape(3, o_n, -1, 128).transpose(2, 0, 1, 3).reshape(-1, 3, half_w)
    return (
        output,
        grad_tokens,
        d_qkv,
        vec[6 + up_rows : 9 + up_rows],
        d_up_out[:, half_u:],
        vec[3],
        vec[4],
        vec[5],
        d_up_out[:, :half_u],
        vec[6 : 6 + up_rows].reshape(-1),
        d_down,
        vec[0],
        vec[1],
        vec[2],
    )


def solution(mesh):
    dp_count = mesh.shape["dp"]
    fine = jax.sharding.Mesh(mesh.devices.reshape(dp_count // 4, 2, 2, 2), every_axis)
    dp = ("z", "y", "c")
    rows = P(every_axis, None)
    in_specs = (rows, P(dp, None)) + (P(),) * 13 + (rows,)
    out_specs = (
        rows, rows, P(dp, None, "x"), P(), P(dp, "x"), P(), P(), P(),
        P(dp, "x"), P(), P(dp, "x"), P(), P(), P(),
    )
    return jax.shard_map(body, mesh=fine, in_specs=in_specs, out_specs=out_specs, check_vma=False)
```

time: 309 us -> 228 us (0.74)
  waiting for transfers between devices: 76.4 us -> 28.4 us
  local copies, waits for them, and re-layouts: 38.9 us -> 16.4 us
  other arithmetic: 16.5 us -> 3.86 us
  Pallas kernels: 139 us -> 150 us
  matrix products: 4.9 us -> 0 us
  starting transfers between devices: 27.9 us -> 23.6 us
    ppermute x27 -> x24, waiting for transfers between devices: 76.4 us -> 28.4 us  [exchange(): lax.ppermute(values, every_axis, [(i, i ^ mask) for i in range(2 * dp_cou...]
    dynamic_slice x11 -> x0, local copies, waits for them, and re-layouts: 19.4 us -> none  [the longest x3 12.9 us: reduce_scatter(): keep = lax.dynamic_index_in_dim(part, mine, dim, keepdims=False)]
    convert_element_type x16 -> x11, other arithmetic: 11.8 us -> 0.87 us  [the longest x6 0.82 us: added(): functools.reduce(jnp.add, [p.astype(f32) for p in parts]).astype(dtype)]
    pallas_call x5 -> x11, Pallas kernels: 139 us -> 150 us  [the longest x4 114 us: run(): pl.pallas_call(kernel, name=name, grid=grid, in_specs=list(in_specs) + fe...]
    reshape x9 -> x1, local copies, waits for them, and re-layouts: 10.2 us -> 0.61 us  [body(): vec[6:6 + up_rows].reshape(-1)]
    slice x3 -> x17, local copies, waits for them, and re-layouts: 1.25 us -> 6.16 us  [the longest x5 1.63 us: odd_even(): return [pairs[:, :, k].reshape(part.shape[0], -1, 128) for k in range(2)]]
    dot_general x1 -> x0, matrix products: 4.9 us -> none  [mm_nt(): return lax.dot_general(a, b, nt_dims, preferred_element_type=f32)]
    ppermute x27 -> x24, starting transfers between devices: 27.9 us -> 23.6 us  [exchange(): lax.ppermute(values, every_axis, [(i, i ^ mask) for i in range(2 * dp_cou...]
  transfers between devices with their start and end apart: 27 -> 24, of which waited for: 14 -> 10; matrix products, arithmetic and copies ran while one was open for 16% -> 4% of each run, Pallas kernels for 10% -> 30%
where the time goes in v2:
time: 228 us; the launch traced here: 224 us
  Pallas kernels  150 us (66%)
  waiting for transfers between devices  28.4 us (12%)
  starting transfers between devices  23.6 us (10%)
  local copies, waits for them, and re-layouts  16.4 us (7%)
  other arithmetic  3.86 us (2%)
    pallas_call x4, Pallas kernels, run(): pl.pallas_call(kernel, name=name, grid=grid, in_specs=list(in_specs) + fe...  114 us
    ppermute x24, waiting for transfers between devices, exchange(): lax.ppermute(values, every_axis, [(i, i ^ mask) for i in range(2 * dp_cou...  28.4 us
    ppermute x24, starting transfers between devices, exchange(): lax.ppermute(values, every_axis, [(i, i ^ mask) for i in range(2 * dp_cou...  23.6 us
    pallas_call x5, Pallas kernels, route(): pl.pallas_call(kernel, name=name, grid=(grid,), in_specs=[spec(a.shape) f...  17.6 us
    pallas_call x1, Pallas kernels, body(): pl.pallas_call(functools.partial(forward_keys, **static), name='key_state...  11.9 us
    pallas_call x1, Pallas kernels, body(): pl.pallas_call(functools.partial(forward_queries, heads=heads, hdim=hdim)...  7.43 us
    unnamed x75, local copies, waits for them, and re-layouts  5.08 us
  transfers between devices with their start and end apart: 24, of which 10 were waited for; matrix products, arithmetic and copies ran while one was open for 4% of the time, Pallas kernels for 30%

profile of v2, /device:TPU:0, one launch (start us, length us, event | category | flops | bytes accessed | tf_op | source)
XLA Modules:
  0.0 224.3 jit_solution(4325041870005763966)
XLA Ops:
  0.6 3.8 %slice_bitcast_fusion = (bf16[768,768]{1,0:T(8,128)(2,1)}, bf16[768,768]{1,0:T(8,128)(2,1)}, bf16[768,768]{1,0:T(8,128)(2,1)}) fusion(bf16[768,3,768]{2,0,1:T(8,128)(2,1)} %param.19), kind=kLoop, calls=%fused_computation.2 | loop fusion | bytes 7077888 | tf_op jit(solution)/shard_map/squeeze | solution.py:707
  4.5 11.9 %key_states.1 = (bf16[1024,1536]{1,0:T(8,128)(2,1)}, bf16[3072,256]{1,0:T(8,128)(2,1)}, f32[96,256]{1,0:T(8,128)}, f32[768,256]{1,0:T(8,128)}, bf16[784,256]{1,0:T(8,128)(2,1)}) custom-call(s32[1,4]{1,0:T(1,128)} %len_ref.7, bf16[1024,768]{1,0:T(8,128)(2,1)} %tok_ref.9, bf16[768,768]{1,0:T(8,128)(2,1)} %get-tuple-element.130.wk_ref, ...), custom_call_target="tpu_custom_call" | custom-call | flops 13200000000 | bytes 12000000 | tf_op jit(solution)/shard_map/key_states/pallas_call | solution.py:745
  16.3 3.0 %collective-permute-start = (bf16[784,256]{1,0:T(8,128)(2,1)}, bf16[784,256]{1,0:T(8,128)(2,1)S(1)}, u32[]{:S(2)}, u32[]{:S(2)}) collective-permute-start(bf16[784,256]{1,0:T(8,128)(2,1)} %get-tuple-element.69), channel_id=1, source_target_pairs={{0,1},{1,0},{2,3},{3,2},{4,5},{5,4},{6,7},{7,6},{8,9},{9,8},{10,11... | collective-permute-start | bytes 1204232 | tf_op jit(solution)/shard_map/ppermute | solution.py:590
  19.3 7.4 %query_features.1 = (bf16[1024,768]{1,0:T(8,128)(2,1)}, bf16[1024,3072]{1,0:T(8,128)(2,1)}) custom-call(bf16[1024,768]{1,0:T(8,128)(2,1)} %tok_ref.9, bf16[768,768]{1,0:T(8,128)(2,1)} %get-tuple-element.129.wq_ref, f32[3,768]{1,0:T(4,128)} %b_ref.3, bf16[12,64,256]{2,1,0:T(8,128)(2,1)} %map_ref.7), custom_call_target="tpu_custom_call" | custom-call | flops 7699999744 | bytes 7000000 | tf_op jit(solution)/shard_map/query_features/pallas_call | solution.py:756
  26.7 2.1 collective-permute-done.recv_ref
  29.5 70.9 %chain.1 = (bf16[1024,768]{1,0:T(8,128)(2,1)}, bf16[1024,768]{1,0:T(8,128)(2,1)}, bf16[1024,768]{1,0:T(8,128)(2,1)}, bf16[1024,128]{1,0:T(8,128)(2,1)}, f32[16,7...) custom-call(s32[1,4]{1,0:T(1,128)} %len_ref.7, ...), custom_call_target="tpu_custom_call" | custom-call | flops 72600002560 | bytes 66000000 | tf_op jit(solution)/shard_map/chain/pallas_call | solution.py:738
  101.0 1.7 collective-permute-start.2
  102.7 5.2 %collective-permute-done.1.refs_1_ = bf16[2,2,12,192,128]{4,3,2,1,0:T(8,128)(2,1)} collective-permute-done((bf16[2,2,12,192,128]{4,3,2,1,0:T(8,128)(2,1)}, bf16[2,2,12,192,128]{4,3,2,1,0:T(8,128)(2,1)}, u32[]{:S(2)}, u32[]{:S(2)}) %collective-permute-start.1) | collective-permute-done | bytes 2359328 | tf_op jit(solution)/shard_map/ppermute | solution.py:590
  107.9 3.8 %down_1.1 = (bf16[2,6,192,128]{3,2,1,0:T(8,128)(2,1)}, bf16[2,6,192,128]{3,2,1,0:T(8,128)(2,1)}, bf16[2,6,192,128]{3,2,1,0:T(8,128)(2,1)}, bf16[2,6,192,128]{3,2,1,0:T(8,128)(2,1)}) custom-call(bf16[2,2,12,192,128]{4,3,2,1,0:T(8,128)(2,1)} %get-tuple-element.75.refs_0_, bf16[2,2,12,192,128]{4,3,2,1,0:T(8,128)(2,1)} %collective-permute-done.1.refs_1_), custom_call_target="tpu_custom_call" | custom-call | flops 3300000000 | bytes 3000000 | tf_op jit(solution)/shard_map/down_1/pallas_call | solution.py:644
  111.7 1.7 collective-permute-start.3
  113.4 1.5 collective-permute-start.4
  114.9 16.3 %query_back.1 = (bf16[1024,768]{1,0:T(8,128)(2,1)}, f32[8,768]{1,0:T(8,128)}, bf16[2,2,3,192,128]{4,3,2,1,0:T(8,128)(2,1)}, bf16[2,2,3,192,128]{4,3,2,1,0:T(8,128)(2,1)}) custom-call(s32[1,4]{1,0:T(1,128)} %len_ref.7, bf16[1024,768]{1,0:T(8,128)(2,1)} %get-tuple-element.72.q_ref, bf16[1024,768]{1,0:T(8,128)(2,1)} %get-tuple-element.73.num_ref, ...), custom_call_target="tpu_custom_call" | custom-call | flops 19800000512 | bytes 18000000 | tf_op jit(solution)/shard_map/query_back/pallas_call | solution.py:738
  133.2 5.2 %down_2_up_1.1 = (bf16[12,192,128]{2,1,0:T(8,128)(2,1)}, bf16[2,7,192,128]{3,2,1,0:T(8,128)(2,1)}, bf16[2,8,192,128]{3,2,1,0:T(8,128)(2,1)}, bf16[20,192,128]{2,1,0:T(8,128)(2,1)}, bf16[22,192,128]{2,1,0:T(8,128)(2,1)}) custom-call(bf16[2,6,192,128]{3,2,1,0:T(8,128)(2,1)} %get-tuple-element.77.refs_0_, bf16[2,6,192,128]{3,2,1,0:T(8,128)(2,1)} %copy-done.12, ...), custom_call_target="tpu_custom_call" | custom-call | flops 3300000000 | bytes 3000000 | tf_op jit(solution)/shard_map/down_2_up_1/pallas_call | solution.py:644
  139.3 18.2 %key_back.1 = (bf16[1024,1536]{1,0:T(8,128)(2,1)}, f32[8,768]{1,0:T(8,128)}, bf16[2,2,6,192,128]{4,3,2,1,0:T(8,128)(2,1)}, bf16[2,2,6,192,128]{4,3,2,1,0:T(8,128)(2,1)}) custom-call(s32[1,4]{1,0:T(1,128)} %len_ref.7, bf16[1024,1536]{1,0:T(8,128)(2,1)} %get-tuple-element.79.kv_ref, bf16[1024,768]{1,0:T(8,128)(2,1)} %tok_ref.9, bf16[12,64,256]{2,1,0:T(8,128)(2,1)} %map_ref.7, ...), custom_call_target="tpu_custom_call" | custom-call | flops 19800000512 | bytes 18000000 | tf_op jit(solution)/shard_map/key_back/pallas_call | solution.py:738
  159.0 1.6 collective-permute-done.9
  162.8 1.5 collective-permute-done.11
  165.3 1.6 collective-permute-start.16
  167.8 2.9 %up_2.1 = (bf16[15,192,128]{2,1,0:T(8,128)(2,1)}, bf16[7,192,128]{2,1,0:T(8,128)(2,1)}, bf16[8,192,128]{2,1,0:T(8,128)(2,1)}) custom-call(bf16[2,7,192,128]{3,2,1,0:T(8,128)(2,1)} %get-tuple-element.100.refs_0_, bf16[2,7,192,128]{3,2,1,0:T(8,128)(2,1)} %bitcast.117, bf16[2,8,192,128]{3,2,1,0:T(8,128)(2,1)} %get-tuple-element.102.refs_2_, ...), custom_call_target="tpu_custom_call" | custom-call | flops 3300000000 | bytes 3000000 | tf_op jit(solution)/shard_map/up_2/pallas_call | solution.py:644
  171.1 1.5 collective-permute-start.15
  172.6 1.0 copy-done.9
  173.6 3.3 %qkv_1.1 = (bf16[2,4,192,128]{3,2,1,0:T(8,128)(2,1)}, bf16[9,192,128]{2,1,0:T(8,128)(2,1)}, bf16[2,5,192,128]{3,2,1,0:T(8,128)(2,1)}, bf16[2,5,192,128]{3,2,1,0:T(8,128)(2,1)}, f32[16,768]{1,0:T(8,128)}) custom-call(bf16[2,2,3,192,128]{4,3,2,1,0:T(8,128)(2,1)} %get-tuple-element.94.refs_0_, bf16[2,2,3,192,128]{4,3,2,1,0:T(8,128)(2,1)} %collective-permute-done.7.refs_1_, ...), custom_call_target="tpu_custom_call" | custom-call | flops 3300000000 | bytes 3000000 | tf_op jit(solution)/shard_map/qkv_1/pallas_call | solution.py:644
  177.5 1.5 collective-permute-start.13
  179.0 8.2 %token_grads.1.refs_7_ = bf16[1024,768]{1,0:T(8,128)(2,1)} custom-call(bf16[1024,768]{1,0:T(8,128)(2,1)} %get-tuple-element.71.agrad_ref, bf16[1024,768]{1,0:T(8,128)(2,1)} %get-tuple-element.78.pgq_ref, bf16[1024,1536]{1,0:T(8,128)(2,1)} %get-tuple-element.93.pgkv_ref, bf16[768,768]{1,0:T(8,128)(2,1)} %get-tuple-element.129.wq_ref, ...), custom_call_target="tpu_custom_call" | custom-call | flops 8800000000 | bytes 8000000 | tf_op jit(solution)/shard_map/token_grads/pallas_call | solution.py:738
  188.0 2.6 %collective-permute-start.23 = (bf16[12,48,128]{2,1,0:T(8,128)(2,1)S(1)}, bf16[12,48,128]{2,1,0:T(8,128)(2,1)S(1)}, u32[]{:S(2)}, u32[]{:S(2)}) collective-permute-start(bf16[12,48,128]{2,1,0:T(8,128)(2,1)S(1)} %get-tuple-element.139), channel_id=1, source_target_pairs={{0,16},{1,17},{2,18},{3,19},{4,20},{5,21},{6,22},{7,23},{8,24},{9,... | collective-permute-start | bytes 442376 | tf_op jit(solution)/shard_map/ppermute | solution.py:590
  193.0 2.5 %qkv_2.1 = (bf16[9,192,128]{2,1,0:T(8,128)(2,1)}, bf16[5,192,128]{2,1,0:T(8,128)(2,1)}, bf16[5,192,128]{2,1,0:T(8,128)(2,1)}, f32[16,768]{1,0:T(8,128)}) custom-call(bf16[2,4,192,128]{3,2,1,0:T(8,128)(2,1)} %get-tuple-element.105.refs_0_, bf16[9,192,128]{2,1,0:T(8,128)(2,1)} %copy-done.15, bf16[2,5,192,128]{3,2,1,0:T(8,128)(2,1)} %get-tuple-element.107.refs_2_, ...), custom_call_target="tpu_custom_call" | custom-call | flops 3300000000 | bytes 3000000 | tf_op jit(solution)/shard_map/qkv_2/pallas_call | solution.py:644
  196.8 1.5 collective-permute-start.18
  198.4 3.6 %collective-permute-done.17 = bf16[5,192,128]{2,1,0:T(8,128)(2,1)S(1)} collective-permute-done((bf16[5,192,128]{2,1,0:T(8,128)(2,1)}, bf16[5,192,128]{2,1,0:T(8,128)(2,1)S(1)}, u32[]{:S(2)}, u32[]{:S(2)}) %collective-permute-start.17) | collective-permute-done | bytes 245792 | tf_op jit(solution)/shard_map/ppermute | solution.py:590
  202.1 1.1 collective-permute-done.18
  203.6 1.7 collective-permute-start.19
  206.2 6.7 %collective-permute-done.19 = bf16[1056,128]{1,0:T(8,128)(2,1)S(1)} collective-permute-done((bf16[1056,128]{1,0:T(8,128)(2,1)S(1)}, bf16[1056,128]{1,0:T(8,128)(2,1)S(1)}, u32[]{:S(2)}, u32[]{:S(2)}) %collective-permute-start.19) | collective-permute-done | bytes 270368 | tf_op jit(solution)/shard_map/ppermute | solution.py:590
  213.7 4.0 %collective-permute-done.22 = bf16[15,48,128]{2,0,1:T(8,128)(2,1)S(1)} collective-permute-done((bf16[15,48,128]{2,0,1:T(8,128)(2,1)S(1)}, bf16[15,48,128]{2,0,1:T(8,128)(2,1)S(1)}, u32[]{:S(2)}, u32[]{:S(2)}) %collective-permute-start.22) | collective-permute-done | bytes 184352 | tf_op jit(solution)/shard_map/ppermute | solution.py:590
  219.2 1.9 collective-permute-done.20
  (148 shorter events, 21.4 us)
Async XLA Ops:
  16.3 12.5 %collective-permute-start = (bf16[784,256]{1,0:T(8,128)(2,1)}, bf16[784,256]{1,0:T(8,128)(2,1)S(1)}, u32[]{:S(2)}, u32[]{:S(2)}) collective-permute-start(bf16[784,256]{1,0:T(8,128)(2,1)} %get-tuple-element.69), channel_id=1, source_target_pairs={{0,1},{1,0},{2,3},{3,2},{4,5},{5,4},{6,7},{7,6},{8,9},{9,8},{10,11... | collective-permute-start | bytes 1204232 | tf_op jit(solution)/shard_map/ppermute | solution.py:590
  100.4 7.5 %collective-permute-start.1 = (bf16[2,2,12,192,128]{4,3,2,1,0:T(8,128)(2,1)}, bf16[2,2,12,192,128]{4,3,2,1,0:T(8,128)(2,1)}, u32[]{:S(2)}, u32[]{:S(2)}) collective-permute-start(bf16[2,2,12,192,128]{4,3,2,1,0:T(8,128)(2,1)} %get-tuple-element.76), channel_id=1, source_target_pairs={{0,2},{1,3},{2,0},{3,1},{4,6},{5,7},{6,4},{7,5},{8,10},{9,11},{10,... | collective-permute-start | bytes 7077896 | tf_op jit(solution)/shard_map/ppermute | solution.py:590
  100.5 30.8 %collective-permute-start.5 = (bf16[2,2,12,192,128]{4,3,2,1,0:T(8,128)(2,1)}, bf16[2,2,12,192,128]{4,3,2,1,0:T(8,128)(2,1)S(1)}, u32[]{:S(2)}, u32[]{:S(2)}) collective-permute-start(bf16[2,2,12,192,128]{4,3,2,1,0:T(8,128)(2,1)} %get-tuple-element.88), channel_id=1, source_target_pairs={{0,2},{1,3},{2,0},{3,1},{4,6},{5,7},{6,4},{7,5},{8,10},{9,11},{10,... | collective-permute-start | bytes 7077896 | tf_op jit(solution)/shard_map/ppermute | solution.py:590
  101.0 38.3 %collective-permute-start.2 = (bf16[784,256]{1,0:T(8,128)(2,1)}, bf16[784,256]{1,0:T(8,128)(2,1)}, u32[]{:S(2)}, u32[]{:S(2)}) collective-permute-start(bf16[784,256]{1,0:T(8,128)(2,1)} %get-tuple-element.83), channel_id=1, source_target_pairs={{0,1},{1,0},{2,3},{3,2},{4,5},{5,4},{6,7},{7,6},{8,9},{9,8},{10,11... | collective-permute-start | bytes 1204232 | tf_op jit(solution)/shard_map/ppermute | solution.py:590
  102.7 28.5 %collective-permute-start.6 = (bf16[2,2,3,192,128]{4,3,2,1,0:T(8,128)(2,1)}, bf16[2,2,3,192,128]{4,3,2,1,0:T(8,128)(2,1)S(1)}, u32[]{:S(2)}, u32[]{:S(2)}) collective-permute-start(bf16[2,2,3,192,128]{4,3,2,1,0:T(8,128)(2,1)} %get-tuple-element.90), channel_id=1, source_target_pairs={{0,2},{1,3},{2,0},{3,1},{4,6},{5,7},{6,4},{7,5},{8,10},{9,11},{10,... | collective-permute-start | bytes 1769480 | tf_op jit(solution)/shard_map/ppermute | solution.py:590
  111.7 19.6 %collective-permute-start.3 = (bf16[2,6,192,128]{3,2,1,0:T(8,128)(2,1)}, bf16[2,6,192,128]{3,2,1,0:T(8,128)(2,1)S(1)}, u32[]{:S(2)}, u32[]{:S(2)}) collective-permute-start(bf16[2,6,192,128]{3,2,1,0:T(8,128)(2,1)} %get-tuple-element.84), channel_id=1, source_target_pairs={{0,1},{1,0},{2,3},{3,2},{4,5},{5,4},{6,7},{7,6},{8,9},{9,8},{10,11... | collective-permute-start | bytes 1769480 | tf_op jit(solution)/shard_map/ppermute | solution.py:590
  113.4 17.9 %collective-permute-start.4 = (bf16[2,6,192,128]{3,2,1,0:T(8,128)(2,1)}, bf16[2,6,192,128]{3,2,1,0:T(8,128)(2,1)S(1)}, u32[]{:S(2)}, u32[]{:S(2)}) collective-permute-start(bf16[2,6,192,128]{3,2,1,0:T(8,128)(2,1)} %get-tuple-element.86), channel_id=1, source_target_pairs={{0,4},{1,5},{2,6},{3,7},{4,0},{5,1},{6,2},{7,3},{8,12},{9,13},{10,... | collective-permute-start | bytes 1769480 | tf_op jit(solution)/shard_map/ppermute | solution.py:590
  138.4 23.5 %collective-permute-start.10 = (bf16[20,192,128]{2,1,0:T(8,128)(2,1)}, bf16[20,192,128]{2,1,0:T(8,128)(2,1)S(1)}, u32[]{:S(2)}, u32[]{:S(2)}) collective-permute-start(bf16[20,192,128]{2,1,0:T(8,128)(2,1)} %get-tuple-element.101), channel_id=1, source_target_pairs={{0,1},{1,0},{2,3},{3,2},{4,5},{5,4},{6,7},{7,6},{8,9},{9,8},{10,11... | collective-permute-start | bytes 2949128 | tf_op jit(solution)/shard_map/ppermute | solution.py:590
  139.0 25.3 %collective-permute-start.11 = (bf16[22,192,128]{2,1,0:T(8,128)(2,1)}, bf16[22,192,128]{2,1,0:T(8,128)(2,1)S(1)}, u32[]{:S(2)}, u32[]{:S(2)}) collective-permute-start(bf16[22,192,128]{2,1,0:T(8,128)(2,1)} %get-tuple-element.103), channel_id=1, source_target_pairs={{0,4},{1,5},{2,6},{3,7},{4,0},{5,1},{6,2},{7,3},{8,12},{9,13},{10,... | collective-permute-start | bytes 3244040 | tf_op jit(solution)/shard_map/ppermute | solution.py:590
  139.3 18.3 %copy-start.7 = (f32[8,768]{1,0:T(8,128)S(1)}, f32[8,768]{1,0:T(8,128)}, u32[]{:S(2)}) copy-start(f32[8,768]{1,0:T(8,128)} %get-tuple-element.92.refs_1_) | copy-start | bytes 73732
  139.3 19.1 %copy-start.5 = (f32[16,768]{1,0:T(8,128)S(1)}, f32[16,768]{1,0:T(8,128)}, u32[]{:S(2)}) copy-start(f32[16,768]{1,0:T(8,128)} %get-tuple-element.98) | copy-start | bytes 147460
  139.3 19.6 %copy-start.10 = (bf16[2,2,3,192,128]{4,3,2,1,0:T(8,128)(2,1)S(1)}, bf16[2,2,3,192,128]{4,3,2,1,0:T(8,128)(2,1)}, u32[]{:S(2)}) copy-start(bf16[2,2,3,192,128]{4,3,2,1,0:T(8,128)(2,1)} %get-tuple-element.95) | copy-start | bytes 1769476
  157.5 6.8 %copy-start.3 = (bf16[12,192,128]{2,1,0:T(8,128)(2,1)S(1)}, bf16[12,192,128]{2,1,0:T(8,128)(2,1)}, u32[]{:S(2)}) copy-start(bf16[12,192,128]{2,1,0:T(8,128)(2,1)} %get-tuple-element.91.refs_0_) | copy-start | bytes 1769476
  157.5 15.1 %collective-permute-start.8 = (bf16[2,2,6,192,128]{4,3,2,1,0:T(8,128)(2,1)}, bf16[2,2,6,192,128]{4,3,2,1,0:T(8,128)(2,1)S(1)}, u32[]{:S(2)}, u32[]{:S(2)}) collective-permute-start(bf16[2,2,6,192,128]{4,3,2,1,0:T(8,128)(2,1)} %get-tuple-element.97), channel_id=1, source_target_pairs={{0,2},{1,3},{2,0},{3,1},{4,6},{5,7},{6,4},{7,5},{8,10},{9,11},{10,... | collective-permute-start | bytes 3538952 | tf_op jit(solution)/shard_map/ppermute | solution.py:590
  158.4 2.1 collective-permute-start.9
  158.9 13.7 %collective-permute-start.7 = (bf16[2,2,3,192,128]{4,3,2,1,0:T(8,128)(2,1)S(1)}, bf16[2,2,3,192,128]{4,3,2,1,0:T(8,128)(2,1)}, u32[]{:S(2)}, u32[]{:S(2)}) collective-permute-start(bf16[2,2,3,192,128]{4,3,2,1,0:T(8,128)(2,1)S(1)} %copy-done.10), channel_id=1, source_target_pairs={{0,2},{1,3},{2,0},{3,1},{4,6},{5,7},{6,4},{7,5},{8,10},{9,11},{10,... | collective-permute-start | bytes 1769480 | tf_op jit(solution)/shard_map/ppermute | solution.py:590
  165.3 22.0 %collective-permute-start.16 = (bf16[12,96,128]{2,1,0:T(8,128)(2,1)S(1)}, bf16[12,96,128]{2,1,0:T(8,128)(2,1)S(1)}, u32[]{:S(2)}, u32[]{:S(2)}) collective-permute-start(bf16[12,96,128]{2,1,0:T(8,128)(2,1)S(1)} %bitcast.122), channel_id=1, source_target_pairs={{0,8},{1,9},{2,10},{3,11},{4,12},{5,13},{6,14},{7,15},{8,0},{9,1},... | collective-permute-start | bytes 884744 | tf_op jit(solution)/shard_map/ppermute | solution.py:590
  170.6 20.0 %collective-permute-start.14 = (bf16[7,192,128]{2,1,0:T(8,128)(2,1)}, bf16[7,192,128]{2,1,0:T(8,128)(2,1)S(1)}, u32[]{:S(2)}, u32[]{:S(2)}) collective-permute-start(bf16[7,192,128]{2,1,0:T(8,128)(2,1)} %get-tuple-element.110), channel_id=1, source_target_pairs={{0,4},{1,5},{2,6},{3,7},{4,0},{5,1},{6,2},{7,3},{8,12},{9,13},{10,... | collective-permute-start | bytes 1032200 | tf_op jit(solution)/shard_map/ppermute | solution.py:590
  171.1 19.5 %collective-permute-start.15 = (bf16[8,192,128]{2,1,0:T(8,128)(2,1)}, bf16[8,192,128]{2,1,0:T(8,128)(2,1)S(1)}, u32[]{:S(2)}, u32[]{:S(2)}) collective-permute-start(bf16[8,192,128]{2,1,0:T(8,128)(2,1)} %get-tuple-element.111), channel_id=1, source_target_pairs={{0,1},{1,0},{2,3},{3,2},{4,5},{5,4},{6,7},{7,6},{8,9},{9,8},{10,11... | collective-permute-start | bytes 1179656 | tf_op jit(solution)/shard_map/ppermute | solution.py:590
  176.9 15.2 %collective-permute-start.12 = (bf16[9,192,128]{2,1,0:T(8,128)(2,1)}, bf16[9,192,128]{2,1,0:T(8,128)(2,1)S(1)}, u32[]{:S(2)}, u32[]{:S(2)}) collective-permute-start(bf16[9,192,128]{2,1,0:T(8,128)(2,1)} %get-tuple-element.106), channel_id=1, source_target_pairs={{0,1},{1,0},{2,3},{3,2},{4,5},{5,4},{6,7},{7,6},{8,9},{9,8},{10,11... | collective-permute-start | bytes 1327112 | tf_op jit(solution)/shard_map/ppermute | solution.py:590
  177.5 14.6 %collective-permute-start.13 = (bf16[2,5,192,128]{3,2,1,0:T(8,128)(2,1)}, bf16[2,5,192,128]{3,2,1,0:T(8,128)(2,1)S(1)}, u32[]{:S(2)}, u32[]{:S(2)}) collective-permute-start(bf16[2,5,192,128]{3,2,1,0:T(8,128)(2,1)} %get-tuple-element.108), channel_id=1, source_target_pairs={{0,4},{1,5},{2,6},{3,7},{4,0},{5,1},{6,2},{7,3},{8,12},{9,13},{10,... | collective-permute-start | bytes 1474568 | tf_op jit(solution)/shard_map/ppermute | solution.py:590
  179.0 8.2 %copy-start.1 = (bf16[12,2,1,48,128]{4,3,2,1,0:T(8,128)(2,1)S(1)}, bf16[12,2,1,48,128]{4,3,2,1,0:T(8,128)(2,1)}, u32[]{:S(2)}) copy-start(bf16[12,2,1,48,128]{4,3,2,1,0:T(8,128)(2,1)} %get-tuple-element.134) | copy-start | bytes 884740
  187.2 3.4 %copy-start.2 = (bf16[15,192,128]{2,1,0:T(8,128)(2,1)S(1)}, bf16[15,192,128]{2,1,0:T(8,128)(2,1)}, u32[]{:S(2)}) copy-start(bf16[15,192,128]{2,1,0:T(8,128)(2,1)} %get-tuple-element.104.refs_5_) | copy-start | bytes 2211844
  188.0 8.1 %collective-permute-start.23 = (bf16[12,48,128]{2,1,0:T(8,128)(2,1)S(1)}, bf16[12,48,128]{2,1,0:T(8,128)(2,1)S(1)}, u32[]{:S(2)}, u32[]{:S(2)}) collective-permute-start(bf16[12,48,128]{2,1,0:T(8,128)(2,1)S(1)} %get-tuple-element.139), channel_id=1, source_target_pairs={{0,16},{1,17},{2,18},{3,19},{4,20},{5,21},{6,22},{7,23},{8,24},{9,... | collective-permute-start | bytes 442376 | tf_op jit(solution)/shard_map/ppermute | solution.py:590
  191.6 13.7 %collective-permute-start.21 = (bf16[15,96,128]{2,1,0:T(8,128)(2,1)S(1)}, bf16[15,96,128]{2,1,0:T(8,128)(2,1)S(1)}, u32[]{:S(2)}, u32[]{:S(2)}) collective-permute-start(bf16[15,96,128]{2,1,0:T(8,128)(2,1)S(1)} %bitcast.121), channel_id=1, source_target_pairs={{0,8},{1,9},{2,10},{3,11},{4,12},{5,13},{6,14},{7,15},{8,0},{9,1},... | collective-permute-start | bytes 1105928 | tf_op jit(solution)/shard_map/ppermute | solution.py:590
  195.5 7.7 %copy-start.4 = (bf16[9,192,128]{2,1,0:T(8,128)(2,1)S(1)}, bf16[9,192,128]{2,1,0:T(8,128)(2,1)}, u32[]{:S(2)}) copy-start(bf16[9,192,128]{2,1,0:T(8,128)(2,1)} %get-tuple-element.112) | copy-start | bytes 1327108
  195.5 6.5 %collective-permute-start.17 = (bf16[5,192,128]{2,1,0:T(8,128)(2,1)}, bf16[5,192,128]{2,1,0:T(8,128)(2,1)S(1)}, u32[]{:S(2)}, u32[]{:S(2)}) collective-permute-start(bf16[5,192,128]{2,1,0:T(8,128)(2,1)} %get-tuple-element.113), channel_id=1, source_target_pairs={{0,4},{1,5},{2,6},{3,7},{4,0},{5,1},{6,2},{7,3},{8,12},{9,13},{10,... | collective-permute-start | bytes 737288 | tf_op jit(solution)/shard_map/ppermute | solution.py:590
  196.8 6.4 %collective-permute-start.18 = (bf16[5,192,128]{2,1,0:T(8,128)(2,1)}, bf16[5,192,128]{2,1,0:T(8,128)(2,1)S(1)}, u32[]{:S(2)}, u32[]{:S(2)}) collective-permute-start(bf16[5,192,128]{2,1,0:T(8,128)(2,1)} %get-tuple-element.114), channel_id=1, source_target_pairs={{0,1},{1,0},{2,3},{3,2},{4,5},{5,4},{6,7},{7,6},{8,9},{9,8},{10,11... | collective-permute-start | bytes 737288 | tf_op jit(solution)/shard_map/ppermute | solution.py:590
  202.1 3.2 %copy-start = (bf16[15,2,1,48,128]{4,3,2,1,0:T(8,128)(2,1)S(1)}, bf16[15,2,1,48,128]{4,3,2,1,0:T(8,128)(2,1)}, u32[]{:S(2)}) copy-start(bf16[15,2,1,48,128]{4,3,2,1,0:T(8,128)(2,1)} %get-tuple-element.132) | copy-start | bytes 1105924
  203.6 9.3 %collective-permute-start.19 = (bf16[1056,128]{1,0:T(8,128)(2,1)S(1)}, bf16[1056,128]{1,0:T(8,128)(2,1)S(1)}, u32[]{:S(2)}, u32[]{:S(2)}) collective-permute-start(bf16[1056,128]{1,0:T(8,128)(2,1)S(1)} %constant_dynamic-update-slice_fusion.6), channel_id=1, source_target_pairs={{0,8},{1,9},{2,10},{3,11},{4,12},{5,13},{6,14},{7,15},{8,0},{9,1},... | collective-permute-start | bytes 811016 | tf_op jit(solution)/shard_map/ppermute | solution.py:590
  205.5 12.2 %collective-permute-start.22 = (bf16[15,48,128]{2,0,1:T(8,128)(2,1)S(1)}, bf16[15,48,128]{2,0,1:T(8,128)(2,1)S(1)}, u32[]{:S(2)}, u32[]{:S(2)}) collective-permute-start(bf16[15,48,128]{2,0,1:T(8,128)(2,1)S(1)} %bitcast.123), channel_id=1, source_target_pairs={{0,16},{1,17},{2,18},{3,19},{4,20},{5,21},{6,22},{7,23},{8,24},{9,... | collective-permute-start | bytes 552968 | tf_op jit(solution)/shard_map/ppermute | solution.py:590
  213.3 7.9 %collective-permute-start.20 = (bf16[624,128]{1,0:T(8,128)(2,1)S(1)}, bf16[624,128]{1,0:T(8,128)(2,1)S(1)}, u32[]{:S(2)}, u32[]{:S(2)}) collective-permute-start(bf16[624,128]{1,0:T(8,128)(2,1)S(1)} %constant_dynamic-update-slice_fusion.25), channel_id=1, source_target_pairs={{0,16},{1,17},{2,18},{3,19},{4,20},{5,21},{6,22},{7,23},{8,24},{9,... | collective-permute-start | bytes 479240 | tf_op jit(solution)/shard_map/ppermute | solution.py:590
  (9 other events, 11.0 us)

commit v3 on v2

--- a/solution.py
+++ b/solution.py
@@ -12,7 +12,8 @@
 norm_epsilon = 1e-06
 root_half = 0.7071067811865476
 inv_root_tau = 0.3989422804014327
-vmem_limit = 60 * 1024 * 1024
+vmem_limit = 62 * 1024 * 1024
+stream_lead = 6
 nt_dims = (((1,), (1,)), ((), ()))
 
 
@@ -87,7 +88,8 @@
     recv_tot = recv_ref[heads * hdim :, :].astype(f32)
     seg_row = iota((8, feat), 0)
     for h in range(heads):
-        st_ref[h * wide : (h + 1) * wide, :] = own_ref[h * wide : (h + 1) * wide, :]
+        if own_ref is not None:
+            st_ref[h * wide : (h + 1) * wide, :] = own_ref[h * wide : (h + 1) * wide, :]
         both = span_ref[h * hdim : (h + 1) * hdim, :] + recv_ref[h * hdim : (h + 1) * hdim, :].astype(f32)
         at = pl.multiple_of(h * wide + here * hdim, hdim)
         st_ref[pl.ds(at, hdim), :] = both.astype(bf16)
@@ -131,8 +133,8 @@
 
 def seg_masks(first, rows, hdim, nseg, starts, ends):
     pos = first + iota((rows, nseg * hdim), 0)
-    wide = inside(pos, iota((rows, nseg * hdim), 1) // hdim, starts, ends)
-    lane8 = iota((rows, 128), 1) % 8
+    wide = inside(pos, iota((rows, nseg * hdim), 1) >> (hdim.bit_length() - 1), starts, ends)
+    lane8 = iota((rows, 128), 1) & 7
     pos = first + iota((rows, 128), 0)
     eight = jnp.logical_and(lane8 < nseg, inside(pos, lane8, starts, ends))
     return wide, eight
@@ -260,12 +262,26 @@
     return pl.multiple_of(jnp.bitwise_xor(x, xr) * half_width, 128)
 
 
+def interleave(first, second, lead):
+    alive = [first, second]
+    turn = 0
+    while alive:
+        for stream in list(alive):
+            if stream is second and turn < lead and first in alive:
+                continue
+            try:
+                next(stream)
+            except StopIteration:
+                alive.remove(stream)
+        turn += 1
+
+
 def chain(
-    len_ref, tok_ref, qf_ref, cot_ref, own_ref, tot_ref, span_ref, recv_ref, wo_ref, bo_ref, g1_ref, s1_ref,
+    len_ref, tok_ref, qf_ref, cot_ref, own_hbm, tot_ref, span_ref, recv_ref, wo_ref, bo_ref, g1_ref, s1_ref,
     wup_hbm, bup_ref, wdn_hbm, bdn_ref, g2_ref, s2_ref,
-    out_ref, agrad_ref, num_ref, dgm_ref, vec_ref, sown_ref, stot_ref, sspan_ref, ssend_ref,
-    dkeep_ref, dsend_ref, ukeep_ref, usend_ref, okeep_ref, osend_ref,
-    st_ref, totp_ref, acc_ref, act_ref, up_ref, mix_ref, slope_ref, dlhs_ref, ulhs_ref, olhs_ref, tmp_ref, wup_ref, wdn_ref, sem,
+    out_ref, agrad_ref, num_ref, dgm_ref, normed_ref, mixed_ref, ugrad_hbm, vec_ref, sown_ref, stot_ref, sspan_ref, ssend_ref,
+    dkeep_ref, dsend_ref,
+    st_ref, totp_ref, expand_ref, gather_ref, acc_ref, act_ref, ugrad_ref, dlhs_ref, tmp_ref, wup_ref, wdn_ref, sem,
     *, half, nseg, heads, hdim, chunk, steps, dp_count, sort
 ):
     step = pl.program_id(0)
@@ -275,54 +291,68 @@
     hidden_units = wup_ref.shape[1]
     starts, ends = bounds(len_ref, nseg)
     here = spanning(ends, half)
-    first = lax.axis_index("x") * half + step * rows
+    x = lax.axis_index("x")
     fetch = [pltpu.make_async_copy(wup_hbm, wup_ref, sem.at[0]), pltpu.make_async_copy(wdn_hbm, wdn_ref, sem.at[1])]
+    fetch_own = pltpu.make_async_copy(own_hbm, st_ref, sem.at[2])
+
+    def store(n, side):
+        own = hidden_units // 2
+        to = ugrad_hbm.at[pl.ds(pl.multiple_of(n * rows, 128), rows), pl.ds(half_cols(side, own), own)]
+        return pltpu.make_async_copy(ugrad_ref.at[:, side * own : (side + 1) * own], to, sem.at[3 + side])
 
     @pl.when(step == 0)
     def _():
+        fetch_own.start()
         fetch[0].start()
         fetch[1].start()
+        fetch_own.wait()
         vec_ref[...] = jnp.zeros_like(vec_ref)
         acc_ref[...] = jnp.zeros_like(acc_ref)
-        put_states(own_ref, tot_ref, span_ref, recv_ref, st_ref, totp_ref, here, nseg, heads, hdim)
-
-    @pl.when(step < steps)
-    def _():
-        at = pl.multiple_of(step * rows, 128)
-        mine = pl.ds(at, rows)
-        seg_wide, seg8 = seg_masks(first, rows, hdim, nseg, starts, ends)
-        low_half = iota((rows, 128), 1) < hdim
+        put_states(None, tot_ref, span_ref, recv_ref, st_ref, totp_ref, here, nseg, heads, hdim)
+        shift = hdim.bit_length() - 1
+        lane = iota((256, width), 0) & 127
+        expand_ref[:, :width] = as_bf((lane >> 3) == (iota((256, width), 1) >> shift))
+        expand_ref[:, width:] = as_bf(((iota((256, 128), 0) & 127) >> 3) == (iota((256, 128), 1) >> 3))
+        for k in range(2):
+            gather_ref[k * width : (k + 1) * width, :] = as_bf((iota((width, 128), 0) >> shift) == (iota((width, 128), 1) >> 3))
+        fetch[0].wait()
+        fetch[1].wait()
+
+    def part(lo, size):
+        mine = slice(lo, lo + size)
+        at = pl.multiple_of(step * rows + lo, 128)
+        first = x * half + step * rows + lo
+        seg_wide, seg8 = seg_masks(first, size, hdim, nseg, starts, ends)
+        low_half = iota((size, 128), 1) < hdim
         nums = []
         for p in range(heads // 2):
             folded = []
             for j in range(2):
                 h = 2 * p + j
-                r = mm_nt(qf_ref[:, feat * h : feat * (h + 1)], st_ref[wide * h : wide * (h + 1), :])
+                r = mm_nt(qf_ref[mine, feat * h : feat * (h + 1)], st_ref[wide * h : wide * (h + 1), :])
                 r = jnp.where(seg_wide, r, 0.0)
                 folded.append(r[:, :128] + r[:, 128:])
             nums.append(fold_pair(folded, low_half, hdim))
+            yield
         numer = jnp.concatenate(nums, axis=1)
-        den_parts = split_hi_lo(jnp.where(seg8, mm_nt(qf_ref[...], totp_ref[...]), 0.0))
-        expand = as_bf((iota((256, width), 0) % 128) // 8 == iota((256, width), 1) // hdim)
-        same8 = as_bf((iota((256, 128), 0) % 128) // 8 == iota((256, 128), 1) // 8)
-        dead = jnp.where(first + iota((rows, 128), 0) < ends[-1], 0.0, 1.0)
-        spare = jnp.where(iota((rows, 128), 1) < 8 * heads, dead, 1.0)
-        inv_c = 1.0 / (mm(den_parts, same8) + spare)
-        inv_w = 1.0 / (mm(den_parts, expand) + jnp.concatenate([dead] * (width // 128), axis=1))
+        den_parts = split_hi_lo(jnp.where(seg8, mm_nt(qf_ref[mine, :], totp_ref[...]), 0.0))
+        yield
+        dead = jnp.where(first + iota((size, 128), 0) < ends[-1], 0.0, 1.0)
+        spare = jnp.where(iota((size, 128), 1) < 8 * heads, dead, 1.0)
+        den_w = mm(den_parts, expand_ref[...])
+        inv_c = 1.0 / (den_w[:, width:] + spare)
+        inv_w = 1.0 / (den_w[:, :width] + jnp.concatenate([dead] * (width // 128), axis=1))
+        yield
         ratio = numer * inv_w
         mixed = ratio.astype(bf16)
-        mix_ref[mine, :] = mixed
-
-        hidden = tok_ref[...].astype(f32) + mm_nt(mixed, wo_ref[...]) + flat_row(bo_ref)
+        mixed_ref[mine, :] = mixed
+        hidden = tok_ref[mine, :].astype(f32) + mm_nt(mixed, wo_ref[...]) + flat_row(bo_ref)
+        yield
         scaled1, inverse1 = norm_parts(hidden)
         normed = scaled1 * flat_row(g1_ref) + flat_row(s1_ref)
         normed_bf = normed.astype(bf16)
-        put_transposed(ulhs_ref, tmp_ref, normed_bf, at, row_sources(dp_count) if sort else [])
-
-        @pl.when(step == 0)
-        def _():
-            fetch[0].wait()
-            fetch[1].wait()
+        normed_ref[mine, :] = normed_bf
+        yield
 
         count = hidden_units // chunk
         cols = [slice(c * chunk, (c + 1) * chunk) for c in range(count)]
@@ -334,30 +364,32 @@
             later = mm(normed_bf, wup_ref[:, cols[c + 1]]) + bup[:, cols[c + 1]] if c + 1 < count else None
             act, slope = gelu_parts(up)
             act = act.astype(bf16)
-            act_ref[mine, cols[c]] = act
-            slope_ref[:, cols[c]] = slope.astype(slope_ref.dtype)
+            act_ref[pl.ds(at, size), cols[c]] = act
+            ugrad_ref[mine, cols[c]] = slope.astype(bf16)
             if last is not None:
                 branch += mm_nt(last, wdn_ref[:, cols[c - 1]])
             last, up = act, later
+            yield
         final = branch + mm_nt(last, wdn_ref[:, cols[count - 1]])
+        yield
         scaled2, inverse2 = norm_parts(final)
         gain2 = flat_row(g2_ref)
-        out_ref[...] = (scaled2 * gain2 + flat_row(s2_ref)).astype(bf16)
-        incoming = cot_ref[...].astype(f32)
+        out_ref[mine, :] = (scaled2 * gain2 + flat_row(s2_ref)).astype(bf16)
+        incoming = cot_ref[mine, :].astype(f32)
         grad_final = norm_backward(incoming, scaled2, inverse2, gain2)
         bgrad = grad_final.astype(bf16)
         add_row(vec_ref, 0, grad_final)
         add_row(vec_ref, 1, incoming * scaled2)
         add_row(vec_ref, 2, incoming)
+        yield
         put_transposed(dlhs_ref, tmp_ref, bgrad, at, row_sources(dp_count) if sort else [])
-
         grad_normed = grad_final
         wide_grad = mm(bgrad, wdn_ref[:, cols[0]])
         last = None
         for c in range(count):
             later = mm(bgrad, wdn_ref[:, cols[c + 1]]) if c + 1 < count else None
-            ugrad = (wide_grad * slope_ref[:, cols[c]].astype(f32)).astype(bf16)
-            up_ref[mine, cols[c]] = ugrad
+            ugrad = (wide_grad * ugrad_ref[mine, cols[c]].astype(f32)).astype(bf16)
+            ugrad_ref[mine, cols[c]] = ugrad
             sums = jnp.sum(ugrad.astype(f32), axis=0, keepdims=True)
             for k in range(0, chunk, 128):
                 row, col = divmod(c * chunk + k, width)
@@ -365,26 +397,29 @@
             if last is not None:
                 grad_normed += mm_nt(last, wup_ref[:, cols[c - 1]])
             last, wide_grad = ugrad, later
+            yield
         grad_normed += mm_nt(last, wup_ref[:, cols[count - 1]])
+        yield
 
         grad_hidden = norm_backward(grad_normed, scaled1, inverse1, flat_row(g1_ref))
         add_row(vec_ref, 3, grad_hidden)
         add_row(vec_ref, 4, grad_normed * scaled1)
         add_row(vec_ref, 5, grad_normed)
         agrad = grad_hidden.astype(bf16)
-        agrad_ref[...] = agrad
-        put_transposed(olhs_ref, tmp_ref, agrad, at, row_sources(dp_count) if sort else [])
+        agrad_ref[mine, :] = agrad
+        yield
 
         grad_mixed = mm(agrad, wo_ref[...])
         num_grad = (grad_mixed * inv_w).astype(bf16)
-        num_ref[...] = num_grad
+        num_ref[mine, :] = num_grad
         inner = split_hi_lo(grad_mixed * ratio)
-        gather = as_bf((iota((2 * width, 128), 0) % width) // hdim == iota((2 * width, 128), 1) // 8)
-        den_m = jnp.where(seg8, -(mm(inner, gather) * inv_c), 0.0).astype(bf16)
-        dgm_ref[...] = den_m
+        yield
+        den_m = jnp.where(seg8, -(mm(inner, gather_ref[...]) * inv_c), 0.0).astype(bf16)
+        dgm_ref[mine, :] = den_m
         den_t = den_m.T
-        masks, _ = lane_segment_masks(first, rows, hdim, starts, ends)
-        pad = jnp.zeros((8, rows), bf16)
+        masks, _ = lane_segment_masks(first, size, hdim, starts, ends)
+        pad = jnp.zeros((8, size), bf16)
+        yield
         for p in range(heads // 2):
             num_t = num_grad[:, 128 * p : 128 * (p + 1)].T
             tails = den_t[16 * p : 16 * p + 16, :]
@@ -392,7 +427,20 @@
                 h = 2 * p + j
                 tail = jnp.concatenate([tails[8 * j : 8 * j + 8, :], pad], axis=0)
                 lhs = masked_rows(num_t[j * hdim : (j + 1) * hdim, :], masks, tail)
-                acc_ref[h] += mm(lhs, qf_ref[:, feat * h : feat * (h + 1)])
+                acc_ref[h] += mm(lhs, qf_ref[mine, feat * h : feat * (h + 1)])
+            yield
+
+    @pl.when(jnp.logical_and(step >= 1, step <= steps))
+    def _():
+        store(step - 1, 0).wait()
+        store(step - 1, 1).wait()
+
+    @pl.when(step < steps)
+    def _():
+        size = rows // 2
+        interleave(part(0, size), part(size, size), stream_lead)
+        store(step, 0).start()
+        store(step, 1).start()
 
     @pl.when(step == steps - 1)
     def _():
@@ -402,22 +450,38 @@
     count = hidden_units // chunk
     tile = step - steps
 
-    @pl.when(jnp.logical_and(tile >= 0, tile < count))
+    @pl.when(tile >= 0)
     def _():
         xr = tile // (count // 2)
         at = half_cols(xr, own) + (tile - xr * (count // 2)) * chunk
         rhs = act_ref[:, pl.ds(pl.multiple_of(at, 128), chunk)]
         put_grad(dkeep_ref, dsend_ref, mm(dlhs_ref[...], rhs))
 
-    @pl.when(jnp.logical_and(tile >= count, tile < 2 * count))
-    def _():
-        xr = (tile - count) // (count // 2)
-        at = half_cols(xr, own) + (tile - count - xr * (count // 2)) * chunk
-        put_grad(ukeep_ref, usend_ref, mm(ulhs_ref[...], up_ref[:, pl.ds(pl.multiple_of(at, 128), chunk)]))
-
-    @pl.when(tile >= 2 * count)
-    def _():
-        rhs = mix_ref[:, pl.ds(half_cols(tile - 2 * count, width // 2), width // 2)]
+
+def up_out_grads(
+    normed_ref, agrad_ref, mixed_ref, ugrad_ref,
+    *refs,
+    count, dp_count, sort
+):
+    ukeep_ref, usend_ref, okeep_ref, osend_ref, ulhs_ref, olhs_ref, tmp_ref = refs[-7:]
+    step = pl.program_id(0)
+    width = normed_ref.shape[1]
+
+    @pl.when(step == 0)
+    def _():
+        put_transposed(ulhs_ref, tmp_ref, normed_ref[...], 0, row_sources(dp_count) if sort else [])
+
+    @pl.when(step < count)
+    def _():
+        put_grad(ukeep_ref, usend_ref, mm(ulhs_ref[...], ugrad_ref[...]))
+
+    @pl.when(step == count)
+    def _():
+        put_transposed(olhs_ref, tmp_ref, agrad_ref[...], 0, row_sources(dp_count) if sort else [])
+
+    @pl.when(step >= count)
+    def _():
+        rhs = mixed_ref[:, pl.ds(half_cols(step - count, width // 2), width // 2)]
         put_grad(okeep_ref, osend_ref, mm(olhs_ref[...], rhs))
 
 
@@ -452,8 +516,8 @@
 
 def key_back(
     len_ref, kv_ref, tok_ref, map_ref, own_ref, tot_ref, span_ref, recv_ref,
-    *refs,
-    half, nseg, heads, hdim, steps, dp_count, sort
+    vec_in, *refs,
+    half, nseg, heads, hdim, steps, dp_count, sort, row
 ):
     pgo_ref, vec_ref, keep_ref, send_ref, sg_ref, sgt_ref, mapg_ref, pg_ref, lhs_ref, tmp_ref = refs[-10:]
     step = pl.program_id(0)
@@ -467,7 +531,7 @@
 
     @pl.when(step == 0)
     def _():
-        vec_ref[...] = jnp.zeros_like(vec_ref)
+        vec_ref[...] = vec_in[...]
         put_states(own_ref, tot_ref, span_ref, recv_ref, sg_ref, sgt_ref, here, nseg, heads, hdim)
         map_back(map_ref, mapg_ref, heads, hdim)
 
@@ -497,8 +561,8 @@
             pg_ref[mine, v_cols] = fold_pair(folded, low_half, hdim).astype(bf16)
         grads = pg_ref[mine, :]
         pgo_ref[...] = grads
-        add_row(vec_ref, 1, grads[:, :width].astype(f32))
-        add_row(vec_ref, 2, grads[:, width:].astype(f32))
+        add_row(vec_ref, row + 1, grads[:, :width].astype(f32))
+        add_row(vec_ref, row + 2, grads[:, width:].astype(f32))
         put_transposed(lhs_ref, tmp_ref, tok_ref[...], at, row_sources(dp_count) if sort else [])
 
     weight_parts(step, steps, lhs_ref, pg_ref, keep_ref, send_ref, width)
@@ -506,8 +570,8 @@
 
 def query_back(
     len_ref, q_ref, num_ref, dgm_ref, tok_ref, map_ref, own_ref, tot_ref, span_ref, recv_ref,
-    *refs,
-    half, nseg, heads, hdim, steps, dp_count, sort
+    vec_in, *refs,
+    half, nseg, heads, hdim, steps, dp_count, sort, row
 ):
     pgo_ref, vec_ref, keep_ref, send_ref, st_ref, totp_ref, mapg_ref, pg_ref, lhs_ref, tmp_ref = refs[-10:]
     step = pl.program_id(0)
@@ -520,7 +584,7 @@
 
     @pl.when(step == 0)
     def _():
-        vec_ref[...] = jnp.zeros_like(vec_ref)
+        vec_ref[...] = vec_in[...]
         put_states(own_ref, tot_ref, span_ref, recv_ref, st_ref, totp_ref, spanning(ends, half), nseg, heads, hdim)
         map_back(map_ref, mapg_ref, heads, hdim)
 
@@ -550,7 +614,7 @@
             pg_ref[mine, cols] = rows_grad(logs, mapg_ref[p], q_pair, factor)
         grads = pg_ref[mine, :]
         pgo_ref[...] = grads
-        add_row(vec_ref, 0, grads.astype(f32))
+        add_row(vec_ref, row, grads.astype(f32))
         put_transposed(lhs_ref, tmp_ref, tok_ref[...], at, row_sources(dp_count) if sort else [])
 
     weight_parts(step, steps, lhs_ref, pg_ref, keep_ref, send_ref, width)
@@ -704,10 +768,11 @@
     assert 2 * hdim == 128 and wide == 256 and 8 * heads <= 128
     sort = (width // dp_count) % 16 == 0
     layout = dict(dp_count=dp_count, sort=sort)
-    wq, wk, wv = (qkv_weight[:, c, :] for c in range(3))
+    by_part = qkv_weight.transpose(1, 0, 2)
     rows = min(256, half)
     steps = half // rows
     big = min(512, half)
+    big_steps = half // big
     span_rows = heads * hdim + 16
     state_shapes = [
         sds((heads * wide, feat), bf16), sds((heads * 8, feat), f32),
@@ -718,6 +783,7 @@
     acc = pltpu.VMEM((heads, wide + 16, feat), f32)
     features = whole(feature_map.shape)
     square = whole((width, width))
+    w_specs = [pl.BlockSpec((None, width, width), lambda i, c=c: (c, 0, 0), pipeline_mode=pl.Buffered(1)) for c in range(3)]
 
     def tile(cols):
         return pl.BlockSpec((rows, cols), lambda i: (jnp.minimum(i, steps - 1), 0))
@@ -746,28 +812,29 @@
         functools.partial(forward_keys, **static),
         name="key_states",
         grid=(steps,),
-        in_specs=[lens, tile(width), square, square, whole((3, width)), features],
+        in_specs=[lens, tile(width), w_specs[1], w_specs[2], whole((3, width)), features],
         out_specs=[tile(2 * width)] + state_specs,
         out_shape=[sds((half, 2 * width), bf16)] + state_shapes,
         scratch_shapes=[acc],
         **params(12),
-    )(lengths, tokens, wk, wv, qkv_bias, feature_map)
+    )(lengths, tokens, by_part, by_part, qkv_bias, feature_map)
     recv = exchange(send, 1, dp_count)
     q_rows, q_feats = pl.pallas_call(
         functools.partial(forward_queries, heads=heads, hdim=hdim),
         name="query_features",
         grid=(steps,),
-        in_specs=[tile(width), square, whole((3, width)), features],
+        in_specs=[tile(width), w_specs[0], whole((3, width)), features],
         out_specs=[tile(width), tile(heads * feat)],
         out_shape=[sds((half, width), bf16), sds((half, heads * feat), bf16)],
         **params(7),
-    )(tokens, wq, qkv_bias, feature_map)
+    )(tokens, by_part, qkv_bias, feature_map)
 
     chunk = 512
     count = hidden_units // chunk
     half_w, half_u = width // 2, hidden_units // 2
-    vec_rows = 6 + hidden_units // width
-    vec_rows += -vec_rows % 8
+    sum_at = 6 + hidden_units // width
+    vec_rows = 16
+    assert sum_at + 3 <= vec_rows and 2 * vec_rows * width // 128 == width // 4
 
     def tiles(cols, size, before):
         per = cols // size
@@ -779,16 +846,19 @@
         shape = sds((2, 2, cols // 128, width // 4, 128), bf16)
         return [pl.BlockSpec((2, 1, size // 128, width // 4, 128), at)] * 2, [shape] * 2
 
-    d_specs, d_shapes = tiles(half_u, chunk, steps)
-    u_specs, u_shapes = tiles(half_u, chunk, steps + count)
-    o_specs, o_shapes = tiles(half_w, half_w, steps + 2 * count)
+    d_specs, d_shapes = tiles(half_u, chunk, big_steps)
     hbm = pl.BlockSpec(memory_space=pl.ANY)
-    (output, agrad, num_grad, den_m, vec_1, s_own, s_tot, s_span, s_send, d_keep, d_send, u_keep, u_send, o_keep, o_send) = run(
-        functools.partial(chain, chunk=chunk, steps=steps, **layout, **static),
+
+    def big_tile(cols):
+        return pl.BlockSpec((big, cols), lambda i: (jnp.minimum(i, big_steps - 1), 0))
+
+    tile_cols = (width, width, width, 128, width, width)
+    (output, agrad, num_grad, den_m, normed, mixed, ugrad, vec, s_own, s_tot, s_span, s_send, d_keep, d_send) = run(
+        functools.partial(chain, chunk=chunk, steps=big_steps, **layout, **static),
         "chain",
-        (steps + 2 * count + 2,),
-        [lens, tile(width), tile(heads * feat), tile(width)]
-        + [whole(v.shape) for v in (own, tot, span, recv)]
+        (big_steps + count,),
+        [lens, big_tile(width), big_tile(heads * feat), big_tile(width)]
+        + [hbm] + [whole(v.shape) for v in (tot, span, recv)]
         + [square, vector(width), vector(width), vector(width)]
         + [hbm, vector(hidden_units), hbm]
         + [vector(width)] * 3,
@@ -797,30 +867,41 @@
             up_weight, up_bias, down_weight, down_bias, ln2_gain, ln2_shift,
         ),
         (),
-        out_specs=[tile(c) for c in (width, width, width, 128)] + [resident((vec_rows, width))] + state_specs + d_specs + u_specs + o_specs,
-        out_shape=[sds((half, c), bf16) for c in (width, width, width, 128)]
-        + [sds((vec_rows, width), f32)]
-        + state_shapes + d_shapes + u_shapes + o_shapes,
+        out_specs=[big_tile(c) for c in tile_cols] + [hbm, whole((vec_rows, width))] + [whole(v.shape) for v in state_shapes] + d_specs,
+        out_shape=[sds((half, c), bf16) for c in tile_cols + (hidden_units,)] + [sds((vec_rows, width), f32)] + state_shapes + d_shapes,
         scratch_shapes=[
             pltpu.VMEM((heads * wide, feat), bf16),
             pltpu.VMEM((128, heads * feat), bf16),
+            pltpu.VMEM((256, width + 128), bf16),
+            pltpu.VMEM((2 * width, 128), bf16),
             acc,
             pltpu.VMEM((half, hidden_units), bf16),
-            pltpu.VMEM((half, hidden_units), bf16),
-            pltpu.VMEM((half, width), bf16),
-            pltpu.VMEM((rows, hidden_units), bf16),
+            pltpu.VMEM((big, hidden_units), bf16),
             pltpu.VMEM((width, half), bf16),
-            pltpu.VMEM((width, half), bf16),
-            pltpu.VMEM((width, half), bf16),
-            pltpu.VMEM((width, rows), bf16),
+            pltpu.VMEM((width, big // 2), bf16),
             pltpu.VMEM(up_weight.shape, bf16),
             pltpu.VMEM(down_weight.shape, bf16),
-            pltpu.SemaphoreType.DMA((2,)),
+            pltpu.SemaphoreType.DMA((5,)),
         ],
-        **params(66),
+        **params(58),
     )
     s_recv = exchange(s_send, 1, dp_count)
     d_keep, d_got = over_core(d_keep, d_send)
+    u_specs, u_shapes = tiles(half_u, chunk, 0)
+    o_specs, o_shapes = tiles(half_w, half_w, count)
+    whole_rows = whole((half, width))
+    u_keep, u_send, o_keep, o_send = run(
+        functools.partial(up_out_grads, count=count, **layout),
+        "up_out_grads",
+        (count + 2,),
+        [whole_rows] * 3 + [pl.BlockSpec((half, chunk), lambda i: (0, jnp.minimum(i, count - 1)))],
+        (normed, agrad, mixed, ugrad),
+        (),
+        out_specs=u_specs + o_specs,
+        out_shape=u_shapes + o_shapes,
+        scratch_shapes=[pltpu.VMEM((width, half), bf16)] * 3,
+        **params(9),
+    )
     u_keep, u_got = over_core(u_keep, u_send)
     o_keep, o_got = over_core(o_keep, o_send)
     block = (width // 4, 128)
@@ -828,7 +909,7 @@
     d_l, uo_l, qkv_n, qkv_l = d_n // 2, (u_n + o_n) // 2, 3 * o_n, 3 * o_n // 2
     d_r, uo_r, qkv_r = d_n - d_l, u_n + o_n - uo_l, qkv_n - qkv_l
     pair = lambda n: (2, n) + block
-    d_lk, d_ls, d_rk, d_rs = route("down_1", [d_keep, d_got], [pair(d_l)] * 2 + [pair(d_r)] * 2, first_moves([(0, d_n)], d_l))
+    d_lk, d_ls, d_rk, d_rs = route("down_1", [d_keep, d_got], [pair(d_l)] * 2 + [pair(d_r)] * 2, first_moves([(0, d_n)], d_l), None, (u_keep, s_recv))
     x_got, y_got = exchange(d_ls, 1, dp_count), exchange(d_rs, 4, dp_count)
     rows = min(512, half)
     steps = half // rows
@@ -843,15 +924,17 @@
 
     q_specs, q_shapes = parts(half_w, steps, 1)
     state_scratch = [pltpu.VMEM((heads * wide, feat), bf16), pltpu.VMEM((128, heads * feat), bf16)]
-    pg_q, vec_2, q_keep, q_send = run(
-        functools.partial(query_back, steps=steps, **layout, **static),
+    sums = resident((vec_rows, width))
+    sums_shape = sds((vec_rows, width), f32)
+    pg_q, vec, q_keep, q_send = run(
+        functools.partial(query_back, steps=steps, row=sum_at, **layout, **static),
         "query_back",
         (steps + 2,),
-        [lens, tile(width), tile(width), tile(128), tile(width), features] + [whole(v.shape) for v in (own, tot, span, recv)],
-        (lengths, q_rows, num_grad, den_m, tokens, feature_map, own, tot, span, recv),
+        [lens, tile(width), tile(width), tile(128), tile(width), features] + [whole(v.shape) for v in (own, tot, span, recv)] + [sums],
+        (lengths, q_rows, num_grad, den_m, tokens, feature_map, own, tot, span, recv, vec),
         (d_lk,),
-        out_specs=[tile(width), resident((8, width))] + q_specs,
-        out_shape=[sds((half, width), bf16), sds((8, width), f32)] + q_shapes,
+        out_specs=[tile(width), sums] + q_specs,
+        out_shape=[sds((half, width), bf16), sums_shape] + q_shapes,
         scratch_shapes=state_scratch + back_scratch(1),
         **params(18),
     )
@@ -873,27 +956,35 @@
     x_got, y_got = exchange(x_send, 1, dp_count), exchange(y_send, 4, dp_count)
 
     kv_specs, kv_shapes = parts(2 * half_w, steps, 1)
-    pg_kv, vec_3, kv_keep, kv_send = run(
-        functools.partial(key_back, steps=steps, **layout, **static),
+    pg_kv, vec, kv_keep, kv_send = run(
+        functools.partial(key_back, steps=steps, row=sum_at, **layout, **static),
         "key_back",
         (steps + 2,),
-        [lens, tile(2 * width), tile(width), features] + [whole(v.shape) for v in (s_own, s_tot, s_span, s_recv)],
-        (lengths, kv, tokens, feature_map, s_own, s_tot, s_span, s_recv),
-        (d_part, vec_2),
-        out_specs=[tile(2 * width), resident((8, width))] + kv_specs,
-        out_shape=[sds((half, 2 * width), bf16), sds((8, width), f32)] + kv_shapes,
+        [lens, tile(2 * width), tile(width), features] + [whole(v.shape) for v in (s_own, s_tot, s_span, s_recv)] + [sums],
+        (lengths, kv, tokens, feature_map, s_own, s_tot, s_span, s_recv, vec),
+        (d_part,),
+        out_specs=[tile(2 * width), sums] + kv_specs,
+        out_shape=[sds((half, 2 * width), bf16), sums_shape] + kv_shapes,
         scratch_shapes=state_scratch + back_scratch(2),
         **params(18),
     )
     kv_keep, kv_got = over_core(kv_keep, kv_send)
-    up_rows = hidden_units // width
-    vec = jnp.concatenate([vec_1[: 6 + up_rows], (vec_2 + vec_3)[:3]], axis=0)
-    vec = jnp.pad(vec, ((0, -vec.shape[0] % 16), (0, 0)))
     vec_got = exchange(vec, 2, dp_count)
-    d_x, uo_x = x_got[:d_r], x_got[d_r:].reshape(pair(uo_l))
-    d_y, uo_y = y_got[:d_l], y_got[d_l:].reshape(pair(uo_r))
+    moves = []
+    for out, at, terms in second_moves(3, uo_l, uo_r, 0):
+        placed = []
+        for n, index in terms:
+            if n == 4:
+                n, index = 1, (d_r + index[0] * uo_l + index[1],)
+            elif n == 6:
+                n, index = 2, (d_l + index[0] * uo_r + index[1],)
+            elif n == 5:
+                n = 4
+            placed.append((n, index))
+        moves.append((out, at, placed))
+    d_x, d_y = x_got[:d_r], y_got[:d_l]
     uo_part, uo_ls, uo_rs = route(
-        "up_2", [uo_lk, uo_x, uo_rk, uo_y], [flat(uo_l + uo_r), flat(uo_l), flat(uo_r)], second_moves(0, uo_l, uo_r, 0)
+        "up_2", [d_part, x_got, y_got, uo_lk, uo_rk], [flat(uo_l + uo_r), flat(uo_l), flat(uo_r)], moves
     )
     x_got, y_got = exchange(uo_rs, 1, dp_count), exchange(uo_ls, 4, dp_count)
     z_bits = [8 << b for b in range((dp_count // 4).bit_length() - 1)]
@@ -916,7 +1007,7 @@
             for out, at, terms in first_moves([(0, o_n), (2, 2 * o_n)], qkv_l)
         ],
         (vec + vec_got, None, (1, (2 * qkv_l,))),
-        (uo_part, down_z[0]),
+        (uo_part,),
     )
     qkv_x, qkv_y = exchange(qkv_ls, 1, dp_count), exchange(qkv_rs, 4, dp_count)
 
@@ -924,9 +1015,9 @@
         token_grads,
         "token_grads",
         (steps,),
-        [tile(width), tile(width), tile(2 * width), square, square, square],
-        (agrad, pg_q, pg_kv, wq, wk, wv),
-        (qkv_lk,),
+        [tile(width), tile(width), tile(2 * width)] + w_specs,
+        (agrad, pg_q, pg_kv, by_part, by_part, by_part),
+        (qkv_lk, down_z[0]),
         out_specs=tile(width),
         out_shape=sds((half, width), bf16),
         **params(8),
@@ -983,13 +1074,13 @@
         output,
         grad_tokens,
         d_qkv,
-        vec[6 + up_rows : 9 + up_rows],
+        vec[sum_at : sum_at + 3],
         d_up_out[:, half_u:],
         vec[3],
         vec[4],
         vec[5],
         d_up_out[:, :half_u],
-        vec[6 : 6 + up_rows].reshape(-1),
+        vec[6:sum_at].reshape(-1),
         d_down,
         vec[0],
         vec[1],

time: 228 us -> 220 us (0.965)
  local copies, waits for them, and re-layouts: 16.4 us -> 9.71 us
  waiting for transfers between devices: 28.4 us -> 21.9 us
  Pallas kernels: 150 us -> 153 us
  starting transfers between devices: 23.6 us -> 26 us
    ppermute x24, waiting for transfers between devices: 28.4 us -> 21.9 us  [exchange(): lax.ppermute(values, every_axis, [(i, i ^ mask) for i in range(2 * dp_cou...]
    squeeze x1 -> x0, local copies, waits for them, and re-layouts: 3.81 us -> none  [body(): wq, wk, wv = (qkv_weight[:, c, :] for c in range(3))]
    pallas_call x4 -> x5, Pallas kernels: 114 us -> 116 us  [run(): pl.pallas_call(kernel, name=name, grid=grid, in_specs=list(in_specs) + fe...]
    ppermute x24, starting transfers between devices: 23.6 us -> 26 us  [exchange(): lax.ppermute(values, every_axis, [(i, i ^ mask) for i in range(2 * dp_cou...]
    unnamed x75 -> x65, local copies, waits for them, and re-layouts: 5.08 us -> 3.11 us
  transfers between devices with their start and end apart: 24 -> 24, of which waited for: 10 -> 9; matrix products, arithmetic and copies ran while one was open for 4% -> 4% of each run, Pallas kernels for 30% -> 36%
where the time goes in v3:
time: 220 us; the launch traced here: 216 us
  Pallas kernels  153 us (70%)
  starting transfers between devices  26 us (12%)
  waiting for transfers between devices  21.9 us (10%)
  local copies, waits for them, and re-layouts  9.71 us (4%)
  other arithmetic  3.83 us (2%)
    pallas_call x5, Pallas kernels, run(): pl.pallas_call(kernel, name=name, grid=grid, in_specs=list(in_specs) + fe...  116 us
    ppermute x24, starting transfers between devices, exchange(): lax.ppermute(values, every_axis, [(i, i ^ mask) for i in range(2 * dp_cou...  26 us
    ppermute x24, waiting for transfers between devices, exchange(): lax.ppermute(values, every_axis, [(i, i ^ mask) for i in range(2 * dp_cou...  21.9 us
    pallas_call x5, Pallas kernels, route(): pl.pallas_call(kernel, name=name, grid=(grid,), in_specs=[spec(a.shape) f...  17.9 us
    pallas_call x1, Pallas kernels, body(): pl.pallas_call(functools.partial(forward_keys, **static), name='key_state...  11.9 us
    pallas_call x1, Pallas kernels, body(): pl.pallas_call(functools.partial(forward_queries, heads=heads, hdim=hdim)...  7.41 us
  transfers between devices with their start and end apart: 24, of which 9 were waited for; matrix products, arithmetic and copies ran while one was open for 4% of the time, Pallas kernels for 36%

profile of v3, /device:TPU:0, one launch (start us, length us, event | category | flops | bytes accessed | tf_op | source)
XLA Modules:
  0.0 216.2 jit_solution(18423900179786847383)
XLA Ops:
  0.6 11.9 %key_states.1 = (bf16[1024,1536]{1,0:T(8,128)(2,1)}, bf16[3072,256]{1,0:T(8,128)(2,1)}, f32[96,256]{1,0:T(8,128)}, f32[768,256]{1,0:T(8,128)}, bf16[784,256]{1,0:T(8,128)(2,1)}) custom-call(s32[1,4]{1,0:T(1,128)} %len_ref.7, bf16[1024,768]{1,0:T(8,128)(2,1)} %tok_ref.9, bf16[3,768,768]{2,1,0:T(8,128)(2,1)} %bitcast.114, bf16[3,768,768]{2,1,0:T(8,128)(2,1)} %bitcast.115, ...), custom_call_target="tpu_custom_call" | custom-call | flops 13200000000 | bytes 12000000 | tf_op jit(solution)/shard_map/key_states/pallas_call | solution.py:811
  12.5 3.0 %collective-permute-start = (bf16[784,256]{1,0:T(8,128)(2,1)}, bf16[784,256]{1,0:T(8,128)(2,1)S(1)}, u32[]{:S(2)}, u32[]{:S(2)}) collective-permute-start(bf16[784,256]{1,0:T(8,128)(2,1)} %get-tuple-element.72), channel_id=1, source_target_pairs={{0,1},{1,0},{2,3},{3,2},{4,5},{5,4},{6,7},{7,6},{8,9},{9,8},{10,11... | collective-permute-start | bytes 1204232 | tf_op jit(solution)/shard_map/ppermute | solution.py:654
  15.5 7.4 %query_features.1 = (bf16[1024,768]{1,0:T(8,128)(2,1)}, bf16[1024,3072]{1,0:T(8,128)(2,1)}) custom-call(bf16[1024,768]{1,0:T(8,128)(2,1)} %tok_ref.9, bf16[3,768,768]{2,1,0:T(8,128)(2,1)} %bitcast.116, f32[3,768]{1,0:T(4,128)} %b_ref.3, bf16[12,64,256]{2,1,0:T(8,128)(2,1)} %map_ref.7), custom_call_target="tpu_custom_call" | custom-call | flops 7699999744 | bytes 7000000 | tf_op jit(solution)/shard_map/query_features/pallas_call | solution.py:822
  22.9 2.1 collective-permute-done.recv_ref
  25.8 58.9 %chain.1 = (bf16[1024,768]{1,0:T(8,128)(2,1)}, bf16[1024,768]{1,0:T(8,128)(2,1)}, bf16[1024,768]{1,0:T(8,128)(2,1)}, bf16[1024,128]{1,0:T(8,128)(2,1)}, bf16[102...) custom-call(s32[1,4]{1,0:T(1,128)} %len_ref.7, ...), custom_call_target="tpu_custom_call" | custom-call | flops 63800000512 | bytes 58000000 | tf_op jit(solution)/shard_map/chain/pallas_call | solution.py:804
  84.8 1.8 collective-permute-start.2
  86.6 14.5 %up_out_grads.1 = (bf16[2,2,12,192,128]{4,3,2,1,0:T(8,128)(2,1)}, bf16[2,2,12,192,128]{4,3,2,1,0:T(8,128)(2,1)}, bf16[2,2,3,192,128]{4,3,2,1,0:T(8,128)(2,1)}, bf16[2,2,3,192,128]{4,3,2,1,0:T(8,128)(2,1)}) custom-call(bf16[1024,768]{1,0:T(8,128)(2,1)} %get-tuple-element.81.normed_ref, bf16[1024,768]{1,0:T(8,128)(2,1)} %get-tuple-element.74.agrad_ref, ...), custom_call_target="tpu_custom_call" | custom-call | flops 9900000256 | bytes 9000000 | tf_op jit(solution)/shard_map/up_out_grads/pallas_call | solution.py:804
  102.4 3.7 %down_1.1 = (bf16[2,6,192,128]{3,2,1,0:T(8,128)(2,1)}, bf16[2,6,192,128]{3,2,1,0:T(8,128)(2,1)}, bf16[2,6,192,128]{3,2,1,0:T(8,128)(2,1)}, bf16[2,6,192,128]{3,2,1,0:T(8,128)(2,1)}) custom-call(bf16[2,2,12,192,128]{4,3,2,1,0:T(8,128)(2,1)} %get-tuple-element.79.refs_0_, bf16[2,2,12,192,128]{4,3,2,1,0:T(8,128)(2,1)} %collective-permute-done.1.refs_1_, ...), custom_call_target="tpu_custom_call" | custom-call | flops 3300000000 | bytes 3000000 | tf_op jit(solution)/shard_map/down_1/pallas_call | solution.py:708
  106.4 1.8 collective-permute-start.4
  108.1 16.5 %query_back.1 = (bf16[1024,768]{1,0:T(8,128)(2,1)}, f32[16,768]{1,0:T(8,128)}, bf16[2,2,3,192,128]{4,3,2,1,0:T(8,128)(2,1)}, bf16[2,2,3,192,128]{4,3,2,1,0:T(8,128)(2,1)}) custom-call(s32[1,4]{1,0:T(1,128)} %len_ref.7, bf16[1024,768]{1,0:T(8,128)(2,1)} %get-tuple-element.75.q_ref, bf16[1024,768]{1,0:T(8,128)(2,1)} %get-tuple-element.76.num_ref, ...), custom_call_target="tpu_custom_call" | custom-call | flops 19800000512 | bytes 18000000 | tf_op jit(solution)/shard_map/query_back/pallas_call | solution.py:804
  125.8 5.3 %down_2_up_1.1 = (bf16[12,192,128]{2,1,0:T(8,128)(2,1)}, bf16[2,7,192,128]{3,2,1,0:T(8,128)(2,1)}, bf16[2,8,192,128]{3,2,1,0:T(8,128)(2,1)}, bf16[20,192,128]{2,1,0:T(8,128)(2,1)}, bf16[22,192,128]{2,1,0:T(8,128)(2,1)}) custom-call(bf16[2,6,192,128]{3,2,1,0:T(8,128)(2,1)} %get-tuple-element.86.refs_0_, bf16[2,6,192,128]{3,2,1,0:T(8,128)(2,1)} %copy-done.8, ...), custom_call_target="tpu_custom_call" | custom-call | flops 3300000000 | bytes 3000000 | tf_op jit(solution)/shard_map/down_2_up_1/pallas_call | solution.py:708
  131.0 1.6 collective-permute-start.10
  133.1 18.1 %key_back.1 = (bf16[1024,1536]{1,0:T(8,128)(2,1)}, f32[16,768]{1,0:T(8,128)}, bf16[2,2,6,192,128]{4,3,2,1,0:T(8,128)(2,1)}, bf16[2,2,6,192,128]{4,3,2,1,0:T(8,128)(2,1)}) custom-call(s32[1,4]{1,0:T(1,128)} %len_ref.7, bf16[1024,1536]{1,0:T(8,128)(2,1)} %get-tuple-element.88.kv_ref, bf16[1024,768]{1,0:T(8,128)(2,1)} %tok_ref.9, bf16[12,64,256]{2,1,0:T(8,128)(2,1)} %map_ref.7, ...), custom_call_target="tpu_custom_call" | custom-call | flops 19800000512 | bytes 18000000 | tf_op jit(solution)/shard_map/key_back/pallas_call | solution.py:804
  151.9 2.2 %collective-permute-done.9 = f32[16,768]{1,0:T(8,128)S(1)} collective-permute-done((f32[16,768]{1,0:T(8,128)}, f32[16,768]{1,0:T(8,128)S(1)}, u32[]{:S(2)}, u32[]{:S(2)}) %collective-permute-start.9) | collective-permute-done | bytes 49184 | tf_op jit(solution)/shard_map/ppermute | solution.py:654
  154.1 1.4 add.57.refs_4_
  155.6 2.5 %collective-permute-done.11.refs_2_ = bf16[22,192,128]{2,1,0:T(8,128)(2,1)} collective-permute-done((bf16[22,192,128]{2,1,0:T(8,128)(2,1)}, bf16[22,192,128]{2,1,0:T(8,128)(2,1)}, u32[]{:S(2)}, u32[]{:S(2)}) %collective-permute-start.11) | collective-permute-done | bytes 1081376 | tf_op jit(solution)/shard_map/ppermute | solution.py:654
  160.0 1.6 collective-permute-start.16
  161.5 3.2 %up_2.1 = (bf16[15,192,128]{2,1,0:T(8,128)(2,1)}, bf16[7,192,128]{2,1,0:T(8,128)(2,1)}, bf16[8,192,128]{2,1,0:T(8,128)(2,1)}) custom-call(bf16[12,192,128]{2,1,0:T(8,128)(2,1)} %get-tuple-element.99.refs_0_, bf16[20,192,128]{2,1,0:T(8,128)(2,1)} %copy-done.5, bf16[22,192,128]{2,1,0:T(8,128)(2,1)} %collective-permute-done.11.refs_2_, ...), custom_call_target="tpu_custom_call" | custom-call | flops 3300000000 | bytes 3000000 | tf_op jit(solution)/shard_map/up_2/pallas_call | solution.py:708
  165.8 3.2 %qkv_1.1 = (bf16[2,4,192,128]{3,2,1,0:T(8,128)(2,1)}, bf16[9,192,128]{2,1,0:T(8,128)(2,1)}, bf16[2,5,192,128]{3,2,1,0:T(8,128)(2,1)}, bf16[2,5,192,128]{3,2,1,0:T(8,128)(2,1)}, f32[16,768]{1,0:T(8,128)}) custom-call(bf16[2,2,3,192,128]{4,3,2,1,0:T(8,128)(2,1)} %get-tuple-element.101.refs_0_, bf16[2,2,3,192,128]{4,3,2,1,0:T(8,128)(2,1)} %collective-permute-done.7.refs_1_, ...), custom_call_target="tpu_custom_call" | custom-call | flops 3300000000 | bytes 3000000 | tf_op jit(solution)/shard_map/qkv_1/pallas_call | solution.py:708
  169.0 1.6 collective-permute-start.12
  170.6 1.5 collective-permute-start.13
  172.1 8.2 %token_grads.1.refs_7_ = bf16[1024,768]{1,0:T(8,128)(2,1)} custom-call(bf16[1024,768]{1,0:T(8,128)(2,1)} %get-tuple-element.74.agrad_ref, bf16[1024,768]{1,0:T(8,128)(2,1)} %get-tuple-element.87.pgq_ref, bf16[1024,1536]{1,0:T(8,128)(2,1)} %get-tuple-element.100.pgkv_ref, bf16[3,768,768]{2,1,0:T(8,128)(2,1)} %bitcast.117, bf16[3,768,768]{2,1,0:T(8,128)(2,1)} %bitcast.118, ...), custom_call_target="tpu_custom_call" | custom-call | flops 8800000000 | bytes 8000000 | tf_op jit(solution)/shard_map/token_grads/pallas_call | solution.py:804
  181.1 2.6 %collective-permute-start.23 = (bf16[12,48,128]{2,1,0:T(8,128)(2,1)S(1)}, bf16[12,48,128]{2,1,0:T(8,128)(2,1)S(1)}, u32[]{:S(2)}, u32[]{:S(2)}) collective-permute-start(bf16[12,48,128]{2,1,0:T(8,128)(2,1)S(1)} %get-tuple-element.142), channel_id=1, source_target_pairs={{0,16},{1,17},{2,18},{3,19},{4,20},{5,21},{6,22},{7,23},{8,24},{9,... | collective-permute-start | bytes 442376 | tf_op jit(solution)/shard_map/ppermute | solution.py:654
  185.2 2.5 %qkv_2.1 = (bf16[9,192,128]{2,1,0:T(8,128)(2,1)}, bf16[5,192,128]{2,1,0:T(8,128)(2,1)}, bf16[5,192,128]{2,1,0:T(8,128)(2,1)}, f32[16,768]{1,0:T(8,128)}) custom-call(bf16[2,4,192,128]{3,2,1,0:T(8,128)(2,1)} %get-tuple-element.111.refs_0_, bf16[9,192,128]{2,1,0:T(8,128)(2,1)} %collective-permute-done.12.refs_1_, ...), custom_call_target="tpu_custom_call" | custom-call | flops 3300000000 | bytes 3000000 | tf_op jit(solution)/shard_map/qkv_2/pallas_call | solution.py:708
  190.0 4.1 %collective-permute-done.17 = bf16[5,192,128]{2,1,0:T(8,128)(2,1)S(1)} collective-permute-done((bf16[5,192,128]{2,1,0:T(8,128)(2,1)}, bf16[5,192,128]{2,1,0:T(8,128)(2,1)S(1)}, u32[]{:S(2)}, u32[]{:S(2)}) %collective-permute-start.17) | collective-permute-done | bytes 245792 | tf_op jit(solution)/shard_map/ppermute | solution.py:654
  194.3 1.6 collective-permute-done.18
  196.3 1.1 collective-permute-start.19
  197.7 1.6 collective-permute-start.22
  199.3 4.6 %collective-permute-done.19 = bf16[1056,128]{1,0:T(8,128)(2,1)S(1)} collective-permute-done((bf16[1056,128]{1,0:T(8,128)(2,1)S(1)}, bf16[1056,128]{1,0:T(8,128)(2,1)S(1)}, u32[]{:S(2)}, u32[]{:S(2)}) %collective-permute-start.19) | collective-permute-done | bytes 270368 | tf_op jit(solution)/shard_map/ppermute | solution.py:654
  204.3 3.3 %collective-permute-start.20 = (bf16[624,128]{1,0:T(8,128)(2,1)S(1)}, bf16[624,128]{1,0:T(8,128)(2,1)S(1)}, u32[]{:S(2)}, u32[]{:S(2)}) collective-permute-start(bf16[624,128]{1,0:T(8,128)(2,1)S(1)} %constant_dynamic-update-slice_fusion.25), channel_id=1, source_target_pairs={{0,16},{1,17},{2,18},{3,19},{4,20},{5,21},{6,22},{7,23},{8,24},{9,... | collective-permute-start | bytes 479240 | tf_op jit(solution)/shard_map/ppermute | solution.py:654
  207.6 1.9 collective-permute-done.22
  211.0 2.3 %collective-permute-done.20 = bf16[624,128]{1,0:T(8,128)(2,1)S(1)} collective-permute-done((bf16[624,128]{1,0:T(8,128)(2,1)S(1)}, bf16[624,128]{1,0:T(8,128)(2,1)S(1)}, u32[]{:S(2)}, u32[]{:S(2)}) %collective-permute-start.20) | collective-permute-done | bytes 159776 | tf_op jit(solution)/shard_map/ppermute | solution.py:654
  (134 shorter events, 17.2 us)
Async XLA Ops:
  12.5 12.5 %collective-permute-start = (bf16[784,256]{1,0:T(8,128)(2,1)}, bf16[784,256]{1,0:T(8,128)(2,1)S(1)}, u32[]{:S(2)}, u32[]{:S(2)}) collective-permute-start(bf16[784,256]{1,0:T(8,128)(2,1)} %get-tuple-element.72), channel_id=1, source_target_pairs={{0,1},{1,0},{2,3},{3,2},{4,5},{5,4},{6,7},{7,6},{8,9},{9,8},{10,11... | collective-permute-start | bytes 1204232 | tf_op jit(solution)/shard_map/ppermute | solution.py:654
  84.7 16.9 %collective-permute-start.1 = (bf16[2,2,12,192,128]{4,3,2,1,0:T(8,128)(2,1)}, bf16[2,2,12,192,128]{4,3,2,1,0:T(8,128)(2,1)}, u32[]{:S(2)}, u32[]{:S(2)}) collective-permute-start(bf16[2,2,12,192,128]{4,3,2,1,0:T(8,128)(2,1)} %get-tuple-element.80), channel_id=1, source_target_pairs={{0,2},{1,3},{2,0},{3,1},{4,6},{5,7},{6,4},{7,5},{8,10},{9,11},{10,... | collective-permute-start | bytes 7077896 | tf_op jit(solution)/shard_map/ppermute | solution.py:654
  84.8 16.9 %collective-permute-start.2 = (bf16[784,256]{1,0:T(8,128)(2,1)}, bf16[784,256]{1,0:T(8,128)(2,1)S(1)}, u32[]{:S(2)}, u32[]{:S(2)}) collective-permute-start(bf16[784,256]{1,0:T(8,128)(2,1)} %get-tuple-element.85), channel_id=1, source_target_pairs={{0,1},{1,0},{2,3},{3,2},{4,5},{5,4},{6,7},{7,6},{8,9},{9,8},{10,11... | collective-permute-start | bytes 1204232 | tf_op jit(solution)/shard_map/ppermute | solution.py:654
  101.1 23.5 %collective-permute-start.5 = (bf16[2,2,12,192,128]{4,3,2,1,0:T(8,128)(2,1)}, bf16[2,2,12,192,128]{4,3,2,1,0:T(8,128)(2,1)}, u32[]{:S(2)}, u32[]{:S(2)}) collective-permute-start(bf16[2,2,12,192,128]{4,3,2,1,0:T(8,128)(2,1)} %get-tuple-element.96), channel_id=1, source_target_pairs={{0,2},{1,3},{2,0},{3,1},{4,6},{5,7},{6,4},{7,5},{8,10},{9,11},{10,... | collective-permute-start | bytes 7077896 | tf_op jit(solution)/shard_map/ppermute | solution.py:654
  101.3 23.3 %collective-permute-start.6 = (bf16[2,2,3,192,128]{4,3,2,1,0:T(8,128)(2,1)}, bf16[2,2,3,192,128]{4,3,2,1,0:T(8,128)(2,1)S(1)}, u32[]{:S(2)}, u32[]{:S(2)}) collective-permute-start(bf16[2,2,3,192,128]{4,3,2,1,0:T(8,128)(2,1)} %get-tuple-element.98), channel_id=1, source_target_pairs={{0,2},{1,3},{2,0},{3,1},{4,6},{5,7},{6,4},{7,5},{8,10},{9,11},{10,... | collective-permute-start | bytes 1769480 | tf_op jit(solution)/shard_map/ppermute | solution.py:654
  106.1 18.5 %collective-permute-start.3 = (bf16[2,6,192,128]{3,2,1,0:T(8,128)(2,1)}, bf16[2,6,192,128]{3,2,1,0:T(8,128)(2,1)S(1)}, u32[]{:S(2)}, u32[]{:S(2)}) collective-permute-start(bf16[2,6,192,128]{3,2,1,0:T(8,128)(2,1)} %get-tuple-element.93), channel_id=1, source_target_pairs={{0,1},{1,0},{2,3},{3,2},{4,5},{5,4},{6,7},{7,6},{8,9},{9,8},{10,11... | collective-permute-start | bytes 1769480 | tf_op jit(solution)/shard_map/ppermute | solution.py:654
  106.4 18.3 %collective-permute-start.4 = (bf16[2,6,192,128]{3,2,1,0:T(8,128)(2,1)}, bf16[2,6,192,128]{3,2,1,0:T(8,128)(2,1)S(1)}, u32[]{:S(2)}, u32[]{:S(2)}) collective-permute-start(bf16[2,6,192,128]{3,2,1,0:T(8,128)(2,1)} %get-tuple-element.95), channel_id=1, source_target_pairs={{0,4},{1,5},{2,6},{3,7},{4,0},{5,1},{6,2},{7,3},{8,12},{9,13},{10,... | collective-permute-start | bytes 1769480 | tf_op jit(solution)/shard_map/ppermute | solution.py:654
  124.6 1.1 copy-start.9
  131.0 24.5 %collective-permute-start.10 = (bf16[20,192,128]{2,1,0:T(8,128)(2,1)}, bf16[20,192,128]{2,1,0:T(8,128)(2,1)S(1)}, u32[]{:S(2)}, u32[]{:S(2)}) collective-permute-start(bf16[20,192,128]{2,1,0:T(8,128)(2,1)} %get-tuple-element.106), channel_id=1, source_target_pairs={{0,1},{1,0},{2,3},{3,2},{4,5},{5,4},{6,7},{7,6},{8,9},{9,8},{10,11... | collective-permute-start | bytes 2949128 | tf_op jit(solution)/shard_map/ppermute | solution.py:654
  132.6 25.4 %collective-permute-start.11 = (bf16[22,192,128]{2,1,0:T(8,128)(2,1)}, bf16[22,192,128]{2,1,0:T(8,128)(2,1)}, u32[]{:S(2)}, u32[]{:S(2)}) collective-permute-start(bf16[22,192,128]{2,1,0:T(8,128)(2,1)} %get-tuple-element.107), channel_id=1, source_target_pairs={{0,4},{1,5},{2,6},{3,7},{4,0},{5,1},{6,2},{7,3},{8,12},{9,13},{10,... | collective-permute-start | bytes 3244040 | tf_op jit(solution)/shard_map/ppermute | solution.py:654
  151.2 7.8 %copy-start.3 = (bf16[12,192,128]{2,1,0:T(8,128)(2,1)S(1)}, bf16[12,192,128]{2,1,0:T(8,128)(2,1)}, u32[]{:S(2)}) copy-start(bf16[12,192,128]{2,1,0:T(8,128)(2,1)} %get-tuple-element.99.refs_0_) | copy-start | bytes 1769476
  151.2 14.5 %collective-permute-start.8 = (bf16[2,2,6,192,128]{4,3,2,1,0:T(8,128)(2,1)}, bf16[2,2,6,192,128]{4,3,2,1,0:T(8,128)(2,1)}, u32[]{:S(2)}, u32[]{:S(2)}) collective-permute-start(bf16[2,2,6,192,128]{4,3,2,1,0:T(8,128)(2,1)} %get-tuple-element.104), channel_id=1, source_target_pairs={{0,2},{1,3},{2,0},{3,1},{4,6},{5,7},{6,4},{7,5},{8,10},{9,11},{10,... | collective-permute-start | bytes 3538952 | tf_op jit(solution)/shard_map/ppermute | solution.py:654
  151.3 2.8 %collective-permute-start.9 = (f32[16,768]{1,0:T(8,128)}, f32[16,768]{1,0:T(8,128)S(1)}, u32[]{:S(2)}, u32[]{:S(2)}) collective-permute-start(f32[16,768]{1,0:T(8,128)} %get-tuple-element.105), channel_id=1, source_target_pairs={{0,2},{1,3},{2,0},{3,1},{4,6},{5,7},{6,4},{7,5},{8,10},{9,11},{10,... | collective-permute-start | bytes 147464 | tf_op jit(solution)/shard_map/ppermute | solution.py:654
  151.8 14.0 %collective-permute-start.7 = (bf16[2,2,3,192,128]{4,3,2,1,0:T(8,128)(2,1)}, bf16[2,2,3,192,128]{4,3,2,1,0:T(8,128)(2,1)}, u32[]{:S(2)}, u32[]{:S(2)}) collective-permute-start(bf16[2,2,3,192,128]{4,3,2,1,0:T(8,128)(2,1)} %get-tuple-element.102), channel_id=1, source_target_pairs={{0,2},{1,3},{2,0},{3,1},{4,6},{5,7},{6,4},{7,5},{8,10},{9,11},{10,... | collective-permute-start | bytes 1769480 | tf_op jit(solution)/shard_map/ppermute | solution.py:654
  155.6 4.4 %copy-start.5 = (bf16[20,192,128]{2,1,0:T(8,128)(2,1)}, bf16[20,192,128]{2,1,0:T(8,128)(2,1)S(1)}, u32[]{:S(2)}) copy-start(bf16[20,192,128]{2,1,0:T(8,128)(2,1)S(1)} %collective-permute-done.10.refs_1_) | copy-start | bytes 2949124
  160.0 20.3 %collective-permute-start.16 = (bf16[12,96,128]{2,1,0:T(8,128)(2,1)S(1)}, bf16[12,96,128]{2,1,0:T(8,128)(2,1)S(1)}, u32[]{:S(2)}, u32[]{:S(2)}) collective-permute-start(bf16[12,96,128]{2,1,0:T(8,128)(2,1)S(1)} %bitcast.112), channel_id=1, source_target_pairs={{0,8},{1,9},{2,10},{3,11},{4,12},{5,13},{6,14},{7,15},{8,0},{9,1},... | collective-permute-start | bytes 884744 | tf_op jit(solution)/shard_map/ppermute | solution.py:654
  164.8 18.9 %collective-permute-start.14 = (bf16[7,192,128]{2,1,0:T(8,128)(2,1)}, bf16[7,192,128]{2,1,0:T(8,128)(2,1)S(1)}, u32[]{:S(2)}, u32[]{:S(2)}) collective-permute-start(bf16[7,192,128]{2,1,0:T(8,128)(2,1)} %get-tuple-element.116), channel_id=1, source_target_pairs={{0,4},{1,5},{2,6},{3,7},{4,0},{5,1},{6,2},{7,3},{8,12},{9,13},{10,... | collective-permute-start | bytes 1032200 | tf_op jit(solution)/shard_map/ppermute | solution.py:654
  165.3 18.4 %collective-permute-start.15 = (bf16[8,192,128]{2,1,0:T(8,128)(2,1)}, bf16[8,192,128]{2,1,0:T(8,128)(2,1)S(1)}, u32[]{:S(2)}, u32[]{:S(2)}) collective-permute-start(bf16[8,192,128]{2,1,0:T(8,128)(2,1)} %get-tuple-element.117), channel_id=1, source_target_pairs={{0,1},{1,0},{2,3},{3,2},{4,5},{5,4},{6,7},{7,6},{8,9},{9,8},{10,11... | collective-permute-start | bytes 1179656 | tf_op jit(solution)/shard_map/ppermute | solution.py:654
  169.0 16.2 %collective-permute-start.12 = (bf16[9,192,128]{2,1,0:T(8,128)(2,1)}, bf16[9,192,128]{2,1,0:T(8,128)(2,1)}, u32[]{:S(2)}, u32[]{:S(2)}) collective-permute-start(bf16[9,192,128]{2,1,0:T(8,128)(2,1)} %get-tuple-element.112), channel_id=1, source_target_pairs={{0,1},{1,0},{2,3},{3,2},{4,5},{5,4},{6,7},{7,6},{8,9},{9,8},{10,11... | collective-permute-start | bytes 1327112 | tf_op jit(solution)/shard_map/ppermute | solution.py:654
  170.6 14.6 %collective-permute-start.13 = (bf16[2,5,192,128]{3,2,1,0:T(8,128)(2,1)}, bf16[2,5,192,128]{3,2,1,0:T(8,128)(2,1)}, u32[]{:S(2)}, u32[]{:S(2)}) collective-permute-start(bf16[2,5,192,128]{3,2,1,0:T(8,128)(2,1)} %get-tuple-element.114), channel_id=1, source_target_pairs={{0,4},{1,5},{2,6},{3,7},{4,0},{5,1},{6,2},{7,3},{8,12},{9,13},{10,... | collective-permute-start | bytes 1474568 | tf_op jit(solution)/shard_map/ppermute | solution.py:654
  172.1 8.2 %copy-start.1 = (bf16[12,2,1,48,128]{4,3,2,1,0:T(8,128)(2,1)S(1)}, bf16[12,2,1,48,128]{4,3,2,1,0:T(8,128)(2,1)}, u32[]{:S(2)}) copy-start(bf16[12,2,1,48,128]{4,3,2,1,0:T(8,128)(2,1)} %get-tuple-element.137) | copy-start | bytes 884740
  180.3 3.4 %copy-start.2 = (bf16[15,192,128]{2,1,0:T(8,128)(2,1)S(1)}, bf16[15,192,128]{2,1,0:T(8,128)(2,1)}, u32[]{:S(2)}) copy-start(bf16[15,192,128]{2,1,0:T(8,128)(2,1)} %get-tuple-element.110.refs_5_) | copy-start | bytes 2211844
  181.1 7.7 %collective-permute-start.23 = (bf16[12,48,128]{2,1,0:T(8,128)(2,1)S(1)}, bf16[12,48,128]{2,1,0:T(8,128)(2,1)S(1)}, u32[]{:S(2)}, u32[]{:S(2)}) collective-permute-start(bf16[12,48,128]{2,1,0:T(8,128)(2,1)S(1)} %get-tuple-element.142), channel_id=1, source_target_pairs={{0,16},{1,17},{2,18},{3,19},{4,20},{5,21},{6,22},{7,23},{8,24},{9,... | collective-permute-start | bytes 442376 | tf_op jit(solution)/shard_map/ppermute | solution.py:654
  184.7 12.7 %collective-permute-start.21 = (bf16[15,96,128]{2,1,0:T(8,128)(2,1)S(1)}, bf16[15,96,128]{2,1,0:T(8,128)(2,1)S(1)}, u32[]{:S(2)}, u32[]{:S(2)}) collective-permute-start(bf16[15,96,128]{2,1,0:T(8,128)(2,1)S(1)} %bitcast.111), channel_id=1, source_target_pairs={{0,8},{1,9},{2,10},{3,11},{4,12},{5,13},{6,14},{7,15},{8,0},{9,1},... | collective-permute-start | bytes 1105928 | tf_op jit(solution)/shard_map/ppermute | solution.py:654
  187.7 8.3 %copy-start.4 = (bf16[9,192,128]{2,1,0:T(8,128)(2,1)S(1)}, bf16[9,192,128]{2,1,0:T(8,128)(2,1)}, u32[]{:S(2)}) copy-start(bf16[9,192,128]{2,1,0:T(8,128)(2,1)} %get-tuple-element.118) | copy-start | bytes 1327108
  187.7 6.5 %collective-permute-start.17 = (bf16[5,192,128]{2,1,0:T(8,128)(2,1)}, bf16[5,192,128]{2,1,0:T(8,128)(2,1)S(1)}, u32[]{:S(2)}, u32[]{:S(2)}) collective-permute-start(bf16[5,192,128]{2,1,0:T(8,128)(2,1)} %get-tuple-element.119), channel_id=1, source_target_pairs={{0,4},{1,5},{2,6},{3,7},{4,0},{5,1},{6,2},{7,3},{8,12},{9,13},{10,... | collective-permute-start | bytes 737288 | tf_op jit(solution)/shard_map/ppermute | solution.py:654
  189.5 6.4 %collective-permute-start.18 = (bf16[5,192,128]{2,1,0:T(8,128)(2,1)}, bf16[5,192,128]{2,1,0:T(8,128)(2,1)S(1)}, u32[]{:S(2)}, u32[]{:S(2)}) collective-permute-start(bf16[5,192,128]{2,1,0:T(8,128)(2,1)} %get-tuple-element.120), channel_id=1, source_target_pairs={{0,1},{1,0},{2,3},{3,2},{4,5},{5,4},{6,7},{7,6},{8,9},{9,8},{10,11... | collective-permute-start | bytes 737288 | tf_op jit(solution)/shard_map/ppermute | solution.py:654
  194.2 1.9 copy-start.6
  194.3 3.2 %copy-start = (bf16[15,2,1,48,128]{4,3,2,1,0:T(8,128)(2,1)S(1)}, bf16[15,2,1,48,128]{4,3,2,1,0:T(8,128)(2,1)}, u32[]{:S(2)}) copy-start(bf16[15,2,1,48,128]{4,3,2,1,0:T(8,128)(2,1)} %get-tuple-element.135) | copy-start | bytes 1105924
  196.3 7.6 %collective-permute-start.19 = (bf16[1056,128]{1,0:T(8,128)(2,1)S(1)}, bf16[1056,128]{1,0:T(8,128)(2,1)S(1)}, u32[]{:S(2)}, u32[]{:S(2)}) collective-permute-start(bf16[1056,128]{1,0:T(8,128)(2,1)S(1)} %constant_dynamic-update-slice_fusion.6), channel_id=1, source_target_pairs={{0,8},{1,9},{2,10},{3,11},{4,12},{5,13},{6,14},{7,15},{8,0},{9,1},... | collective-permute-start | bytes 811016 | tf_op jit(solution)/shard_map/ppermute | solution.py:654
  197.7 11.7 %collective-permute-start.22 = (bf16[15,48,128]{2,0,1:T(8,128)(2,1)S(1)}, bf16[15,48,128]{2,0,1:T(8,128)(2,1)S(1)}, u32[]{:S(2)}, u32[]{:S(2)}) collective-permute-start(bf16[15,48,128]{2,0,1:T(8,128)(2,1)S(1)} %bitcast.113), channel_id=1, source_target_pairs={{0,16},{1,17},{2,18},{3,19},{4,20},{5,21},{6,22},{7,23},{8,24},{9,... | collective-permute-start | bytes 552968 | tf_op jit(solution)/shard_map/ppermute | solution.py:654
  204.3 9.0 %collective-permute-start.20 = (bf16[624,128]{1,0:T(8,128)(2,1)S(1)}, bf16[624,128]{1,0:T(8,128)(2,1)S(1)}, u32[]{:S(2)}, u32[]{:S(2)}) collective-permute-start(bf16[624,128]{1,0:T(8,128)(2,1)S(1)} %constant_dynamic-update-slice_fusion.25), channel_id=1, source_target_pairs={{0,16},{1,17},{2,18},{3,19},{4,20},{5,21},{6,22},{7,23},{8,24},{9,... | collective-permute-start | bytes 479240 | tf_op jit(solution)/shard_map/ppermute | solution.py:654
  (4 other events, 3.3 us)

commit v4 on v3

--- a/solution.py
+++ b/solution.py
@@ -459,16 +459,19 @@
 
 
 def up_out_grads(
-    normed_ref, agrad_ref, mixed_ref, ugrad_ref,
+    normed_ref, agrad_hbm, mixed_hbm, ugrad_ref,
     *refs,
     count, dp_count, sort
 ):
-    ukeep_ref, usend_ref, okeep_ref, osend_ref, ulhs_ref, olhs_ref, tmp_ref = refs[-7:]
+    ukeep_ref, usend_ref, okeep_ref, osend_ref, ulhs_ref, olhs_ref, tmp_ref, agrad_ref, mixed_ref, sem = refs[-10:]
     step = pl.program_id(0)
+    fetch = [pltpu.make_async_copy(agrad_hbm, agrad_ref, sem.at[0]), pltpu.make_async_copy(mixed_hbm, mixed_ref, sem.at[1])]
     width = normed_ref.shape[1]
 
     @pl.when(step == 0)
     def _():
+        fetch[0].start()
+        fetch[1].start()
         put_transposed(ulhs_ref, tmp_ref, normed_ref[...], 0, row_sources(dp_count) if sort else [])
 
     @pl.when(step < count)
@@ -477,6 +480,8 @@
 
     @pl.when(step == count)
     def _():
+        fetch[0].wait()
+        fetch[1].wait()
         put_transposed(olhs_ref, tmp_ref, agrad_ref[...], 0, row_sources(dp_count) if sort else [])
 
     @pl.when(step >= count)
@@ -665,9 +670,9 @@
 def route(name, arrays, outs, moves, vec=None, after=()):
     rows = arrays[0].shape[-2]
     grid = 2 if rows % 32 == 0 else 1
-    own, got, send = vec if vec is not None else (None, None, None)
-    extra = [own] if vec is not None else []
+    extra, got, send = vec if vec is not None else ([], None, None)
     if vec is not None:
+        own = extra[0]
         count, blocks = own.shape[0], own.shape[1] // 128
         assert grid == 2 and 2 * count * blocks == rows
 
@@ -688,7 +693,7 @@
 
             @pl.when(step == 0)
             def _():
-                sums_ref[...] = refs[len(arrays)][...]
+                sums_ref[...] = functools.reduce(jnp.add, [ref[...] for ref in refs[len(arrays) : len(arrays) + len(extra)]])
 
             if got is not None:
                 other = ins[got[0]][got[1]].astype(f32)
@@ -887,19 +892,21 @@
     )
     s_recv = exchange(s_send, 1, dp_count)
     d_keep, d_got = over_core(d_keep, d_send)
-    u_specs, u_shapes = tiles(half_u, chunk, 0)
-    o_specs, o_shapes = tiles(half_w, half_w, count)
+    wide_chunk = half_u // 2
+    up_count = hidden_units // wide_chunk
+    u_specs, u_shapes = tiles(half_u, wide_chunk, 0)
+    o_specs, o_shapes = tiles(half_w, half_w, up_count)
     whole_rows = whole((half, width))
     u_keep, u_send, o_keep, o_send = run(
-        functools.partial(up_out_grads, count=count, **layout),
+        functools.partial(up_out_grads, count=up_count, **layout),
         "up_out_grads",
-        (count + 2,),
-        [whole_rows] * 3 + [pl.BlockSpec((half, chunk), lambda i: (0, jnp.minimum(i, count - 1)))],
+        (up_count + 2,),
+        [whole_rows, hbm, hbm] + [pl.BlockSpec((half, wide_chunk), lambda i: (0, jnp.minimum(i, up_count - 1)))],
         (normed, agrad, mixed, ugrad),
         (),
         out_specs=u_specs + o_specs,
         out_shape=u_shapes + o_shapes,
-        scratch_shapes=[pltpu.VMEM((width, half), bf16)] * 3,
+        scratch_shapes=[pltpu.VMEM((width, half), bf16)] * 3 + [pltpu.VMEM((half, width), bf16)] * 2 + [pltpu.SemaphoreType.DMA((2,))],
         **params(9),
     )
     u_keep, u_got = over_core(u_keep, u_send)
@@ -1006,7 +1013,7 @@
             (out, (at[0] * qkv_l + at[1],) if out == 1 else at, terms)
             for out, at, terms in first_moves([(0, o_n), (2, 2 * o_n)], qkv_l)
         ],
-        (vec + vec_got, None, (1, (2 * qkv_l,))),
+        ([vec, vec_got], None, (1, (2 * qkv_l,))),
         (uo_part,),
     )
     qkv_x, qkv_y = exchange(qkv_ls, 1, dp_count), exchange(qkv_rs, 4, dp_count)
@@ -1035,7 +1042,7 @@
         [qkv_lk, qkv_x, qkv_rk, qkv_y],
         [flat(qkv_n), flat(qkv_l + 1), flat(qkv_r)],
         moves,
-        (vec, (1, (2 * qkv_l,)), (1, (qkv_l,))),
+        ([vec], (1, (2 * qkv_l,)), (1, (qkv_l,))),
         (up_z[0], down_z[0], grad_tokens),
     )
     qkv_x, qkv_y = exchange(qkv_rs, 1, dp_count), exchange(qkv_ls, 4, dp_count)

time: 220 us -> 219 us (level)
  transfers between devices with their start and end apart: 24 -> 24, of which waited for: 9 -> 9; matrix products, arithmetic and copies ran while one was open for 4% -> 3% of each run, Pallas kernels for 36% -> 35%
where the time goes in v4:
time: 219 us; the launch traced here: 215 us
  Pallas kernels  152 us (69%)
  starting transfers between devices  26.4 us (12%)
  waiting for transfers between devices  23.1 us (11%)
  local copies, waits for them, and re-layouts  10.3 us (5%)
  other arithmetic  2.41 us (1%)
    pallas_call x5, Pallas kernels, run(): pl.pallas_call(kernel, name=name, grid=grid, in_specs=list(in_specs) + fe...  114 us
    ppermute x24, starting transfers between devices, exchange(): lax.ppermute(values, every_axis, [(i, i ^ mask) for i in range(2 * dp_cou...  26.4 us
    ppermute x24, waiting for transfers between devices, exchange(): lax.ppermute(values, every_axis, [(i, i ^ mask) for i in range(2 * dp_cou...  23.1 us
    pallas_call x5, Pallas kernels, route(): pl.pallas_call(kernel, name=name, grid=(grid,), in_specs=[spec(a.shape) f...  18 us
    pallas_call x1, Pallas kernels, body(): pl.pallas_call(functools.partial(forward_keys, **static), name='key_state...  11.9 us
    pallas_call x1, Pallas kernels, body(): pl.pallas_call(functools.partial(forward_queries, heads=heads, hdim=hdim)...  7.42 us
  transfers between devices with their start and end apart: 24, of which 9 were waited for; matrix products, arithmetic and copies ran while one was open for 3% of the time, Pallas kernels for 35%

profile of v4, /device:TPU:0, one launch (start us, length us, event | category | flops | bytes accessed | tf_op | source)
XLA Modules:
  0.0 215.4 jit_solution(1863748269463651741)
XLA Ops:
  0.6 11.9 %key_states.1 = (bf16[1024,1536]{1,0:T(8,128)(2,1)}, bf16[3072,256]{1,0:T(8,128)(2,1)}, f32[96,256]{1,0:T(8,128)}, f32[768,256]{1,0:T(8,128)}, bf16[784,256]{1,0:T(8,128)(2,1)}) custom-call(s32[1,4]{1,0:T(1,128)} %len_ref.7, bf16[1024,768]{1,0:T(8,128)(2,1)} %tok_ref.9, bf16[3,768,768]{2,1,0:T(8,128)(2,1)} %bitcast.114, bf16[3,768,768]{2,1,0:T(8,128)(2,1)} %bitcast.115, ...), custom_call_target="tpu_custom_call" | custom-call | flops 13200000000 | bytes 12000000 | tf_op jit(solution)/shard_map/key_states/pallas_call | solution.py:816
  12.5 3.0 %collective-permute-start = (bf16[784,256]{1,0:T(8,128)(2,1)}, bf16[784,256]{1,0:T(8,128)(2,1)S(1)}, u32[]{:S(2)}, u32[]{:S(2)}) collective-permute-start(bf16[784,256]{1,0:T(8,128)(2,1)} %get-tuple-element.72), channel_id=1, source_target_pairs={{0,1},{1,0},{2,3},{3,2},{4,5},{5,4},{6,7},{7,6},{8,9},{9,8},{10,11... | collective-permute-start | bytes 1204232 | tf_op jit(solution)/shard_map/ppermute | solution.py:659
  15.5 7.4 %query_features.1 = (bf16[1024,768]{1,0:T(8,128)(2,1)}, bf16[1024,3072]{1,0:T(8,128)(2,1)}) custom-call(bf16[1024,768]{1,0:T(8,128)(2,1)} %tok_ref.9, bf16[3,768,768]{2,1,0:T(8,128)(2,1)} %bitcast.116, f32[3,768]{1,0:T(4,128)} %b_ref.3, bf16[12,64,256]{2,1,0:T(8,128)(2,1)} %map_ref.7), custom_call_target="tpu_custom_call" | custom-call | flops 7699999744 | bytes 7000000 | tf_op jit(solution)/shard_map/query_features/pallas_call | solution.py:827
  22.9 2.1 collective-permute-done.recv_ref
  25.8 58.9 %chain.1 = (bf16[1024,768]{1,0:T(8,128)(2,1)}, bf16[1024,768]{1,0:T(8,128)(2,1)}, bf16[1024,768]{1,0:T(8,128)(2,1)}, bf16[1024,128]{1,0:T(8,128)(2,1)}, bf16[102...) custom-call(s32[1,4]{1,0:T(1,128)} %len_ref.7, ...), custom_call_target="tpu_custom_call" | custom-call | flops 63800000512 | bytes 58000000 | tf_op jit(solution)/shard_map/chain/pallas_call | solution.py:809
  84.8 1.9 collective-permute-start.2
  86.7 12.8 %up_out_grads.1 = (bf16[2,2,12,192,128]{4,3,2,1,0:T(8,128)(2,1)}, bf16[2,2,12,192,128]{4,3,2,1,0:T(8,128)(2,1)}, bf16[2,2,3,192,128]{4,3,2,1,0:T(8,128)(2,1)}, bf16[2,2,3,192,128]{4,3,2,1,0:T(8,128)(2,1)}) custom-call(bf16[1024,768]{1,0:T(8,128)(2,1)} %get-tuple-element.81.normed_ref, bf16[1024,768]{1,0:T(8,128)(2,1)} %get-tuple-element.74.agrad_hbm.agrad_ref, ...), custom_call_target="tpu_custom_call" | custom-call | flops 9900000256 | bytes 9000000 | tf_op jit(solution)/shard_map/up_out_grads/pallas_call | solution.py:809
  100.9 3.7 %down_1.1 = (bf16[2,6,192,128]{3,2,1,0:T(8,128)(2,1)}, bf16[2,6,192,128]{3,2,1,0:T(8,128)(2,1)}, bf16[2,6,192,128]{3,2,1,0:T(8,128)(2,1)}, bf16[2,6,192,128]{3,2,1,0:T(8,128)(2,1)}) custom-call(bf16[2,2,12,192,128]{4,3,2,1,0:T(8,128)(2,1)} %get-tuple-element.79.refs_0_, bf16[2,2,12,192,128]{4,3,2,1,0:T(8,128)(2,1)} %collective-permute-done.1.refs_1_, ...), custom_call_target="tpu_custom_call" | custom-call | flops 3300000000 | bytes 3000000 | tf_op jit(solution)/shard_map/down_1/pallas_call | solution.py:713
  104.7 1.8 collective-permute-start.4
  106.5 16.4 %query_back.1 = (bf16[1024,768]{1,0:T(8,128)(2,1)}, f32[16,768]{1,0:T(8,128)}, bf16[2,2,3,192,128]{4,3,2,1,0:T(8,128)(2,1)}, bf16[2,2,3,192,128]{4,3,2,1,0:T(8,128)(2,1)}) custom-call(s32[1,4]{1,0:T(1,128)} %len_ref.7, bf16[1024,768]{1,0:T(8,128)(2,1)} %get-tuple-element.75.q_ref, bf16[1024,768]{1,0:T(8,128)(2,1)} %get-tuple-element.76.num_ref, ...), custom_call_target="tpu_custom_call" | custom-call | flops 19800000512 | bytes 18000000 | tf_op jit(solution)/shard_map/query_back/pallas_call | solution.py:809
  124.1 5.3 %down_2_up_1.1 = (bf16[12,192,128]{2,1,0:T(8,128)(2,1)}, bf16[2,7,192,128]{3,2,1,0:T(8,128)(2,1)}, bf16[2,8,192,128]{3,2,1,0:T(8,128)(2,1)}, bf16[20,192,128]{2,1,0:T(8,128)(2,1)}, bf16[22,192,128]{2,1,0:T(8,128)(2,1)}) custom-call(bf16[2,6,192,128]{3,2,1,0:T(8,128)(2,1)} %get-tuple-element.86.refs_0_, bf16[2,6,192,128]{3,2,1,0:T(8,128)(2,1)} %copy-done.8, ...), custom_call_target="tpu_custom_call" | custom-call | flops 3300000000 | bytes 3000000 | tf_op jit(solution)/shard_map/down_2_up_1/pallas_call | solution.py:713
  129.5 1.7 collective-permute-start.10
  131.7 18.1 %key_back.1 = (bf16[1024,1536]{1,0:T(8,128)(2,1)}, f32[16,768]{1,0:T(8,128)}, bf16[2,2,6,192,128]{4,3,2,1,0:T(8,128)(2,1)}, bf16[2,2,6,192,128]{4,3,2,1,0:T(8,128)(2,1)}) custom-call(s32[1,4]{1,0:T(1,128)} %len_ref.7, bf16[1024,1536]{1,0:T(8,128)(2,1)} %get-tuple-element.88.kv_ref, bf16[1024,768]{1,0:T(8,128)(2,1)} %tok_ref.9, bf16[12,64,256]{2,1,0:T(8,128)(2,1)} %map_ref.7, ...), custom_call_target="tpu_custom_call" | custom-call | flops 19800000512 | bytes 18000000 | tf_op jit(solution)/shard_map/key_back/pallas_call | solution.py:809
  150.4 2.6 %collective-permute-done.10.refs_1_ = bf16[20,192,128]{2,1,0:T(8,128)(2,1)S(1)} collective-permute-done((bf16[20,192,128]{2,1,0:T(8,128)(2,1)}, bf16[20,192,128]{2,1,0:T(8,128)(2,1)S(1)}, u32[]{:S(2)}, u32[]{:S(2)}) %collective-permute-start.10) | collective-permute-done | bytes 983072 | tf_op jit(solution)/shard_map/ppermute | solution.py:659
  153.0 3.5 %collective-permute-done.11.refs_2_ = bf16[22,192,128]{2,1,0:T(8,128)(2,1)} collective-permute-done((bf16[22,192,128]{2,1,0:T(8,128)(2,1)}, bf16[22,192,128]{2,1,0:T(8,128)(2,1)}, u32[]{:S(2)}, u32[]{:S(2)}) %collective-permute-start.11) | collective-permute-done | bytes 1081376 | tf_op jit(solution)/shard_map/ppermute | solution.py:659
  156.5 1.0 slice.338
  158.5 1.6 collective-permute-start.16
  160.0 3.2 %up_2.1 = (bf16[15,192,128]{2,1,0:T(8,128)(2,1)}, bf16[7,192,128]{2,1,0:T(8,128)(2,1)}, bf16[8,192,128]{2,1,0:T(8,128)(2,1)}) custom-call(bf16[12,192,128]{2,1,0:T(8,128)(2,1)} %get-tuple-element.99.refs_0_, bf16[20,192,128]{2,1,0:T(8,128)(2,1)} %copy-done.5, bf16[22,192,128]{2,1,0:T(8,128)(2,1)} %collective-permute-done.11.refs_2_, ...), custom_call_target="tpu_custom_call" | custom-call | flops 3300000000 | bytes 3000000 | tf_op jit(solution)/shard_map/up_2/pallas_call | solution.py:713
  164.8 3.3 %qkv_1.1 = (bf16[2,4,192,128]{3,2,1,0:T(8,128)(2,1)}, bf16[9,192,128]{2,1,0:T(8,128)(2,1)}, bf16[2,5,192,128]{3,2,1,0:T(8,128)(2,1)}, bf16[2,5,192,128]{3,2,1,0:T(8,128)(2,1)}, f32[16,768]{1,0:T(8,128)}) custom-call(bf16[2,2,3,192,128]{4,3,2,1,0:T(8,128)(2,1)} %get-tuple-element.101.refs_0_, bf16[2,2,3,192,128]{4,3,2,1,0:T(8,128)(2,1)} %collective-permute-done.7.refs_1_, ...), custom_call_target="tpu_custom_call" | custom-call | flops 3300000000 | bytes 3000000 | tf_op jit(solution)/shard_map/qkv_1/pallas_call | solution.py:713
  168.1 1.7 collective-permute-start.12
  169.8 1.5 collective-permute-start.13
  171.3 8.2 %token_grads.1.refs_7_ = bf16[1024,768]{1,0:T(8,128)(2,1)} custom-call(bf16[1024,768]{1,0:T(8,128)(2,1)} %get-tuple-element.74.agrad_hbm.agrad_ref, bf16[1024,768]{1,0:T(8,128)(2,1)} %get-tuple-element.87.pgq_ref, bf16[1024,1536]{1,0:T(8,128)(2,1)} %get-tuple-element.100.pgkv_ref, bf16[3,768,768]{2,1,0:T(8,128)(2,1)} %bitcast.117, ...), custom_call_target="tpu_custom_call" | custom-call | flops 8800000000 | bytes 8000000 | tf_op jit(solution)/shard_map/token_grads/pallas_call | solution.py:809
  180.3 2.6 %collective-permute-start.23 = (bf16[12,48,128]{2,1,0:T(8,128)(2,1)S(1)}, bf16[12,48,128]{2,1,0:T(8,128)(2,1)S(1)}, u32[]{:S(2)}, u32[]{:S(2)}) collective-permute-start(bf16[12,48,128]{2,1,0:T(8,128)(2,1)S(1)} %get-tuple-element.142), channel_id=1, source_target_pairs={{0,16},{1,17},{2,18},{3,19},{4,20},{5,21},{6,22},{7,23},{8,24},{9,... | collective-permute-start | bytes 442376 | tf_op jit(solution)/shard_map/ppermute | solution.py:659
  183.1 0.8 fusion.2
  184.3 2.5 %qkv_2.1 = (bf16[9,192,128]{2,1,0:T(8,128)(2,1)}, bf16[5,192,128]{2,1,0:T(8,128)(2,1)}, bf16[5,192,128]{2,1,0:T(8,128)(2,1)}, f32[16,768]{1,0:T(8,128)}) custom-call(bf16[2,4,192,128]{3,2,1,0:T(8,128)(2,1)} %get-tuple-element.111.refs_0_, bf16[9,192,128]{2,1,0:T(8,128)(2,1)} %collective-permute-done.12.refs_1_, ...), custom_call_target="tpu_custom_call" | custom-call | flops 3300000000 | bytes 3000000 | tf_op jit(solution)/shard_map/qkv_2/pallas_call | solution.py:713
  189.2 4.2 %collective-permute-done.17 = bf16[5,192,128]{2,1,0:T(8,128)(2,1)S(1)} collective-permute-done((bf16[5,192,128]{2,1,0:T(8,128)(2,1)}, bf16[5,192,128]{2,1,0:T(8,128)(2,1)S(1)}, u32[]{:S(2)}, u32[]{:S(2)}) %collective-permute-start.17) | collective-permute-done | bytes 245792 | tf_op jit(solution)/shard_map/ppermute | solution.py:659
  193.5 1.6 collective-permute-done.18
  195.5 1.1 collective-permute-start.19
  196.9 1.6 collective-permute-start.22
  198.4 4.3 %collective-permute-done.19 = bf16[1056,128]{1,0:T(8,128)(2,1)S(1)} collective-permute-done((bf16[1056,128]{1,0:T(8,128)(2,1)S(1)}, bf16[1056,128]{1,0:T(8,128)(2,1)S(1)}, u32[]{:S(2)}, u32[]{:S(2)}) %collective-permute-start.19) | collective-permute-done | bytes 270368 | tf_op jit(solution)/shard_map/ppermute | solution.py:659
  203.1 3.6 %collective-permute-start.20 = (bf16[624,128]{1,0:T(8,128)(2,1)S(1)}, bf16[624,128]{1,0:T(8,128)(2,1)S(1)}, u32[]{:S(2)}, u32[]{:S(2)}) collective-permute-start(bf16[624,128]{1,0:T(8,128)(2,1)S(1)} %constant_dynamic-update-slice_fusion.25), channel_id=1, source_target_pairs={{0,16},{1,17},{2,18},{3,19},{4,20},{5,21},{6,22},{7,23},{8,24},{9,... | collective-permute-start | bytes 479240 | tf_op jit(solution)/shard_map/ppermute | solution.py:659
  206.7 4.0 %collective-permute-done.22 = bf16[15,48,128]{2,0,1:T(8,128)(2,1)S(1)} collective-permute-done((bf16[15,48,128]{2,0,1:T(8,128)(2,1)S(1)}, bf16[15,48,128]{2,0,1:T(8,128)(2,1)S(1)}, u32[]{:S(2)}, u32[]{:S(2)}) %collective-permute-start.22) | collective-permute-done | bytes 184352 | tf_op jit(solution)/shard_map/ppermute | solution.py:659
  (135 shorter events, 16.1 us)
Async XLA Ops:
  12.5 12.5 %collective-permute-start = (bf16[784,256]{1,0:T(8,128)(2,1)}, bf16[784,256]{1,0:T(8,128)(2,1)S(1)}, u32[]{:S(2)}, u32[]{:S(2)}) collective-permute-start(bf16[784,256]{1,0:T(8,128)(2,1)} %get-tuple-element.72), channel_id=1, source_target_pairs={{0,1},{1,0},{2,3},{3,2},{4,5},{5,4},{6,7},{7,6},{8,9},{9,8},{10,11... | collective-permute-start | bytes 1204232 | tf_op jit(solution)/shard_map/ppermute | solution.py:659
  84.7 15.4 %collective-permute-start.1 = (bf16[2,2,12,192,128]{4,3,2,1,0:T(8,128)(2,1)}, bf16[2,2,12,192,128]{4,3,2,1,0:T(8,128)(2,1)}, u32[]{:S(2)}, u32[]{:S(2)}) collective-permute-start(bf16[2,2,12,192,128]{4,3,2,1,0:T(8,128)(2,1)} %get-tuple-element.80), channel_id=1, source_target_pairs={{0,2},{1,3},{2,0},{3,1},{4,6},{5,7},{6,4},{7,5},{8,10},{9,11},{10,... | collective-permute-start | bytes 7077896 | tf_op jit(solution)/shard_map/ppermute | solution.py:659
  84.8 15.3 %collective-permute-start.2 = (bf16[784,256]{1,0:T(8,128)(2,1)}, bf16[784,256]{1,0:T(8,128)(2,1)S(1)}, u32[]{:S(2)}, u32[]{:S(2)}) collective-permute-start(bf16[784,256]{1,0:T(8,128)(2,1)} %get-tuple-element.85), channel_id=1, source_target_pairs={{0,1},{1,0},{2,3},{3,2},{4,5},{5,4},{6,7},{7,6},{8,9},{9,8},{10,11... | collective-permute-start | bytes 1204232 | tf_op jit(solution)/shard_map/ppermute | solution.py:659
  99.6 23.4 %collective-permute-start.5 = (bf16[2,2,12,192,128]{4,3,2,1,0:T(8,128)(2,1)}, bf16[2,2,12,192,128]{4,3,2,1,0:T(8,128)(2,1)}, u32[]{:S(2)}, u32[]{:S(2)}) collective-permute-start(bf16[2,2,12,192,128]{4,3,2,1,0:T(8,128)(2,1)} %get-tuple-element.96), channel_id=1, source_target_pairs={{0,2},{1,3},{2,0},{3,1},{4,6},{5,7},{6,4},{7,5},{8,10},{9,11},{10,... | collective-permute-start | bytes 7077896 | tf_op jit(solution)/shard_map/ppermute | solution.py:659
  99.8 23.2 %collective-permute-start.6 = (bf16[2,2,3,192,128]{4,3,2,1,0:T(8,128)(2,1)}, bf16[2,2,3,192,128]{4,3,2,1,0:T(8,128)(2,1)S(1)}, u32[]{:S(2)}, u32[]{:S(2)}) collective-permute-start(bf16[2,2,3,192,128]{4,3,2,1,0:T(8,128)(2,1)} %get-tuple-element.98), channel_id=1, source_target_pairs={{0,2},{1,3},{2,0},{3,1},{4,6},{5,7},{6,4},{7,5},{8,10},{9,11},{10,... | collective-permute-start | bytes 1769480 | tf_op jit(solution)/shard_map/ppermute | solution.py:659
  104.6 18.4 %collective-permute-start.3 = (bf16[2,6,192,128]{3,2,1,0:T(8,128)(2,1)}, bf16[2,6,192,128]{3,2,1,0:T(8,128)(2,1)S(1)}, u32[]{:S(2)}, u32[]{:S(2)}) collective-permute-start(bf16[2,6,192,128]{3,2,1,0:T(8,128)(2,1)} %get-tuple-element.93), channel_id=1, source_target_pairs={{0,1},{1,0},{2,3},{3,2},{4,5},{5,4},{6,7},{7,6},{8,9},{9,8},{10,11... | collective-permute-start | bytes 1769480 | tf_op jit(solution)/shard_map/ppermute | solution.py:659
  104.7 18.3 %collective-permute-start.4 = (bf16[2,6,192,128]{3,2,1,0:T(8,128)(2,1)}, bf16[2,6,192,128]{3,2,1,0:T(8,128)(2,1)S(1)}, u32[]{:S(2)}, u32[]{:S(2)}) collective-permute-start(bf16[2,6,192,128]{3,2,1,0:T(8,128)(2,1)} %get-tuple-element.95), channel_id=1, source_target_pairs={{0,4},{1,5},{2,6},{3,7},{4,0},{5,1},{6,2},{7,3},{8,12},{9,13},{10,... | collective-permute-start | bytes 1769480 | tf_op jit(solution)/shard_map/ppermute | solution.py:659
  123.0 1.1 copy-start.9
  129.5 23.5 %collective-permute-start.10 = (bf16[20,192,128]{2,1,0:T(8,128)(2,1)}, bf16[20,192,128]{2,1,0:T(8,128)(2,1)S(1)}, u32[]{:S(2)}, u32[]{:S(2)}) collective-permute-start(bf16[20,192,128]{2,1,0:T(8,128)(2,1)} %get-tuple-element.106), channel_id=1, source_target_pairs={{0,1},{1,0},{2,3},{3,2},{4,5},{5,4},{6,7},{7,6},{8,9},{9,8},{10,11... | collective-permute-start | bytes 2949128 | tf_op jit(solution)/shard_map/ppermute | solution.py:659
  131.1 25.4 %collective-permute-start.11 = (bf16[22,192,128]{2,1,0:T(8,128)(2,1)}, bf16[22,192,128]{2,1,0:T(8,128)(2,1)}, u32[]{:S(2)}, u32[]{:S(2)}) collective-permute-start(bf16[22,192,128]{2,1,0:T(8,128)(2,1)} %get-tuple-element.107), channel_id=1, source_target_pairs={{0,4},{1,5},{2,6},{3,7},{4,0},{5,1},{6,2},{7,3},{8,12},{9,13},{10,... | collective-permute-start | bytes 3244040 | tf_op jit(solution)/shard_map/ppermute | solution.py:659
  149.7 7.8 %copy-start.3 = (bf16[12,192,128]{2,1,0:T(8,128)(2,1)S(1)}, bf16[12,192,128]{2,1,0:T(8,128)(2,1)}, u32[]{:S(2)}) copy-start(bf16[12,192,128]{2,1,0:T(8,128)(2,1)} %get-tuple-element.99.refs_0_) | copy-start | bytes 1769476
  149.7 14.5 %collective-permute-start.8 = (bf16[2,2,6,192,128]{4,3,2,1,0:T(8,128)(2,1)}, bf16[2,2,6,192,128]{4,3,2,1,0:T(8,128)(2,1)}, u32[]{:S(2)}, u32[]{:S(2)}) collective-permute-start(bf16[2,2,6,192,128]{4,3,2,1,0:T(8,128)(2,1)} %get-tuple-element.104), channel_id=1, source_target_pairs={{0,2},{1,3},{2,0},{3,1},{4,6},{5,7},{6,4},{7,5},{8,10},{9,11},{10,... | collective-permute-start | bytes 3538952 | tf_op jit(solution)/shard_map/ppermute | solution.py:659
  149.8 14.0 %collective-permute-start.7 = (bf16[2,2,3,192,128]{4,3,2,1,0:T(8,128)(2,1)}, bf16[2,2,3,192,128]{4,3,2,1,0:T(8,128)(2,1)}, u32[]{:S(2)}, u32[]{:S(2)}) collective-permute-start(bf16[2,2,3,192,128]{4,3,2,1,0:T(8,128)(2,1)} %get-tuple-element.102), channel_id=1, source_target_pairs={{0,2},{1,3},{2,0},{3,1},{4,6},{5,7},{6,4},{7,5},{8,10},{9,11},{10,... | collective-permute-start | bytes 1769480 | tf_op jit(solution)/shard_map/ppermute | solution.py:659
  150.3 13.9 %collective-permute-start.9 = (f32[16,768]{1,0:T(8,128)}, f32[16,768]{1,0:T(8,128)S(1)}, u32[]{:S(2)}, u32[]{:S(2)}) collective-permute-start(f32[16,768]{1,0:T(8,128)} %get-tuple-element.105.refs_4_), channel_id=1, source_target_pairs={{0,2},{1,3},{2,0},{3,1},{4,6},{5,7},{6,4},{7,5},{8,10},{9,11},{10,... | collective-permute-start | bytes 147464 | tf_op jit(solution)/shard_map/ppermute | solution.py:659
  153.0 5.5 %copy-start.5 = (bf16[20,192,128]{2,1,0:T(8,128)(2,1)}, bf16[20,192,128]{2,1,0:T(8,128)(2,1)S(1)}, u32[]{:S(2)}) copy-start(bf16[20,192,128]{2,1,0:T(8,128)(2,1)S(1)} %collective-permute-done.10.refs_1_) | copy-start | bytes 2949124
  158.5 21.0 %collective-permute-start.16 = (bf16[12,96,128]{2,1,0:T(8,128)(2,1)S(1)}, bf16[12,96,128]{2,1,0:T(8,128)(2,1)S(1)}, u32[]{:S(2)}, u32[]{:S(2)}) collective-permute-start(bf16[12,96,128]{2,1,0:T(8,128)(2,1)S(1)} %bitcast.112), channel_id=1, source_target_pairs={{0,8},{1,9},{2,10},{3,11},{4,12},{5,13},{6,14},{7,15},{8,0},{9,1},... | collective-permute-start | bytes 884744 | tf_op jit(solution)/shard_map/ppermute | solution.py:659
  163.3 19.6 %collective-permute-start.14 = (bf16[7,192,128]{2,1,0:T(8,128)(2,1)}, bf16[7,192,128]{2,1,0:T(8,128)(2,1)S(1)}, u32[]{:S(2)}, u32[]{:S(2)}) collective-permute-start(bf16[7,192,128]{2,1,0:T(8,128)(2,1)} %get-tuple-element.116), channel_id=1, source_target_pairs={{0,4},{1,5},{2,6},{3,7},{4,0},{5,1},{6,2},{7,3},{8,12},{9,13},{10,... | collective-permute-start | bytes 1032200 | tf_op jit(solution)/shard_map/ppermute | solution.py:659
  163.8 19.1 %collective-permute-start.15 = (bf16[8,192,128]{2,1,0:T(8,128)(2,1)}, bf16[8,192,128]{2,1,0:T(8,128)(2,1)S(1)}, u32[]{:S(2)}, u32[]{:S(2)}) collective-permute-start(bf16[8,192,128]{2,1,0:T(8,128)(2,1)} %get-tuple-element.117), channel_id=1, source_target_pairs={{0,1},{1,0},{2,3},{3,2},{4,5},{5,4},{6,7},{7,6},{8,9},{9,8},{10,11... | collective-permute-start | bytes 1179656 | tf_op jit(solution)/shard_map/ppermute | solution.py:659
  168.1 16.2 %collective-permute-start.12 = (bf16[9,192,128]{2,1,0:T(8,128)(2,1)}, bf16[9,192,128]{2,1,0:T(8,128)(2,1)}, u32[]{:S(2)}, u32[]{:S(2)}) collective-permute-start(bf16[9,192,128]{2,1,0:T(8,128)(2,1)} %get-tuple-element.112), channel_id=1, source_target_pairs={{0,1},{1,0},{2,3},{3,2},{4,5},{5,4},{6,7},{7,6},{8,9},{9,8},{10,11... | collective-permute-start | bytes 1327112 | tf_op jit(solution)/shard_map/ppermute | solution.py:659
  169.8 14.6 %collective-permute-start.13 = (bf16[2,5,192,128]{3,2,1,0:T(8,128)(2,1)}, bf16[2,5,192,128]{3,2,1,0:T(8,128)(2,1)}, u32[]{:S(2)}, u32[]{:S(2)}) collective-permute-start(bf16[2,5,192,128]{3,2,1,0:T(8,128)(2,1)} %get-tuple-element.114), channel_id=1, source_target_pairs={{0,4},{1,5},{2,6},{3,7},{4,0},{5,1},{6,2},{7,3},{8,12},{9,13},{10,... | collective-permute-start | bytes 1474568 | tf_op jit(solution)/shard_map/ppermute | solution.py:659
  171.3 8.2 %copy-start.1 = (bf16[12,2,1,48,128]{4,3,2,1,0:T(8,128)(2,1)S(1)}, bf16[12,2,1,48,128]{4,3,2,1,0:T(8,128)(2,1)}, u32[]{:S(2)}) copy-start(bf16[12,2,1,48,128]{4,3,2,1,0:T(8,128)(2,1)} %get-tuple-element.137) | copy-start | bytes 884740
  179.5 3.4 %copy-start.2 = (bf16[15,192,128]{2,1,0:T(8,128)(2,1)S(1)}, bf16[15,192,128]{2,1,0:T(8,128)(2,1)}, u32[]{:S(2)}) copy-start(bf16[15,192,128]{2,1,0:T(8,128)(2,1)} %get-tuple-element.110.refs_6_) | copy-start | bytes 2211844
  180.3 7.7 %collective-permute-start.23 = (bf16[12,48,128]{2,1,0:T(8,128)(2,1)S(1)}, bf16[12,48,128]{2,1,0:T(8,128)(2,1)S(1)}, u32[]{:S(2)}, u32[]{:S(2)}) collective-permute-start(bf16[12,48,128]{2,1,0:T(8,128)(2,1)S(1)} %get-tuple-element.142), channel_id=1, source_target_pairs={{0,16},{1,17},{2,18},{3,19},{4,20},{5,21},{6,22},{7,23},{8,24},{9,... | collective-permute-start | bytes 442376 | tf_op jit(solution)/shard_map/ppermute | solution.py:659
  183.9 12.8 %collective-permute-start.21 = (bf16[15,96,128]{2,1,0:T(8,128)(2,1)S(1)}, bf16[15,96,128]{2,1,0:T(8,128)(2,1)S(1)}, u32[]{:S(2)}, u32[]{:S(2)}) collective-permute-start(bf16[15,96,128]{2,1,0:T(8,128)(2,1)S(1)} %bitcast.111), channel_id=1, source_target_pairs={{0,8},{1,9},{2,10},{3,11},{4,12},{5,13},{6,14},{7,15},{8,0},{9,1},... | collective-permute-start | bytes 1105928 | tf_op jit(solution)/shard_map/ppermute | solution.py:659
  186.9 8.3 %copy-start.4 = (bf16[9,192,128]{2,1,0:T(8,128)(2,1)S(1)}, bf16[9,192,128]{2,1,0:T(8,128)(2,1)}, u32[]{:S(2)}) copy-start(bf16[9,192,128]{2,1,0:T(8,128)(2,1)} %get-tuple-element.118) | copy-start | bytes 1327108
  186.9 6.5 %collective-permute-start.17 = (bf16[5,192,128]{2,1,0:T(8,128)(2,1)}, bf16[5,192,128]{2,1,0:T(8,128)(2,1)S(1)}, u32[]{:S(2)}, u32[]{:S(2)}) collective-permute-start(bf16[5,192,128]{2,1,0:T(8,128)(2,1)} %get-tuple-element.119), channel_id=1, source_target_pairs={{0,4},{1,5},{2,6},{3,7},{4,0},{5,1},{6,2},{7,3},{8,12},{9,13},{10,... | collective-permute-start | bytes 737288 | tf_op jit(solution)/shard_map/ppermute | solution.py:659
  188.7 6.4 %collective-permute-start.18 = (bf16[5,192,128]{2,1,0:T(8,128)(2,1)}, bf16[5,192,128]{2,1,0:T(8,128)(2,1)S(1)}, u32[]{:S(2)}, u32[]{:S(2)}) collective-permute-start(bf16[5,192,128]{2,1,0:T(8,128)(2,1)} %get-tuple-element.120), channel_id=1, source_target_pairs={{0,1},{1,0},{2,3},{3,2},{4,5},{5,4},{6,7},{7,6},{8,9},{9,8},{10,11... | collective-permute-start | bytes 737288 | tf_op jit(solution)/shard_map/ppermute | solution.py:659
  193.4 1.9 copy-start.6
  193.5 3.2 %copy-start = (bf16[15,2,1,48,128]{4,3,2,1,0:T(8,128)(2,1)S(1)}, bf16[15,2,1,48,128]{4,3,2,1,0:T(8,128)(2,1)}, u32[]{:S(2)}) copy-start(bf16[15,2,1,48,128]{4,3,2,1,0:T(8,128)(2,1)} %get-tuple-element.135) | copy-start | bytes 1105924
  195.5 7.2 %collective-permute-start.19 = (bf16[1056,128]{1,0:T(8,128)(2,1)S(1)}, bf16[1056,128]{1,0:T(8,128)(2,1)S(1)}, u32[]{:S(2)}, u32[]{:S(2)}) collective-permute-start(bf16[1056,128]{1,0:T(8,128)(2,1)S(1)} %constant_dynamic-update-slice_fusion.6), channel_id=1, source_target_pairs={{0,8},{1,9},{2,10},{3,11},{4,12},{5,13},{6,14},{7,15},{8,0},{9,1},... | collective-permute-start | bytes 811016 | tf_op jit(solution)/shard_map/ppermute | solution.py:659
  196.9 13.9 %collective-permute-start.22 = (bf16[15,48,128]{2,0,1:T(8,128)(2,1)S(1)}, bf16[15,48,128]{2,0,1:T(8,128)(2,1)S(1)}, u32[]{:S(2)}, u32[]{:S(2)}) collective-permute-start(bf16[15,48,128]{2,0,1:T(8,128)(2,1)S(1)} %bitcast.113), channel_id=1, source_target_pairs={{0,16},{1,17},{2,18},{3,19},{4,20},{5,21},{6,22},{7,23},{8,24},{9,... | collective-permute-start | bytes 552968 | tf_op jit(solution)/shard_map/ppermute | solution.py:659
  203.1 9.4 %collective-permute-start.20 = (bf16[624,128]{1,0:T(8,128)(2,1)S(1)}, bf16[624,128]{1,0:T(8,128)(2,1)S(1)}, u32[]{:S(2)}, u32[]{:S(2)}) collective-permute-start(bf16[624,128]{1,0:T(8,128)(2,1)S(1)} %constant_dynamic-update-slice_fusion.25), channel_id=1, source_target_pairs={{0,16},{1,17},{2,18},{3,19},{4,20},{5,21},{6,22},{7,23},{8,24},{9,... | collective-permute-start | bytes 479240 | tf_op jit(solution)/shard_map/ppermute | solution.py:659
  (5 other events, 3.9 us)
